TPU v7x, 32 devices: a whole 2x2x4 slice. The times are simulated.
32 devices in a mesh: groups: 2 (over y), slab: 4 (over z), chan: 4 (over x, core).
Axes of the slice: x: 2, y: 2, z: 4, core: 2. Of those that a mesh axis runs over, the one named last changes fastest.
Arguments:
- inputs: float32 [256, 128, 20, 128], P(('groups', 'slab'), 'chan'), parts along dimension 0, may hold values from -6 to 6
- cotangent: float32 [256, 128, 20, 128], P(('groups', 'slab'), 'chan'), parts along dimension 0, may hold values from -6 to 6
- spectral: float32 [32, 32, 2, 20, 640], P('slab', 'chan'), may hold values from -2.5 to 2.5
- local_weight: float32 [20, 20], replicated, may hold values from -1.25 to 1.25
- bias_vector: float32 [20], replicated, may hold values from -3 to 3
Outputs:
- output: float32 [256, 128, 20, 128], P(('groups', 'slab'), 'chan'), parts along dimension 0
- grad_inputs: float32 [256, 128, 20, 128], P(('groups', 'slab'), 'chan'), parts along dimension 0
- grad_spectral: float32 [64, 32, 2, 20, 640], P(('groups', 'slab'), 'chan'), parts along dimension 0
There are 2 independent parts, one for each index of `groups`. A program takes and returns all parts, laid end to end along the dimension named above; an argument that names none is the same for every part. Nothing has to cross between parts.
All inputs are finite; a program needn't handle non-finite values.
Results may differ from a plain program's by a relative error of at most 0.0001.
Values sent between devices are 32-bit elements; how exact they have to be, the bound alone decides.
No kernel may reach another device: no remote copies, remote signals or barrier semaphores. Data moves between devices by JAX's collectives and lax.ppermute only.
A program may use at most 320 MiB of HBM per device.

v0:
```python
from functools import partial
import math

import jax
import jax.numpy as jnp
import ml_dtypes
import numpy as np
from jax import lax
from jax.experimental import pallas as pl
from jax.experimental.pallas import tpu as pltpu
from jax.sharding import PartitionSpec as P

f32 = jnp.float32
bf16 = jnp.bfloat16
root_half = 0.7071067811865476
inv_root_two_pi = 0.3989422804014327
VMEM_LIMIT = 60 * 1024 * 1024
NT = (((1,), (1,)), ((), ()))
TN = (((0,), (0,)), ((), ()))


def round_up(value, unit):
    return -(-value // unit) * unit


class Plan:
    def __init__(self, nx, ny, nz, channels, wb, wk, mx, slab_count, chan_count):
        self.nx, self.ny, self.nz, self.c = nx, ny, nz, channels
        self.wb, self.wk, self.mx = wb, wk, mx
        self.s, self.ch = slab_count, chan_count
        self.half = chan_count // 2
        self.na = mx // 2 + 1
        self.span = (wb + 1) * self.na
        self.lw = slab_count * self.span
        self.lp = round_up(self.lw, 128)
        self.ll = round_up(2 * self.span, 128)
        self.mk = self.half * wk
        self.rc = round_up(2 * self.mk + 2 * self.half, 8)
        self.chunks = math.gcd(2, channels)
        self.cc = channels // self.chunks
        self.rt = round_up(self.cc * (wk + 1), 8)
        self.xb = math.gcd(8, nx)
        self.blk = self.xb * ny
        self.rows = self.cc * wk
        self.bb = math.gcd(2, wb)
        self.lb = math.gcd(4, nx)
        self.batch = max(d for d in range(1, 6) if self.cc % d == 0)
        self.full_x, self.full_y = nx * slab_count, ny * chan_count

    def starts(self):
        kept = self.wb * self.s
        return [g * self.wb - (kept if 2 * g >= self.s else 0) for g in range(self.s)]

    def columns(self):
        b = np.concatenate([np.repeat(np.arange(st, st + self.wb + 1), self.na) for st in self.starts()])
        a = np.tile(np.arange(self.na), self.s * (self.wb + 1))
        return a, b

    def plane_table(self):
        a, b = self.columns()
        x = np.repeat(np.arange(self.nx), self.ny)[:, None]
        y = np.tile(np.arange(self.ny), self.nx)[:, None]
        total = self.full_x * self.full_y
        phase = (a * x * self.full_y + b * y * self.full_x) % total * (2.0 * np.pi / total)
        table = np.zeros((self.nx * self.ny, 2 * self.lp))
        scale = 1.0 / math.sqrt(total)
        table[:, : self.lw] = np.cos(phase) * scale
        table[:, self.lp : self.lp + self.lw] = -np.sin(phase) * scale
        high, low = (t.reshape(self.nx // self.xb, 1, self.blk, 2 * self.lp) for t in halves(table))
        return np.concatenate([high, high, low], 1).reshape(-1, 3 * self.blk, 2 * self.lp)

    def turns(self):
        a, b = self.columns()
        x = (np.arange(self.s) * self.nx)[:, None, None]
        y = (np.arange(self.ch) * self.ny)[None, :, None]
        total = self.full_x * self.full_y
        phase = (a * x * self.full_y + b * y * self.full_x) % total * (2.0 * np.pi / total)
        table = np.zeros((self.s, self.ch, 2, self.lp), np.float32)
        table[:, :, 0, : self.lw] = np.cos(phase)
        table[:, :, 1, : self.lw] = np.sin(phase)
        return table

    def depth_rows(self):
        main = np.arange(self.mk)
        edge = (np.arange(self.half) + 1) * self.wk
        z = np.arange(self.nz)
        scale = 1.0 / math.sqrt(self.nz)
        angle = lambda k: (k[:, None] * z) % self.nz * (2.0 * np.pi / self.nz)
        rows = [np.cos(angle(main)), np.sin(angle(main)), np.cos(angle(edge)), np.sin(angle(edge))]
        table = np.zeros((self.rc, self.nz))
        table[: 2 * self.mk + 2 * self.half] = np.concatenate(rows) * scale
        return halves(table)

    def depth_forward(self):
        high, low = self.depth_rows()
        return np.concatenate(
            [np.concatenate([high, high], 1), np.concatenate([low, np.zeros_like(low)], 1)], 0
        )

    def depth_inverse(self):
        high, low = self.depth_rows()
        table = np.zeros((round_up(3 * self.rc, 16), self.nz), ml_dtypes.bfloat16)
        table[: 3 * self.rc] = np.concatenate([high, high, low], 0)
        return table

    def selections(self):
        quarters = 128 // self.mx
        own = np.zeros((self.wb, 2, self.ll, 2, quarters, self.mx), np.float32)
        for b in range(self.wb):
            for r in range(2):
                for a in range(self.mx):
                    if a < self.mx // 2:
                        own[b, 0, r * self.span + b * self.na + a, r, :, a] = 1.0
                    else:
                        spot = r * self.span + (self.wb - b) * self.na + self.mx - a
                        own[b, 1, spot, r, :, a] = 1.0 - 2.0 * r
        own = own.reshape(self.wb, 2 * self.ll, 256)
        back = np.swapaxes(own, 1, 2)
        return own.astype(ml_dtypes.bfloat16), np.ascontiguousarray(back).astype(ml_dtypes.bfloat16)

    def orders(self):
        table = np.zeros((2, self.rows, self.rt), np.float32)
        for c in range(self.cc):
            for k in range(self.wk):
                table[0, c * self.wk + k, c * self.wk + k] = 1.0
                mirrored = self.wk - k
                spot = self.rows + c if mirrored == self.wk else c * self.wk + mirrored
                table[1, c * self.wk + k, spot] = 1.0
        return table.astype(ml_dtypes.bfloat16)


def halves(table):
    high = table.astype(np.float32).astype(ml_dtypes.bfloat16)
    low = (table - high.astype(np.float64)).astype(np.float32).astype(ml_dtypes.bfloat16)
    return high, low


def dot(left, right, numbers=(((1,), (0,)), ((), ()))):
    return lax.dot_general(left, right, numbers, preferred_element_type=f32)


def split(value):
    high = value.astype(bf16)
    return high, (value - high.astype(f32)).astype(bf16)


def moved(value, chosen, left=False):
    first, second = split(value)
    if left:
        return dot(chosen, first) + dot(chosen, second)
    rows = value.shape[0]
    if rows % 16:
        return dot(first, chosen) + dot(second, chosen)
    both = dot(jnp.concatenate([first, second], axis=0), chosen)
    return both[:rows] + both[rows:]


def depth_analysis(plan, table_ref, values):
    rows = []
    for value in values:
        high, low = split(value)
        rows.append(jnp.concatenate([high, low], axis=1))
    both = dot(table_ref[...], jnp.concatenate(rows, axis=0), NT)
    lines = both[: plan.rc] + both[plan.rc :]
    return [lines[:, j * plan.blk : (j + 1) * plan.blk] for j in range(len(values))]


def depth_synthesis(plan, table_ref, rows):
    high = rows.astype(bf16).astype(f32)
    parts = [high, rows - high, high]
    extra = table_ref.shape[0] - 3 * plan.rc
    if extra:
        parts.append(jnp.zeros((extra, rows.shape[1]), f32))
    return dot(jnp.concatenate(parts, axis=0).astype(bf16), table_ref[...], TN)


def plane_analysis(plan, step, lines_ref, plane_ref, total_ref):
    high, low = split(lines_ref[...].reshape(plan.cc * plan.rc, plan.blk))
    rows = jnp.concatenate([high, low, high], axis=1)
    for start in range(0, 2 * plan.lp, 256):
        size = min(256, 2 * plan.lp - start)
        columns = pl.ds(start, size)
        part = dot(rows, plane_ref[0, :, columns]).reshape(plan.cc, plan.rc, size)

        @pl.when(step == 0)
        def _():
            total_ref[:, :, columns] = part

        @pl.when(step > 0)
        def _():
            total_ref[:, :, columns] += part


def plane_synthesis(plan, high_rows, low_rows, plane_ref, lines_ref):
    high_table, low_table = plane_ref[0, : plan.blk], plane_ref[0, 2 * plan.blk :]
    lines = (
        dot(high_rows[...], high_table, NT)
        + dot(low_rows[...], high_table, NT)
        + dot(high_rows[...], low_table, NT)
    )
    lines_ref[...] = lines.reshape(plan.cc, plan.rc, plan.blk)


def emit_modes(plan, flag_ref, turn_ref, total_ref, keep_ref, send_ref):
    lp, wk, mk, half = plan.lp, plan.wk, plan.mk, plan.half
    odd = flag_ref[0] == 1
    cosine, sine = turn_ref[0:1, :], turn_ref[1:2, :]
    for c in range(plan.cc):
        real, imag = total_ref[c, :, :lp], total_ref[c, :, lp:]
        real, imag = real * cosine + imag * sine, imag * cosine - real * sine
        for first, size, base, shift in ((0, wk, c * wk, mk), (2 * mk, 1, plan.rows + c, half)):
            made = []
            for g in range(plan.ch):
                h = g if g < half else plan.ch - 1 - g
                even_rows = slice(first + h * size, first + (h + 1) * size)
                odd_rows = slice(first + shift + h * size, first + shift + (h + 1) * size)
                if g < half:
                    made.append((real[even_rows] + imag[odd_rows], imag[even_rows] - real[odd_rows]))
                else:
                    made.append((real[even_rows] - imag[odd_rows], imag[even_rows] + real[odd_rows]))
            for pair in range(half):
                for r in range(2):
                    low, high = made[2 * pair][r], made[2 * pair + 1][r]
                    keep_ref[pair, r, base : base + size, :] = jnp.where(odd, high, low)
                    send_ref[pair, r, base : base + size, :] = jnp.where(odd, low, high)
    used = plan.cc * (wk + 1)
    if used < plan.rt:
        blank = jnp.zeros((plan.half, 2, plan.rt - used, lp), f32)
        keep_ref[:, :, used:, :] = blank
        send_ref[:, :, used:, :] = blank


def take_modes(plan, flag_ref, turn_ref, own_ref, other_ref, total_ref, high_rows, low_rows):
    lp, wk, mk, half = plan.lp, plan.wk, plan.mk, plan.half
    odd = flag_ref[0] == 1
    cosine, sine = turn_ref[0:1, :], turn_ref[1:2, :]

    def group(g, r, rows):
        own, other = own_ref[g // 2, r, rows, :], other_ref[g // 2, r, rows, :]
        return jnp.where(odd, own, other) if g % 2 else jnp.where(odd, other, own)

    for c in range(plan.cc):
        for first, size, base, shift in ((0, wk, c * wk, mk), (2 * mk, 1, plan.rows + c, half)):
            rows = slice(base, base + size)
            for h in range(half):
                plus = [group(h, r, rows) for r in range(2)]
                minus = [group(plan.ch - 1 - h, r, rows) for r in range(2)]
                real, imag = plus[0] + minus[0], plus[1] + minus[1]
                here = slice(first + h * size, first + (h + 1) * size)
                total_ref[c, here, :lp] = real * cosine - imag * sine
                total_ref[c, here, lp:] = imag * cosine + real * sine
                real, imag = plus[0] - minus[0], plus[1] - minus[1]
                here = slice(first + shift + h * size, first + shift + (h + 1) * size)
                total_ref[c, here, :lp] = -(imag * cosine + real * sine)
                total_ref[c, here, lp:] = real * cosine - imag * sine
        used = 2 * mk + 2 * half
        if used < plan.rc:
            total_ref[c, used:, :] = jnp.zeros((plan.rc - used, 2 * lp), f32)
    high, low = split(total_ref[...].reshape(plan.cc * plan.rc, 2 * lp))
    high_rows[...] = high
    low_rows[...] = low


def analyse_kernel(plan, flag_ref, values_ref, plane_ref, depth_ref, turn_ref, keep_ref, send_ref, lines_ref, total_ref):
    step = pl.program_id(0)

    @pl.loop(0, plan.cc, step=plan.batch)
    def _(c):
        values = [values_ref[:, c + j].reshape(plan.blk, plan.nz) for j in range(plan.batch)]
        for j, lines in enumerate(depth_analysis(plan, depth_ref, values)):
            lines_ref[c + j] = lines

    plane_analysis(plan, step, lines_ref, plane_ref, total_ref)

    @pl.when(step == pl.num_programs(0) - 1)
    def _():
        emit_modes(plan, flag_ref, turn_ref, total_ref, keep_ref, send_ref)


def fields(plan, inverse_ref, lines_ref, first):
    lines = jnp.concatenate([lines_ref[first + j] for j in range(plan.batch)], axis=1)
    values = depth_synthesis(plan, inverse_ref, lines)
    return [values[j * plan.blk : (j + 1) * plan.blk] for j in range(plan.batch)]


def middle_kernel(
    plan, flag_ref, own_ref, other_ref, linear_ref, cotangent_ref, plane_ref, depth_ref, inverse_ref, turn_ref,
    output_ref, gradient_ref, keep_ref, send_ref, lines_ref, back_ref, total_ref, high_rows, low_rows,
):
    step = pl.program_id(0)

    @pl.when(step == 0)
    def _():
        take_modes(plan, flag_ref, turn_ref, own_ref, other_ref, total_ref, high_rows, low_rows)

    plane_synthesis(plan, high_rows, low_rows, plane_ref, lines_ref)
    shape = (plan.xb, plan.ny, plan.nz)

    @pl.loop(0, plan.cc, step=plan.batch)
    def _(first):
        gradients = []
        for j, field in enumerate(fields(plan, inverse_ref, lines_ref, first)):
            value = field + linear_ref[:, first + j].reshape(plan.blk, plan.nz)
            gate = 0.5 * (1.0 + lax.erf(value * root_half))
            slope = gate + value * jnp.exp(-0.5 * value * value) * inv_root_two_pi
            output_ref[:, first + j] = (value * gate).reshape(shape)
            gradients.append(cotangent_ref[:, first + j].reshape(plan.blk, plan.nz) * slope)
            gradient_ref[:, first + j] = gradients[-1].reshape(shape)
        for j, lines in enumerate(depth_analysis(plan, depth_ref, gradients)):
            back_ref[first + j] = lines

    plane_analysis(plan, step, back_ref, plane_ref, total_ref)

    @pl.when(step == pl.num_programs(0) - 1)
    def _():
        emit_modes(plan, flag_ref, turn_ref, total_ref, keep_ref, send_ref)


def synthesise_kernel(
    plan, flag_ref, own_ref, other_ref, linear_ref, plane_ref, inverse_ref, turn_ref,
    output_ref, lines_ref, total_ref, high_rows, low_rows,
):
    @pl.when(pl.program_id(0) == 0)
    def _():
        take_modes(plan, flag_ref, turn_ref, own_ref, other_ref, total_ref, high_rows, low_rows)

    plane_synthesis(plan, high_rows, low_rows, plane_ref, lines_ref)

    @pl.loop(0, plan.cc, step=plan.batch)
    def _(first):
        for j, field in enumerate(fields(plan, inverse_ref, lines_ref, first)):
            value = field + linear_ref[:, first + j].reshape(plan.blk, plan.nz)
            output_ref[:, first + j] = value.reshape(plan.xb, plan.ny, plan.nz)


def linear_kernel(plan, values_ref, weight_ref, bias_ref, output_ref):
    tiles = [(x, slice(t * 8, (t + 1) * 8)) for x in range(plan.lb) for t in range(plan.ny // 8)]
    values = [values_ref[x, :, t, :].reshape(plan.c * 8, plan.nz) for x, t in tiles]
    high, low = split(jnp.concatenate(values, axis=1))
    size = 8 * plan.c
    row, column = (lax.broadcasted_iota(jnp.int32, (size, plan.c), n) for n in (0, 1))
    repeat = (row // 8 == column).astype(f32)
    exact = partial(lax.dot_general, precision=lax.Precision.HIGHEST, preferred_element_type=f32)
    spread = exact(exact(repeat, weight_ref[...], (((1,), (0,)), ((), ()))), repeat, NT)
    row, column = (lax.broadcasted_iota(jnp.int32, (size, size), n) for n in (0, 1))
    high_matrix, low_matrix = split(jnp.where(row % 8 == column % 8, spread, 0.0))
    bias = exact(repeat, bias_ref[...], (((1,), (1,)), ((), ())))
    matrix = jnp.concatenate([high_matrix, high_matrix, low_matrix], axis=1)
    mixed = dot(matrix, jnp.concatenate([high, low, high], axis=0)) + bias
    for n, (x, t) in enumerate(tiles):
        output_ref[x, :, t, :] = mixed[:, n * plan.nz : (n + 1) * plan.nz].reshape(plan.c, 8, plan.nz)


def pick(plan, own_refs, mirror_refs, order_ref, chosen_ref, ordered_ref):
    @pl.when(pl.program_id(0) == 0)
    def _():
        for n in range(plan.chunks):
            rows = slice(n * plan.rows, (n + 1) * plan.rows)
            ordered_ref[rows, : plan.ll] = moved(own_refs[n][...], order_ref[...], left=True)
            ordered_ref[rows, plan.ll :] = moved(mirror_refs[n][...], order_ref[...], left=True)

    return [moved(ordered_ref[...], chosen_ref[n]) for n in range(plan.bb)]


def give(plan, made_ref, order_ref, back_ref, own_refs, mirror_refs, sums_ref):
    part = moved(made_ref[0], back_ref[0])
    for n in range(1, plan.bb):
        part = part + moved(made_ref[n], back_ref[n])
    step = pl.program_id(0)

    @pl.when(step == 0)
    def _():
        sums_ref[...] = part

    @pl.when(step > 0)
    def _():
        sums_ref[...] += part

    @pl.when(step == pl.num_programs(0) - 1)
    def _():
        for n in range(plan.chunks):
            rows = slice(n * plan.rows, (n + 1) * plan.rows)
            own_refs[n][...] = moved(sums_ref[rows, : plan.ll], order_ref[...], left=True)
            mirror_refs[n][...] = moved(sums_ref[rows, plan.ll :], order_ref[...], left=True)


def mix_kernel(plan, *refs):
    n = plan.chunks
    owns, mirrors, refs = refs[:n], refs[n : 2 * n], refs[2 * n :]
    order_ref, disorder_ref, chosen_ref, back_ref, weight_ref, modes_ref = refs[:6]
    own_outs, mirror_outs, (ordered_ref, made_ref, sums_ref) = refs[6 : 6 + n], refs[6 + n : 6 + 2 * n], refs[6 + 2 * n :]
    wk, quarters = plan.wk, 128 // plan.mx
    picked = pick(plan, owns, mirrors, order_ref, chosen_ref, ordered_ref)
    place = lax.broadcasted_iota(jnp.int32, (wk, 128), 1) // plan.mx
    for n, modes in enumerate(picked):
        modes_ref[n] = modes
        for t in range(plan.c // quarters):
            columns = slice(t * 128, (t + 1) * 128)
            real = imag = 0.0
            for i in range(plan.c):
                x_real, x_imag = modes[i * wk : (i + 1) * wk, :128], modes[i * wk : (i + 1) * wk, 128:]
                w_real, w_imag = weight_ref[n, 0, i, :, columns], weight_ref[n, 1, i, :, columns]
                real = real + (w_real * x_real - w_imag * x_imag)
                imag = imag + (w_real * x_imag + w_imag * x_real)
            for q in range(quarters):
                o = t * quarters + q
                made_ref[n, o * wk : (o + 1) * wk, :128] = jnp.where(place == q, real, 0.0)
                made_ref[n, o * wk : (o + 1) * wk, 128:] = jnp.where(place == q, imag, 0.0)
    give(plan, made_ref, disorder_ref, back_ref, own_outs, mirror_outs, sums_ref)


def mix_back_kernel(plan, *refs):
    n = plan.chunks
    owns, mirrors, refs = refs[:n], refs[n : 2 * n], refs[2 * n :]
    order_ref, disorder_ref, chosen_ref, back_ref, weight_ref, modes_ref, gradient_ref = refs[:7]
    own_outs, mirror_outs, (ordered_ref, made_ref, sums_ref) = refs[7 : 7 + n], refs[7 + n : 7 + 2 * n], refs[7 + 2 * n :]
    wk, quarters = plan.wk, 128 // plan.mx
    picked = pick(plan, owns, mirrors, order_ref, chosen_ref, ordered_ref)
    place = lax.broadcasted_iota(jnp.int32, (wk, 128), 1) // plan.mx
    for n, grads in enumerate(picked):
        lined = []
        for t in range(plan.c // quarters):
            real = imag = 0.0
            for q in range(quarters):
                o = t * quarters + q
                real = jnp.where(place == q, grads[o * wk : (o + 1) * wk, :128], real)
                imag = jnp.where(place == q, grads[o * wk : (o + 1) * wk, 128:], imag)
            lined.append((real, imag))
        for i in range(plan.c):
            rows = slice(i * wk, (i + 1) * wk)
            x_real, x_imag = modes_ref[n, rows, :128], modes_ref[n, rows, 128:]
            back_real = back_imag = 0.0
            for t, (real, imag) in enumerate(lined):
                columns = slice(t * 128, (t + 1) * 128)
                gradient_ref[n, 0, i, :, columns] = real * x_real + imag * x_imag
                gradient_ref[n, 1, i, :, columns] = imag * x_real - real * x_imag
                w_real, w_imag = weight_ref[n, 0, i, :, columns], weight_ref[n, 1, i, :, columns]
                back_real = back_real + (w_real * real + w_imag * imag)
                back_imag = back_imag + (w_real * imag - w_imag * real)
            made_ref[n, rows, :128] = back_real
            made_ref[n, rows, 128:] = back_imag
    give(plan, made_ref, disorder_ref, back_ref, own_outs, mirror_outs, sums_ref)


def halve_kernel(flag_ref, keep_ref, arrived_ref, kept_ref, send_ref):
    odd = flag_ref[0] == 1
    for pair in range(kept_ref.shape[0]):
        low = keep_ref[2 * pair] + arrived_ref[2 * pair]
        high = keep_ref[2 * pair + 1] + arrived_ref[2 * pair + 1]
        kept_ref[pair] = jnp.where(odd, high, low)
        send_ref[pair] = jnp.where(odd, low, high)


def cut_kernel(plan, slab_ref, keep_ref, arrived_ref, *refs):
    out_refs, held_ref = refs[:-1], refs[-1]
    lane = lax.broadcasted_iota(jnp.int32, (plan.rt, plan.ll), 1)
    real = keep_ref[0, 0] + arrived_ref[0, 0]
    imag = keep_ref[0, 1] + arrived_ref[0, 1]
    for g in range(plan.s):
        first = pltpu.roll(real, (plan.lp - g * plan.span) % plan.lp, 1)[:, : plan.ll]
        second = pltpu.roll(imag, (plan.lp - g * plan.span + plan.span) % plan.lp, 1)[:, : plan.ll]
        held_ref[g] = jnp.where(lane < plan.span, first, jnp.where(lane < 2 * plan.span, second, 0.0))
    for j, out_ref in enumerate(out_refs):
        out_ref[...] = held_ref[slab_ref[0] ^ j]


def join_kernel(plan, slab_ref, *refs):
    piece_refs, total_ref, held_ref = refs[:-2], refs[-2], refs[-1]
    for j, piece_ref in enumerate(piece_refs):
        held_ref[j] = piece_ref[...]
    lane = lax.broadcasted_iota(jnp.int32, (plan.rt, plan.lp), 1)
    real = imag = jnp.zeros((plan.rt, plan.lp), f32)
    blank = jnp.zeros((plan.rt, plan.lp - plan.ll), f32)
    for g in range(plan.s):
        piece = jnp.concatenate([held_ref[slab_ref[0] ^ g], blank], axis=1)
        here = (lane >= g * plan.span) & (lane < (g + 1) * plan.span)
        real = jnp.where(here, pltpu.roll(piece, g * plan.span, 1), real)
        imag = jnp.where(here, pltpu.roll(piece, (g * plan.span - plan.span) % plan.lp, 1), imag)
    total_ref[0, 0] = real
    total_ref[0, 1] = imag


def whole(array):
    zeros = (0,) * array.ndim
    return pl.BlockSpec(array.shape, lambda i: zeros, pipeline_mode=pl.Buffered(1))


def whole_shape(shape):
    zeros = (0,) * len(shape)
    return pl.BlockSpec(shape, lambda i: zeros, pipeline_mode=pl.Buffered(1))


def leading(shape):
    rest = (0,) * (len(shape) - 1)
    return pl.BlockSpec(shape, lambda i: (i,) + rest)


def shaped(*shape):
    return jax.ShapeDtypeStruct(shape, f32)


def anywhere():
    return pl.BlockSpec(memory_space=pl.ANY)


def scalar():
    return pl.BlockSpec(memory_space=pltpu.SMEM)


def call(kernel, name, grid, in_specs, out_specs, out_shape, scratch, cost, before=(), aliases=None):
    skipped = len(before)
    run = pl.pallas_call(
        lambda *refs: kernel(*refs[skipped:]),
        grid=(grid,),
        in_specs=[anywhere()] * skipped + list(in_specs),
        out_specs=out_specs,
        out_shape=out_shape,
        scratch_shapes=scratch,
        name=name,
        input_output_aliases=aliases or {},
        compiler_params=pltpu.CompilerParams(vmem_limit_bytes=VMEM_LIMIT, dimension_semantics=("arbitrary",)),
        cost_estimate=pl.CostEstimate(flops=int(cost * 1.15e9), bytes_accessed=int(cost * 3.6e6), transcendentals=0),
    )
    return partial(run, *before)


def tie(value, *before):
    if not before:
        return value
    return pl.pallas_call(
        lambda *refs: None,
        in_specs=[anywhere()] * (1 + len(before)),
        out_specs=anywhere(),
        out_shape=jax.ShapeDtypeStruct(value.shape, value.dtype),
        input_output_aliases={0: 0},
        name="tie",
    )(value, *before)


class Program:
    def __init__(self, plan):
        self.plan = plan
        self.plane = jnp.asarray(plan.plane_table())
        self.depth = jnp.asarray(plan.depth_forward())
        self.inverse = jnp.asarray(plan.depth_inverse())
        slab, chan = lax.axis_index("slab"), lax.axis_index("chan")
        self.slab, self.chan = slab, chan
        turns = jnp.asarray(plan.turns())
        self.turn = lax.dynamic_index_in_dim(
            lax.dynamic_index_in_dim(turns, slab, 0, False), chan, 0, False
        )
        self.slab_index = slab.astype(jnp.int32).reshape(1)
        self.flag = (chan % 2).astype(jnp.int32).reshape(1)
        orders = jnp.asarray(plan.orders())
        upper = (chan >= plan.half).astype(jnp.int32)
        self.order = lax.dynamic_index_in_dim(orders, upper, 0, False)
        self.disorder = self.order.T
        chosen, back = plan.selections()
        self.chosen, self.back = jnp.asarray(chosen), jnp.asarray(back)

    def half_shape(self):
        plan = self.plan
        return (plan.half, 2, plan.rt, plan.lp)

    def field_spec(self, chunk):
        plan = self.plan
        return pl.BlockSpec((plan.xb, plan.cc, plan.ny, plan.nz), lambda i: (i, chunk, 0, 0))

    def table(self):
        plan = self.plan
        return leading((1, 3 * plan.blk, 2 * plan.lp))

    def lines(self):
        plan = self.plan
        return pltpu.VMEM((plan.cc, plan.rc, plan.blk), f32)

    def spectra(self):
        plan = self.plan
        rows = pltpu.VMEM((plan.cc * plan.rc, 2 * plan.lp), bf16)
        return [pltpu.VMEM((plan.cc, plan.rc, 2 * plan.lp), f32), rows, rows]

    def analyse(self, chunk, before, values):
        plan = self.plan
        half = self.half_shape()
        return call(
            partial(analyse_kernel, plan), "analyse", plan.nx // plan.xb,
            [scalar(), self.field_spec(chunk), self.table(), whole(self.depth), whole(self.turn)],
            [whole_shape(half)] * 2, [shaped(*half)] * 2,
            [self.lines(), self.spectra()[0]], 14, before,
        )(self.flag, values, self.plane, self.depth, self.turn)

    def middle(self, chunk, before, filled, own, other, linear, cotangent):
        plan = self.plan
        half = self.half_shape()
        field, spec = shaped(plan.nx, plan.c, plan.ny, plan.nz), self.field_spec(chunk)
        return call(
            partial(middle_kernel, plan), "middle", plan.nx // plan.xb,
            [scalar(), whole_shape(half), whole_shape(half), spec, spec, self.table(),
             whole(self.depth), whole(self.inverse), whole(self.turn)],
            [spec, spec, whole_shape(half), whole_shape(half)],
            [field, field, shaped(*half), shaped(*half)],
            [self.lines(), self.lines(), *self.spectra()], 24,
            (*filled, *before), {n: n for n in range(len(filled))},
        )(self.flag, own, other, linear, cotangent, self.plane, self.depth, self.inverse, self.turn)

    def synthesise(self, chunk, before, filled, own, other, linear):
        plan = self.plan
        half = self.half_shape()
        spec = self.field_spec(chunk)
        return call(
            partial(synthesise_kernel, plan), "synthesise", plan.nx // plan.xb,
            [scalar(), whole_shape(half), whole_shape(half), spec, self.table(),
             whole(self.inverse), whole(self.turn)],
            [spec], [shaped(plan.nx, plan.c, plan.ny, plan.nz)],
            [self.lines(), *self.spectra()], 10,
            (*filled, *before), {n: n for n in range(len(filled))},
        )(self.flag, own, other, linear, self.plane, self.inverse, self.turn)

    def linear(self, before, values, matrix, bias):
        plan = self.plan
        bias = bias[None]
        spec = leading((plan.lb, plan.c, plan.ny, plan.nz))
        return call(
            partial(linear_kernel, plan), "linear", plan.nx // plan.lb,
            [spec, whole(matrix), whole(bias)],
            spec, shaped(plan.nx, plan.c, plan.ny, plan.nz), [],
            12, before,
        )(values, matrix, bias)

    def mix_specs(self):
        plan = self.plan
        modes = (plan.rt, plan.ll)
        ins = [
            *[whole_shape(modes)] * (2 * plan.chunks), whole(self.order), whole(self.disorder),
            leading((plan.bb,) + self.chosen.shape[1:]), leading((plan.bb,) + self.back.shape[1:]),
            leading((plan.bb, 2, plan.c, plan.wk, plan.c * plan.mx)),
        ]
        scratch = [
            pltpu.VMEM((plan.c * plan.wk, 2 * plan.ll), f32),
            pltpu.VMEM((plan.bb, plan.c * plan.wk, 256), f32),
            pltpu.VMEM((plan.c * plan.wk, 2 * plan.ll), f32),
        ]
        count = 2 * plan.chunks
        return ins, [whole_shape(modes)] * count, [shaped(*modes)] * count, scratch

    def mix(self, before, owns, mirrors, weights):
        plan = self.plan
        ins, outs, shapes, scratch = self.mix_specs()
        rows = plan.c * plan.wk
        modes, *made = call(
            partial(mix_kernel, plan), "mix", plan.wb // plan.bb, ins, [leading((plan.bb, rows, 256)), *outs],
            [shaped(plan.wb, rows, 256), *shapes], scratch, 13, before,
        )(*owns, *mirrors, self.order, self.disorder, self.chosen, self.back, weights)
        return modes, made[: plan.chunks], made[plan.chunks :]

    def mix_back(self, before, owns, mirrors, weights, modes):
        plan = self.plan
        ins, outs, shapes, scratch = self.mix_specs()
        kept = leading((plan.bb, plan.c * plan.wk, 256))
        gradient, *made = call(
            partial(mix_back_kernel, plan), "mix_back", plan.wb // plan.bb, ins + [kept], [ins[-1], *outs],
            [shaped(*weights.shape), *shapes], scratch, 14, before,
        )(*owns, *mirrors, self.order, self.disorder, self.chosen, self.back, weights, modes)
        return gradient, made[: plan.chunks], made[plan.chunks :]

    def across(self, value, axis, bit):
        size = lax.axis_size(axis)
        return lax.ppermute(value, axis, [(i, i ^ bit) for i in range(size)])

    def mirrored(self, value):
        total = self.plan.s * self.plan.ch
        return lax.ppermute(value, ("slab", "chan"), [(i, total - 1 - i) for i in range(total)])

    def sums_over_chan(self, keep, send):
        plan = self.plan
        arrived = self.across(send, "chan", 1)
        bit = 2
        while bit < plan.ch:
            mine = ((self.chan // bit) % 2).astype(jnp.int32).reshape(1)
            half = (keep.shape[0] // 2,) + keep.shape[1:]
            keep, send = call(
                halve_kernel, "halve", 1, [scalar(), whole(keep), whole(keep)], [whole_shape(half)] * 2,
                [shaped(*half)] * 2, [], 2,
            )(mine, keep, arrived)
            arrived = self.across(send, "chan", bit)
            bit *= 2
        return keep, send, arrived

    def sums_over_slab(self, keep, arrived):
        plan = self.plan
        size = (plan.rt, plan.ll)
        mine, *pieces = call(
            partial(cut_kernel, plan), "cut", 1, [scalar(), whole(keep), whole(keep)],
            [whole_shape(size)] * plan.s, [shaped(*size)] * plan.s, [pltpu.VMEM((plan.s, *size), f32)], 2,
        )(self.slab_index, keep, arrived)
        for j, piece in enumerate(pieces):
            mine = mine + self.across(piece, "slab", j + 1)
        return mine

    def gather_chunks(self, run, linear):
        arrived, before, owns, mirrors, mixed = [], [], [], [], None
        sums = []
        for n in range(self.plan.chunks):
            keep, send = run(n, before)
            sums.append(self.sums_over_chan(keep, tie(send, *arrived)))
            arrived, before = [sums[-1][2]], [sums[-1][1]]
        for n, (keep, _, arrived) in enumerate(sums):
            if n == self.plan.chunks - 1:
                mixed = linear(before)
                arrived = tie(arrived, mixed, *owns)
            else:
                arrived = tie(arrived, sums[n + 1][1])
            owns.append(self.sums_over_slab(keep, arrived))
            mirrors.append(self.mirrored(owns[-1]))
        return owns, mirrors, mixed

    def spread_over_slab(self, owns, mirrors):
        plan = self.plan
        totals = []
        sums = [own + self.mirrored(mirror) for own, mirror in zip(owns, mirrors)]
        for mine in sums:
            mine = tie(mine, *totals[-1:])
            arrived = [self.across(mine, "slab", j) for j in range(1, plan.s)]
            total = (1, 2, plan.rt, plan.lp)
            totals.append(call(
                partial(join_kernel, plan), "join", 1, [scalar()] + [whole(mine)] * plan.s,
                whole_shape(total), shaped(*total), [pltpu.VMEM((plan.s, *mine.shape), f32)], 2,
            )(self.slab_index, mine, *arrived))
        return totals

    def spread_chunks(self, owns, mirrors):
        plan = self.plan
        totals = self.spread_over_slab(owns, mirrors)
        sent, arrived = [], []
        for total in totals:
            sent.append(tie(total, *arrived[-1:]))
            arrived.append(self.across(sent[-1], "chan", plan.ch // 2) if plan.ch > 2 else sent[-1])

        def take(n, before):
            total, other = sent[n], tie(arrived[n], *(before or sent[1:]))
            bit = plan.ch // 2
            while bit > 1:
                upper = (self.chan // bit) % 2 == 1
                total = jnp.stack([jnp.where(upper, other, total), jnp.where(upper, total, other)], axis=1)
                total = total.reshape((-1,) + total.shape[2:])
                bit //= 2
                other = self.across(total, "chan", bit)
            return total, other

        return take


def local(inputs, cotangent, spectral, local_weight, bias_vector):
    nx, ny, channels, nz = inputs.shape
    wb, wk = spectral.shape[0], spectral.shape[1]
    plan = Plan(nx, ny, nz, channels, wb, wk, spectral.shape[4] // channels, lax.axis_size("slab"), lax.axis_size("chan"))
    program = Program(plan)
    values = jnp.transpose(inputs, (0, 2, 1, 3))
    slopes = jnp.transpose(cotangent, (0, 2, 1, 3))
    weights = jnp.transpose(spectral, (0, 2, 3, 1, 4))

    owns, mirrors, linear = program.gather_chunks(
        lambda n, before: program.analyse(n, before, values),
        lambda before: program.linear(before, values, local_weight.T, bias_vector),
    )
    modes, owns, mirrors = program.mix([linear], owns, mirrors, weights)

    take = program.spread_chunks(owns, mirrors)
    filled = []

    def middle(n, before):
        own, other = take(n, filled[2:])
        output, gradient, keep, send = program.middle(n, before, filled[:2], own, other, linear, slopes)
        filled[:] = [output, gradient, keep]
        return keep, send

    owns, mirrors, mixed = program.gather_chunks(
        middle, lambda before: program.linear(before, filled[1], local_weight, jnp.zeros_like(bias_vector))
    )
    output = filled[0]
    grad_spectral, owns, mirrors = program.mix_back([mixed], owns, mirrors, weights, modes)
    grad_spectral = tie(jnp.transpose(grad_spectral, (0, 3, 2, 1, 4)), owns[0])

    take = program.spread_chunks(owns, mirrors)
    made = []
    for n in range(plan.chunks):
        own, other = take(n, made)
        made = program.synthesise(n, [grad_spectral], made, own, other, mixed)
    (grad_inputs,) = made
    return (
        jnp.transpose(output, (0, 2, 1, 3)),
        jnp.transpose(grad_inputs, (0, 2, 1, 3)),
        jnp.transpose(grad_spectral, (0, 1, 3, 2, 4)),
    )


def solution(mesh):
    in_specs = (
        P(("groups", "slab"), "chan", None, None),
        P(("groups", "slab"), "chan", None, None),
        P("slab", "chan", None, None, None),
        P(),
        P(),
    )
    out_specs = (
        P(("groups", "slab"), "chan", None, None),
        P(("groups", "slab"), "chan", None, None),
        P(("groups", "slab"), "chan", None, None, None),
    )
    return jax.shard_map(local, mesh=mesh, in_specs=in_specs, out_specs=out_specs, check_vma=False)
```

profile of v0, /device:TPU:0, one launch (start us, length us, event | category | flops | bytes accessed | tf_op | source)
XLA Modules:
  0.0 405.5 jit_solution(5765850405911403650)
XLA Ops:
  1.9 16.0 %analyse.2 = (f32[2,2,96,640]{3,2,1,0:T(8,128)}, f32[2,2,96,640]{3,2,1,0:T(8,128)}) custom-call(s32[1]{0:T(128)} %bitcast.refs_0_.refs_1_.refs_3_.refs_2_, f32[32,20,32,128]{3,2,1,0:T(8,128)} %bitcast.53, bf16[4,768,1280]{2,1,0:T(8,128)(2,1)} %constant.114.clone.refs_2_.refs_3_.refs_5_.refs_8_.refs_6_, ...), custom_call_target="tpu_custom_call" | custom-call | flops 16099999744 | bytes 50400000 | tf_op jit(solution)/shard_map/analyse/pallas_call | solution.py:585
  27.2 16.0 %analyse.3 = (f32[2,2,96,640]{3,2,1,0:T(8,128)}, f32[2,2,96,640]{3,2,1,0:T(8,128)}) custom-call(f32[1,2,96,640]{3,2,1,0:T(8,128)} %get-tuple-element.51.refs_0_, s32[1]{0:T(128)} %bitcast.refs_0_.refs_1_.refs_3_.refs_2_, f32[32,20,32,128]{3,2,1,0:T(8,128)} %bitcast.54, bf16[4,768,1280]{2,1,0:T(8,128)(2,1)} %constant.114.clone.refs_2_.refs_3_.refs_5_.refs_8_.refs_6_, ...), custom_call_target="tpu_custom_call" | custom-call | flops 16099999744 | bytes 50400000 | tf_op jit(solution)/shard_map/analyse/pallas_call | solution.py:585
  57.3 14.2 %linear.2.refs_1_.refs_0_.refs_3_.refs_6_ = f32[32,20,32,128]{3,2,1,0:T(8,128)} custom-call(f32[1,2,96,640]{3,2,1,0:T(8,128)} %get-tuple-element.54.refs_0_.refs_1_, f32[32,20,32,128]{3,2,1,0:T(8,128)} %bitcast.55, f32[20,20]{1,0:T(8,128)} %bitcast.52, f32[1,20]{1,0:T(1,128)} %bitcast.58), custom_call_target="tpu_custom_call" | custom-call | flops 13799999488 | bytes 43200000 | tf_op jit(solution)/shard_map/linear/pallas_call | solution.py:623
  76.2 3.5 collective-permute-start.8
  82.4 11.3 %collective-permute-done.8 = f32[96,384]{1,0:T(8,128)S(1)} collective-permute-done((f32[96,384]{1,0:T(8,128)}, f32[96,384]{1,0:T(8,128)S(1)}, u32[]{:S(2)}, u32[]{:S(2)}) %collective-permute-start.8) | collective-permute-done | bytes 147488 | tf_op jit(solution)/shard_map/ppermute | solution.py:668
  96.1 6.8 %copy.41 = f32[8,8,2,20,640]{4,1,3,2,0:T(8,128)} copy(f32[8,8,2,20,640]{4,2,3,1,0:T(2,128)} %param.14) | data formatting | bytes 13107200 | tf_op args[2]
  103.6 9.0 %mix.1 = (f32[8,160,256]{2,1,0:T(8,128)}, f32[96,384]{1,0:T(8,128)}, f32[96,384]{1,0:T(8,128)}, f32[96,384]{1,0:T(8,128)}, f32[96,384]{1,0:T(8,128)}) custom-call(f32[32,20,32,128]{3,2,1,0:T(8,128)} %linear.2.refs_1_.refs_0_.refs_3_.refs_6_, f32[96,384]{1,0:T(8,128)} %add_add_fusion.3.refs_2_.refs_1_, f32[96,384]{1,0:T(8,128)} %copy-done.21, ...), custom_call_target="tpu_custom_call" | custom-call | flops 14949999616 | bytes 46800000 | tf_op jit(solution)/shard_map/mix/pallas_call | solution.py:650
  112.6 4.5 %collective-permute-start.12 = (f32[96,384]{1,0:T(8,128)}, f32[96,384]{1,0:T(8,128)S(1)}, u32[]{:S(2)}, u32[]{:S(2)}) collective-permute-start(f32[96,384]{1,0:T(8,128)} %get-tuple-element.66), channel_id=1, source_target_pairs={{0,15},{1,14},{2,13},{3,12},{4,11},{5,10},{6,9},{7,8},{8,7},{9,6},... | collective-permute-start | bytes 442376 | tf_op jit(solution)/shard_map/ppermute | solution.py:672
  121.1 4.5 %collective-permute-start.13 = (f32[96,384]{1,0:T(8,128)S(1)}, f32[96,384]{1,0:T(8,128)S(1)}, u32[]{:S(2)}, u32[]{:S(2)}) collective-permute-start(f32[96,384]{1,0:T(8,128)S(1)} %add.90.refs_1_), channel_id=1, source_target_pairs={{0,4},{4,0},{8,12},{12,8},{1,5},{5,1},{9,13},{13,9},{2,6},{6,2},{1... | collective-permute-start | bytes 442376 | tf_op jit(solution)/shard_map/ppermute | solution.py:668
  131.3 11.5 %collective-permute-done.14.refs_3_ = f32[96,384]{1,0:T(8,128)S(1)} collective-permute-done((f32[96,384]{1,0:T(8,128)S(1)}, f32[96,384]{1,0:T(8,128)S(1)}, u32[]{:S(2)}, u32[]{:S(2)}) %collective-permute-start.14) | collective-permute-done | bytes 147488 | tf_op jit(solution)/shard_map/ppermute | solution.py:668
  157.2 8.8 %collective-permute-done.19.refs_3_ = f32[96,384]{1,0:T(8,128)S(1)} collective-permute-done((f32[96,384]{1,0:T(8,128)}, f32[96,384]{1,0:T(8,128)S(1)}, u32[]{:S(2)}, u32[]{:S(2)}) %collective-permute-start.19) | collective-permute-done | bytes 147488 | tf_op jit(solution)/shard_map/ppermute | solution.py:668
  175.2 26.0 %middle.2 = (f32[32,20,32,128]{3,2,1,0:T(8,128)}, f32[32,20,32,128]{3,2,1,0:T(8,128)}, f32[2,2,96,640]{3,2,1,0:T(8,128)}, f32[2,2,96,640]{3,2,1,0:T(8,128)}) custom-call(s32[1]{0:T(128)} %bitcast.refs_0_.refs_1_.refs_3_.refs_2_, f32[2,2,96,640]{3,2,1,0:T(8,128)} %copy-done.13, f32[2,2,96,640]{3,2,1,0:T(8,128)} %copy-done.31, ...), custom_call_target="tpu_custom_call" | custom-call | flops 27599998976 | bytes 86400000 | tf_op jit(solution)/shard_map/middle/pallas_call | solution.py:596
  209.0 25.7 %middle.3 = (f32[32,20,32,128]{3,2,1,0:T(8,128)}, f32[32,20,32,128]{3,2,1,0:T(8,128)}, f32[2,2,96,640]{3,2,1,0:T(8,128)}, f32[2,2,96,640]{3,2,1,0:T(8,128)}) custom-call(f32[32,20,32,128]{3,2,1,0:T(8,128)} %get-tuple-element.69.refs_0_, f32[32,20,32,128]{3,2,1,0:T(8,128)} %get-tuple-element.70.refs_1_, ...), custom_call_target="tpu_custom_call", output_to_operand_aliasing={{0}: (0, {}), {1}: (1, {})} | custom-call | flops 27599998976 | bytes 86400000 | tf_op jit(solution)/shard_map/middle/pallas_call | solution.py:596
  250.6 14.2 %linear.3.refs_1_.refs_0_.refs_4_.refs_5_ = f32[32,20,32,128]{3,2,1,0:T(8,128)} custom-call(f32[1,2,96,640]{3,2,1,0:T(8,128)} %get-tuple-element.77.refs_0_.refs_1_, f32[32,20,32,128]{3,2,1,0:T(8,128)} %get-tuple-element.78.refs_1_, f32[20,20]{1,0:T(8,128)} %refs_2_.2, f32[1,20]{1,0:T(1,128)} %broadcast_1_refs_3_.2.refs_3_), custom_call_target="tpu_custom_call" | custom-call | flops 13799999488 | bytes 43200000 | tf_op jit(solution)/shard_map/linear/pallas_call | solution.py:623
  275.6 10.4 %collective-permute-done.32 = f32[96,384]{1,0:T(8,128)S(1)} collective-permute-done((f32[96,384]{1,0:T(8,128)}, f32[96,384]{1,0:T(8,128)S(1)}, u32[]{:S(2)}, u32[]{:S(2)}) %collective-permute-start.32) | collective-permute-done | bytes 147488 | tf_op jit(solution)/shard_map/ppermute | solution.py:668
  287.0 7.2 %collective-permute-done.35.refs_4_ = f32[96,384]{1,0:T(8,128)S(1)} collective-permute-done((f32[96,384]{1,0:T(8,128)S(1)}, f32[96,384]{1,0:T(8,128)S(1)}, u32[]{:S(2)}, u32[]{:S(2)}) %collective-permute-start.35) | collective-permute-done | bytes 147488 | tf_op jit(solution)/shard_map/ppermute | solution.py:672
  294.9 11.2 %mix_back.1 = (f32[8,2,20,8,640]{4,3,2,1,0:T(8,128)}, f32[96,384]{1,0:T(8,128)}, f32[96,384]{1,0:T(8,128)}, f32[96,384]{1,0:T(8,128)}, f32[96,384]{1,0:T(8,128)}) custom-call(f32[32,20,32,128]{3,2,1,0:T(8,128)} %linear.3.refs_1_.refs_0_.refs_4_.refs_5_, f32[96,384]{1,0:T(8,128)} %add_add_fusion.1.refs_2_.refs_1_, f32[96,384]{1,0:T(8,128)} %copy-done.24, ...), custom_call_target="tpu_custom_call" | custom-call | flops 16099999744 | bytes 50400000 | tf_op jit(solution)/shard_map/mix_back/pallas_call | solution.py:660
  306.5 7.1 %collective-permute-done.36 = f32[96,384]{1,0:T(8,128)S(1)} collective-permute-done((f32[96,384]{1,0:T(8,128)}, f32[96,384]{1,0:T(8,128)S(1)}, u32[]{:S(2)}, u32[]{:S(2)}) %collective-permute-start.36) | collective-permute-done | bytes 147488 | tf_op jit(solution)/shard_map/ppermute | solution.py:672
  314.6 3.7 collective-permute-start.37
  324.8 10.6 %collective-permute-done.38.refs_3_ = f32[96,384]{1,0:T(8,128)S(1)} collective-permute-done((f32[96,384]{1,0:T(8,128)S(1)}, f32[96,384]{1,0:T(8,128)S(1)}, u32[]{:S(2)}, u32[]{:S(2)}) %collective-permute-start.38) | collective-permute-done | bytes 147488 | tf_op jit(solution)/shard_map/ppermute | solution.py:668
  350.1 7.8 %collective-permute-done.43.refs_3_ = f32[96,384]{1,0:T(8,128)S(1)} collective-permute-done((f32[96,384]{1,0:T(8,128)}, f32[96,384]{1,0:T(8,128)S(1)}, u32[]{:S(2)}, u32[]{:S(2)}) %collective-permute-start.43) | collective-permute-done | bytes 147488 | tf_op jit(solution)/shard_map/ppermute | solution.py:668
  363.5 11.0 %copy.40 = f32[8,2,20,8,640]{4,1,2,3,0:T(2,128)} copy(f32[8,2,20,8,640]{4,3,2,1,0:T(8,128)} %get-tuple-element.90) | data formatting | bytes 13107200 | tf_op jit(solution)/shard_map/mix_back/pallas_call | solution.py:660
  376.2 11.9 %synthesise.2.refs_1_.refs_0_ = f32[32,20,32,128]{3,2,1,0:T(8,128)} custom-call(f32[8,8,20,2,640]{4,3,2,1,0:T(2,128)} %tie.25.refs_0_.refs_1_, s32[1]{0:T(128)} %bitcast.refs_0_.refs_1_.refs_3_.refs_2_, f32[2,2,96,640]{3,2,1,0:T(8,128)} %copy-done.12, f32[2,2,96,640]{3,2,1,0:T(8,128)} %copy-done.30, ...), custom_call_target="tpu_custom_call" | custom-call | flops 11500000256 | bytes 36000000 | tf_op jit(solution)/shard_map/synthesise/pallas_call | solution.py:610
  393.6 11.8 %synthesise.3 = f32[32,20,32,128]{3,2,1,0:T(8,128)} custom-call(f32[32,20,32,128]{3,2,1,0:T(8,128)} %synthesise.2.refs_1_.refs_0_, f32[8,8,20,2,640]{4,3,2,1,0:T(2,128)} %tie.25.refs_0_.refs_1_, s32[1]{0:T(128)} %bitcast.refs_0_.refs_1_.refs_3_.refs_2_, f32[2,2,96,640]{3,2,1,0:T(8,128)} %copy-done.4, ...), custom_call_target="tpu_custom_call", output_to_operand_aliasing={{}: (0, {})} | custom-call | flops 11500000256 | bytes 36000000 | tf_op jit(solution)/shard_map/synthesise/pallas_call | solution.py:610
  (232 shorter events, 139.8 us)
Async XLA Ops:
  24.3 18.9 %collective-permute-start.1 = (f32[1,2,96,640]{3,2,1,0:T(8,128)}, f32[1,2,96,640]{3,2,1,0:T(8,128)S(1)}, u32[]{:S(2)}, u32[]{:S(2)}) collective-permute-start(f32[1,2,96,640]{3,2,1,0:T(8,128)} %get-tuple-element.51.refs_0_), channel_id=1, source_target_pairs={{0,2},{1,3},{2,0},{3,1},{4,6},{5,7},{6,4},{7,5},{8,10},{9,11},{10,... | collective-permute-start | bytes 1474568 | tf_op jit(solution)/shard_map/ppermute | solution.py:668
  50.3 21.9 %collective-permute-start.6 = (f32[1,2,96,640]{3,2,1,0:T(8,128)}, f32[1,2,96,640]{3,2,1,0:T(8,128)S(1)}, u32[]{:S(2)}, u32[]{:S(2)}) collective-permute-start(f32[1,2,96,640]{3,2,1,0:T(8,128)} %get-tuple-element.54.refs_0_.refs_1_), channel_id=1, source_target_pairs={{0,2},{1,3},{2,0},{3,1},{4,6},{5,7},{6,4},{7,5},{8,10},{9,11},{10,... | collective-permute-start | bytes 1474568 | tf_op jit(solution)/shard_map/ppermute | solution.py:668
  52.6 18.9 %collective-permute-start.3 = (f32[96,384]{1,0:T(8,128)}, f32[96,384]{1,0:T(8,128)S(1)}, u32[]{:S(2)}, u32[]{:S(2)}) collective-permute-start(f32[96,384]{1,0:T(8,128)} %get-tuple-element.57), channel_id=1, source_target_pairs={{0,4},{4,0},{8,12},{12,8},{1,5},{5,1},{9,13},{13,9},{2,6},{6,2},{1... | collective-permute-start | bytes 442376 | tf_op jit(solution)/shard_map/ppermute | solution.py:668
  54.7 16.8 %collective-permute-start.4 = (f32[96,384]{1,0:T(8,128)}, f32[96,384]{1,0:T(8,128)S(1)}, u32[]{:S(2)}, u32[]{:S(2)}) collective-permute-start(f32[96,384]{1,0:T(8,128)} %get-tuple-element.58), channel_id=1, source_target_pairs={{0,8},{4,12},{8,0},{12,4},{1,9},{5,13},{9,1},{13,5},{2,10},{6,14},... | collective-permute-start | bytes 442376 | tf_op jit(solution)/shard_map/ppermute | solution.py:668
  57.3 14.2 %collective-permute-start.5 = (f32[96,384]{1,0:T(8,128)}, f32[96,384]{1,0:T(8,128)S(1)}, u32[]{:S(2)}, u32[]{:S(2)}) collective-permute-start(f32[96,384]{1,0:T(8,128)} %get-tuple-element.59), channel_id=1, source_target_pairs={{0,12},{4,8},{8,4},{12,0},{1,13},{5,9},{9,5},{13,1},{2,14},{6,10},... | collective-permute-start | bytes 442376 | tf_op jit(solution)/shard_map/ppermute | solution.py:668
  76.2 17.5 %collective-permute-start.8 = (f32[96,384]{1,0:T(8,128)}, f32[96,384]{1,0:T(8,128)S(1)}, u32[]{:S(2)}, u32[]{:S(2)}) collective-permute-start(f32[96,384]{1,0:T(8,128)} %get-tuple-element.63), channel_id=1, source_target_pairs={{0,8},{4,12},{8,0},{12,4},{1,9},{5,13},{9,1},{13,5},{2,10},{6,14},... | collective-permute-start | bytes 442376 | tf_op jit(solution)/shard_map/ppermute | solution.py:668
  79.7 14.1 %collective-permute-start.9 = (f32[96,384]{1,0:T(8,128)}, f32[96,384]{1,0:T(8,128)S(1)}, u32[]{:S(2)}, u32[]{:S(2)}) collective-permute-start(f32[96,384]{1,0:T(8,128)} %get-tuple-element.64), channel_id=1, source_target_pairs={{0,12},{4,8},{8,4},{12,0},{1,13},{5,9},{9,5},{13,1},{2,14},{6,10},... | collective-permute-start | bytes 442376 | tf_op jit(solution)/shard_map/ppermute | solution.py:668
  79.7 23.2 %collective-permute-start.10 = (f32[96,384]{1,0:T(8,128)S(1)}, f32[96,384]{1,0:T(8,128)S(1)}, u32[]{:S(2)}, u32[]{:S(2)}) collective-permute-start(f32[96,384]{1,0:T(8,128)S(1)} %copy-done.15), channel_id=1, source_target_pairs={{0,15},{1,14},{2,13},{3,12},{4,11},{5,10},{6,9},{7,8},{8,7},{9,6},... | collective-permute-start | bytes 442376 | tf_op jit(solution)/shard_map/ppermute | solution.py:672
  125.6 17.1 %collective-permute-start.14 = (f32[96,384]{1,0:T(8,128)S(1)}, f32[96,384]{1,0:T(8,128)S(1)}, u32[]{:S(2)}, u32[]{:S(2)}) collective-permute-start(f32[96,384]{1,0:T(8,128)S(1)} %add.90.refs_1_), channel_id=1, source_target_pairs={{0,8},{4,12},{8,0},{12,4},{1,9},{5,13},{9,1},{13,5},{2,10},{6,14},... | collective-permute-start | bytes 442376 | tf_op jit(solution)/shard_map/ppermute | solution.py:668
  126.3 16.5 %collective-permute-start.15 = (f32[96,384]{1,0:T(8,128)S(1)}, f32[96,384]{1,0:T(8,128)S(1)}, u32[]{:S(2)}, u32[]{:S(2)}) collective-permute-start(f32[96,384]{1,0:T(8,128)S(1)} %add.90.refs_1_), channel_id=1, source_target_pairs={{0,12},{4,8},{8,4},{12,0},{1,13},{5,9},{9,5},{13,1},{2,14},{6,10},... | collective-permute-start | bytes 442376 | tf_op jit(solution)/shard_map/ppermute | solution.py:668
  128.1 19.3 %collective-permute-start.17 = (f32[96,384]{1,0:T(8,128)}, f32[96,384]{1,0:T(8,128)S(1)}, u32[]{:S(2)}, u32[]{:S(2)}) collective-permute-start(f32[96,384]{1,0:T(8,128)} %get-tuple-element.68), channel_id=1, source_target_pairs={{0,15},{1,14},{2,13},{3,12},{4,11},{5,10},{6,9},{7,8},{8,7},{9,6},... | collective-permute-start | bytes 442376 | tf_op jit(solution)/shard_map/ppermute | solution.py:672
  146.3 23.2 %collective-permute-start.16 = (f32[1,2,96,640]{3,2,1,0:T(8,128)}, f32[1,2,96,640]{3,2,1,0:T(8,128)S(1)}, u32[]{:S(2)}, u32[]{:S(2)}) collective-permute-start(f32[1,2,96,640]{3,2,1,0:T(8,128)} %join.4.refs_1_), channel_id=1, source_target_pairs={{0,2},{1,3},{2,0},{3,1},{4,6},{5,7},{6,4},{7,5},{8,10},{9,11},{10,... | collective-permute-start | bytes 1474568 | tf_op jit(solution)/shard_map/ppermute | solution.py:668
  171.6 29.7 %collective-permute-start.23 = (f32[1,2,96,640]{3,2,1,0:T(8,128)}, f32[1,2,96,640]{3,2,1,0:T(8,128)S(1)}, u32[]{:S(2)}, u32[]{:S(2)}) collective-permute-start(f32[1,2,96,640]{3,2,1,0:T(8,128)} %tie.19.refs_1_), channel_id=1, source_target_pairs={{0,2},{1,3},{2,0},{3,1},{4,6},{5,7},{6,4},{7,5},{8,10},{9,11},{10,... | collective-permute-start | bytes 1474568 | tf_op jit(solution)/shard_map/ppermute | solution.py:668
  207.5 27.2 %collective-permute-start.25 = (f32[1,2,96,640]{3,2,1,0:T(8,128)}, f32[1,2,96,640]{3,2,1,0:T(8,128)S(1)}, u32[]{:S(2)}, u32[]{:S(2)}) collective-permute-start(f32[1,2,96,640]{3,2,1,0:T(8,128)} %get-tuple-element.73.refs_2_), channel_id=1, source_target_pairs={{0,2},{1,3},{2,0},{3,1},{4,6},{5,7},{6,4},{7,5},{8,10},{9,11},{10,... | collective-permute-start | bytes 1474568 | tf_op jit(solution)/shard_map/ppermute | solution.py:668
  241.8 23.7 %collective-permute-start.30 = (f32[1,2,96,640]{3,2,1,0:T(8,128)}, f32[1,2,96,640]{3,2,1,0:T(8,128)S(1)}, u32[]{:S(2)}, u32[]{:S(2)}) collective-permute-start(f32[1,2,96,640]{3,2,1,0:T(8,128)} %get-tuple-element.77.refs_0_.refs_1_), channel_id=1, source_target_pairs={{0,2},{1,3},{2,0},{3,1},{4,6},{5,7},{6,4},{7,5},{8,10},{9,11},{10,... | collective-permute-start | bytes 1474568 | tf_op jit(solution)/shard_map/ppermute | solution.py:668
  245.7 19.1 %collective-permute-start.27 = (f32[96,384]{1,0:T(8,128)}, f32[96,384]{1,0:T(8,128)S(1)}, u32[]{:S(2)}, u32[]{:S(2)}) collective-permute-start(f32[96,384]{1,0:T(8,128)} %get-tuple-element.81), channel_id=1, source_target_pairs={{0,4},{4,0},{8,12},{12,8},{1,5},{5,1},{9,13},{13,9},{2,6},{6,2},{1... | collective-permute-start | bytes 442376 | tf_op jit(solution)/shard_map/ppermute | solution.py:668
  247.2 17.6 %collective-permute-start.28 = (f32[96,384]{1,0:T(8,128)}, f32[96,384]{1,0:T(8,128)S(1)}, u32[]{:S(2)}, u32[]{:S(2)}) collective-permute-start(f32[96,384]{1,0:T(8,128)} %get-tuple-element.82), channel_id=1, source_target_pairs={{0,8},{4,12},{8,0},{12,4},{1,9},{5,13},{9,1},{13,5},{2,10},{6,14},... | collective-permute-start | bytes 442376 | tf_op jit(solution)/shard_map/ppermute | solution.py:668
  248.7 16.1 %collective-permute-start.29 = (f32[96,384]{1,0:T(8,128)}, f32[96,384]{1,0:T(8,128)S(1)}, u32[]{:S(2)}, u32[]{:S(2)}) collective-permute-start(f32[96,384]{1,0:T(8,128)} %get-tuple-element.83), channel_id=1, source_target_pairs={{0,12},{4,8},{8,4},{12,0},{1,13},{5,9},{9,5},{13,1},{2,14},{6,10},... | collective-permute-start | bytes 442376 | tf_op jit(solution)/shard_map/ppermute | solution.py:668
  269.2 16.7 %collective-permute-start.32 = (f32[96,384]{1,0:T(8,128)}, f32[96,384]{1,0:T(8,128)S(1)}, u32[]{:S(2)}, u32[]{:S(2)}) collective-permute-start(f32[96,384]{1,0:T(8,128)} %get-tuple-element.87), channel_id=1, source_target_pairs={{0,8},{4,12},{8,0},{12,4},{1,9},{5,13},{9,1},{13,5},{2,10},{6,14},... | collective-permute-start | bytes 442376 | tf_op jit(solution)/shard_map/ppermute | solution.py:668
  271.6 14.3 %collective-permute-start.33 = (f32[96,384]{1,0:T(8,128)}, f32[96,384]{1,0:T(8,128)S(1)}, u32[]{:S(2)}, u32[]{:S(2)}) collective-permute-start(f32[96,384]{1,0:T(8,128)} %get-tuple-element.88), channel_id=1, source_target_pairs={{0,12},{4,8},{8,4},{12,0},{1,13},{5,9},{9,5},{13,1},{2,14},{6,10},... | collective-permute-start | bytes 442376 | tf_op jit(solution)/shard_map/ppermute | solution.py:668
  318.3 17.1 %collective-permute-start.38 = (f32[96,384]{1,0:T(8,128)S(1)}, f32[96,384]{1,0:T(8,128)S(1)}, u32[]{:S(2)}, u32[]{:S(2)}) collective-permute-start(f32[96,384]{1,0:T(8,128)S(1)} %add.98.refs_1_), channel_id=1, source_target_pairs={{0,8},{4,12},{8,0},{12,4},{1,9},{5,13},{9,1},{13,5},{2,10},{6,14},... | collective-permute-start | bytes 442376 | tf_op jit(solution)/shard_map/ppermute | solution.py:668
  319.5 15.9 %collective-permute-start.39 = (f32[96,384]{1,0:T(8,128)S(1)}, f32[96,384]{1,0:T(8,128)S(1)}, u32[]{:S(2)}, u32[]{:S(2)}) collective-permute-start(f32[96,384]{1,0:T(8,128)S(1)} %add.98.refs_1_), channel_id=1, source_target_pairs={{0,12},{4,8},{8,4},{12,0},{1,13},{5,9},{9,5},{13,1},{2,14},{6,10},... | collective-permute-start | bytes 442376 | tf_op jit(solution)/shard_map/ppermute | solution.py:668
  320.9 19.9 %collective-permute-start.41 = (f32[96,384]{1,0:T(8,128)}, f32[96,384]{1,0:T(8,128)S(1)}, u32[]{:S(2)}, u32[]{:S(2)}) collective-permute-start(f32[96,384]{1,0:T(8,128)} %get-tuple-element.94), channel_id=1, source_target_pairs={{0,15},{1,14},{2,13},{3,12},{4,11},{5,10},{6,9},{7,8},{8,7},{9,6},... | collective-permute-start | bytes 442376 | tf_op jit(solution)/shard_map/ppermute | solution.py:672
  338.9 22.5 %collective-permute-start.40 = (f32[1,2,96,640]{3,2,1,0:T(8,128)}, f32[1,2,96,640]{3,2,1,0:T(8,128)S(1)}, u32[]{:S(2)}, u32[]{:S(2)}) collective-permute-start(f32[1,2,96,640]{3,2,1,0:T(8,128)} %join.6.refs_1_), channel_id=1, source_target_pairs={{0,2},{1,3},{2,0},{3,1},{4,6},{5,7},{6,4},{7,5},{8,10},{9,11},{10,... | collective-permute-start | bytes 1474568 | tf_op jit(solution)/shard_map/ppermute | solution.py:668
  (74 other events, 509.5 us)
where the time goes:
time: 407 us; the launch traced here: 405 us
  Pallas kernels  184 us (45%)
  waiting for transfers between devices  98.3 us (24%)
  starting transfers between devices  66.6 us (16%)
  local copies, waits for them, and re-layouts  42.3 us (10%)
  other arithmetic  12.9 us (3%)
    ppermute x40, waiting for transfers between devices, across(): return lax.ppermute(value, axis, [(i, i ^ bit) for i in range(size)])  80.9 us
    ppermute x40, starting transfers between devices, across(): return lax.ppermute(value, axis, [(i, i ^ bit) for i in range(size)])  53.6 us
    pallas_call x2, Pallas kernels, middle(): call(partial(middle_kernel, plan), 'middle', plan.nx // plan.xb, [scalar(...  51.7 us
    pallas_call x2, Pallas kernels, analyse(): call(partial(analyse_kernel, plan), 'analyse', plan.nx // plan.xb, [scala...  32 us
    pallas_call x2, Pallas kernels, linear(): call(partial(linear_kernel, plan), 'linear', plan.nx // plan.lb, [spec, w...  28.3 us
    unnamed x102, local copies, waits for them, and re-layouts  28.2 us
    pallas_call x2, Pallas kernels, synthesise(): call(partial(synthesise_kernel, plan), 'synthesise', plan.nx // plan.xb,...  23.7 us
    ppermute x8, waiting for transfers between devices, mirrored(): lax.ppermute(value, ('slab', 'chan'), [(i, total - 1 - i) for i in range(...  17.5 us
  transfers between devices with their start and end apart: 48, of which 20 were waited for; matrix products, arithmetic and copies ran while one was open for 7% of the time, Pallas kernels for 31%

commit v1 on v0

v1 whole, which is shorter than its diff:
```python
from functools import partial
import math

import jax
import jax.numpy as jnp
import ml_dtypes
import numpy as np
from jax import lax
from jax.experimental import pallas as pl
from jax.experimental.pallas import tpu as pltpu
from jax.sharding import PartitionSpec as P

f32 = jnp.float32
bf16 = jnp.bfloat16
root_half = 0.7071067811865476
inv_root_two_pi = 0.3989422804014327
VMEM_LIMIT = 60 * 1024 * 1024
NT = (((1,), (1,)), ((), ()))
TN = (((0,), (0,)), ((), ()))


def round_up(value, unit):
    return -(-value // unit) * unit


class Plan:
    def __init__(self, nx, ny, nz, channels, wb, wk, mx, slab_count, chan_count):
        self.nx, self.ny, self.nz, self.c = nx, ny, nz, channels
        self.wb, self.wk, self.mx = wb, wk, mx
        self.s, self.ch = slab_count, chan_count
        self.half = chan_count // 2
        self.na = mx // 2 + 1
        self.span = (wb + 1) * self.na
        self.lw = slab_count * self.span
        self.lp = round_up(self.lw, 128)
        self.ll = round_up(2 * self.span, 128)
        self.mk = self.half * wk
        self.rc = round_up(2 * self.mk + 2 * self.half, 8)
        self.chunks = 2
        self.cc = channels
        self.w = (wk // 2, wk - wk // 2)
        self.rts = (round_up(channels * self.w[0], 8), round_up(channels * (self.w[1] + 1), 8))
        self.xb = math.gcd(8, nx)
        self.blk = self.xb * ny
        self.rows = self.cc * wk
        self.bb = math.gcd(2, wb)
        self.lb = math.gcd(4, nx)
        self.batch = max(d for d in range(1, 6) if self.cc % d == 0)
        self.full_x, self.full_y = nx * slab_count, ny * chan_count

    def segments(self, c):
        w0, w1 = self.w
        main = lambda first: lambda h, kind: kind * self.mk + h * self.wk + first
        return (
            (0, c * w0, w0, main(0)),
            (1, c * w1, w1, main(w0)),
            (1, self.c * w1 + c, 1, lambda h, kind: 2 * self.mk + kind * self.half + h),
        )

    def starts(self):
        kept = self.wb * self.s
        return [g * self.wb - (kept if 2 * g >= self.s else 0) for g in range(self.s)]

    def columns(self):
        b = np.concatenate([np.repeat(np.arange(st, st + self.wb + 1), self.na) for st in self.starts()])
        a = np.tile(np.arange(self.na), self.s * (self.wb + 1))
        return a, b

    def plane_table(self):
        a, b = self.columns()
        x = np.repeat(np.arange(self.nx), self.ny)[:, None]
        y = np.tile(np.arange(self.ny), self.nx)[:, None]
        total = self.full_x * self.full_y
        phase = (a * x * self.full_y + b * y * self.full_x) % total * (2.0 * np.pi / total)
        table = np.zeros((self.nx * self.ny, 2 * self.lp))
        scale = 1.0 / math.sqrt(total)
        table[:, : self.lw] = np.cos(phase) * scale
        table[:, self.lp : self.lp + self.lw] = -np.sin(phase) * scale
        high, low = (t.reshape(self.nx // self.xb, 1, self.blk, 2 * self.lp) for t in halves(table))
        return np.concatenate([high, high, low], 1).reshape(-1, 3 * self.blk, 2 * self.lp)

    def turns(self):
        a, b = self.columns()
        x = (np.arange(self.s) * self.nx)[:, None, None]
        y = (np.arange(self.ch) * self.ny)[None, :, None]
        total = self.full_x * self.full_y
        phase = (a * x * self.full_y + b * y * self.full_x) % total * (2.0 * np.pi / total)
        table = np.zeros((self.s, self.ch, 2, self.lp), np.float32)
        table[:, :, 0, : self.lw] = np.cos(phase)
        table[:, :, 1, : self.lw] = np.sin(phase)
        return table

    def depth_rows(self):
        main = np.arange(self.mk)
        edge = (np.arange(self.half) + 1) * self.wk
        z = np.arange(self.nz)
        scale = 1.0 / math.sqrt(self.nz)
        angle = lambda k: (k[:, None] * z) % self.nz * (2.0 * np.pi / self.nz)
        rows = [np.cos(angle(main)), np.sin(angle(main)), np.cos(angle(edge)), np.sin(angle(edge))]
        table = np.zeros((self.rc, self.nz))
        table[: 2 * self.mk + 2 * self.half] = np.concatenate(rows) * scale
        return halves(table)

    def depth_forward(self):
        high, low = self.depth_rows()
        return np.concatenate(
            [np.concatenate([high, high], 1), np.concatenate([low, np.zeros_like(low)], 1)], 0
        )

    def depth_inverse(self):
        high, low = self.depth_rows()
        table = np.zeros((round_up(3 * self.rc, 16), self.nz), ml_dtypes.bfloat16)
        table[: 3 * self.rc] = np.concatenate([high, high, low], 0)
        return table

    def selections(self):
        quarters = 128 // self.mx
        own = np.zeros((self.wb, 2, self.ll, 2, quarters, self.mx), np.float32)
        for b in range(self.wb):
            for r in range(2):
                for a in range(self.mx):
                    if a < self.mx // 2:
                        own[b, 0, r * self.span + b * self.na + a, r, :, a] = 1.0
                    else:
                        spot = r * self.span + (self.wb - b) * self.na + self.mx - a
                        own[b, 1, spot, r, :, a] = 1.0 - 2.0 * r
        own = own.reshape(self.wb, 2 * self.ll, 256)
        back = np.swapaxes(own, 1, 2)
        return own.astype(ml_dtypes.bfloat16), np.ascontiguousarray(back).astype(ml_dtypes.bfloat16)

    def orders(self, chunk):
        w0, w1 = self.w
        table = np.zeros((2, self.rows, self.rts[chunk]), np.float32)
        for c in range(self.c):
            for k in range(self.wk):
                for upper, index in enumerate((k, self.wk - k)):
                    if index < w0:
                        here, spot = 0, c * w0 + index
                    elif index < self.wk:
                        here, spot = 1, c * w1 + index - w0
                    else:
                        here, spot = 1, self.c * w1 + c
                    if here == chunk:
                        table[upper, c * self.wk + k, spot] = 1.0
        return table.astype(ml_dtypes.bfloat16)


def halves(table):
    high = table.astype(np.float32).astype(ml_dtypes.bfloat16)
    low = (table - high.astype(np.float64)).astype(np.float32).astype(ml_dtypes.bfloat16)
    return high, low


def dot(left, right, numbers=(((1,), (0,)), ((), ()))):
    return lax.dot_general(left, right, numbers, preferred_element_type=f32)


def split(value):
    high = value.astype(bf16)
    return high, (value - high.astype(f32)).astype(bf16)


def moved(value, chosen, left=False):
    first, second = split(value)
    if left:
        return dot(chosen, first) + dot(chosen, second)
    rows = value.shape[0]
    if rows % 16:
        return dot(first, chosen) + dot(second, chosen)
    both = dot(jnp.concatenate([first, second], axis=0), chosen)
    return both[:rows] + both[rows:]


def depth_analysis(plan, table_ref, values):
    rows = []
    for value in values:
        high, low = split(value)
        rows.append(jnp.concatenate([high, low], axis=1))
    both = dot(table_ref[...], jnp.concatenate(rows, axis=0), NT)
    lines = both[: plan.rc] + both[plan.rc :]
    return [lines[:, j * plan.blk : (j + 1) * plan.blk] for j in range(len(values))]


def depth_synthesis(plan, table_ref, rows):
    high = rows.astype(bf16).astype(f32)
    parts = [high, rows - high, high]
    extra = table_ref.shape[0] - 3 * plan.rc
    if extra:
        parts.append(jnp.zeros((extra, rows.shape[1]), f32))
    return dot(jnp.concatenate(parts, axis=0).astype(bf16), table_ref[...], TN)


def plane_analysis(plan, step, lines_ref, plane_ref, total_ref):
    high, low = split(lines_ref[...].reshape(plan.cc * plan.rc, plan.blk))
    rows = jnp.concatenate([high, low, high], axis=1)
    for start in range(0, 2 * plan.lp, 256):
        size = min(256, 2 * plan.lp - start)
        columns = pl.ds(start, size)
        part = dot(rows, plane_ref[0, :, columns]).reshape(plan.cc, plan.rc, size)

        @pl.when(step == 0)
        def _():
            total_ref[:, :, columns] = part

        @pl.when(step > 0)
        def _():
            total_ref[:, :, columns] += part


def plane_synthesis(plan, high_rows, low_rows, plane_ref, lines_ref):
    high_table, low_table = plane_ref[0, : plan.blk], plane_ref[0, 2 * plan.blk :]
    lines = (
        dot(high_rows[...], high_table, NT)
        + dot(low_rows[...], high_table, NT)
        + dot(high_rows[...], low_table, NT)
    )
    lines_ref[...] = lines.reshape(plan.cc, plan.rc, plan.blk)


def emit_modes(plan, flag_ref, turn_ref, total_ref, keep_refs, send_refs):
    lp, half = plan.lp, plan.half
    odd = flag_ref[0] == 1
    cosine, sine = turn_ref[0:1, :], turn_ref[1:2, :]
    for c in range(plan.c):
        real, imag = total_ref[c, :, :lp], total_ref[c, :, lp:]
        real, imag = real * cosine + imag * sine, imag * cosine - real * sine
        for m, base, size, place in plan.segments(c):
            made = []
            for g in range(plan.ch):
                h = g if g < half else plan.ch - 1 - g
                even, odd_rows = (slice(place(h, kind), place(h, kind) + size) for kind in (0, 1))
                if g < half:
                    made.append((real[even] + imag[odd_rows], imag[even] - real[odd_rows]))
                else:
                    made.append((real[even] - imag[odd_rows], imag[even] + real[odd_rows]))
            for pair in range(half):
                for r in range(2):
                    low, high = made[2 * pair][r], made[2 * pair + 1][r]
                    keep_refs[m][pair, r, base : base + size, :] = jnp.where(odd, high, low)
                    send_refs[m][pair, r, base : base + size, :] = jnp.where(odd, low, high)
    for m, used in enumerate((plan.c * plan.w[0], plan.c * (plan.w[1] + 1))):
        if used < plan.rts[m]:
            blank = jnp.zeros((half, 2, plan.rts[m] - used, lp), f32)
            keep_refs[m][:, :, used:, :] = blank
            send_refs[m][:, :, used:, :] = blank


def take_modes(plan, flag_ref, turn_ref, own_refs, other_refs, total_ref, high_rows, low_rows):
    lp, half = plan.lp, plan.half
    odd = flag_ref[0] == 1
    cosine, sine = turn_ref[0:1, :], turn_ref[1:2, :]

    def group(m, g, r, rows):
        own, other = own_refs[m][g // 2, r, rows, :], other_refs[m][g // 2, r, rows, :]
        return jnp.where(odd, own, other) if g % 2 else jnp.where(odd, other, own)

    for c in range(plan.c):
        for m, base, size, place in plan.segments(c):
            rows = slice(base, base + size)
            for h in range(half):
                plus = [group(m, h, r, rows) for r in range(2)]
                minus = [group(m, plan.ch - 1 - h, r, rows) for r in range(2)]
                real, imag = plus[0] + minus[0], plus[1] + minus[1]
                here = slice(place(h, 0), place(h, 0) + size)
                total_ref[c, here, :lp] = real * cosine - imag * sine
                total_ref[c, here, lp:] = imag * cosine + real * sine
                real, imag = plus[0] - minus[0], plus[1] - minus[1]
                here = slice(place(h, 1), place(h, 1) + size)
                total_ref[c, here, :lp] = -(imag * cosine + real * sine)
                total_ref[c, here, lp:] = real * cosine - imag * sine
        used = 2 * plan.mk + 2 * half
        if used < plan.rc:
            total_ref[c, used:, :] = jnp.zeros((plan.rc - used, 2 * lp), f32)
    high, low = split(total_ref[...].reshape(plan.c * plan.rc, 2 * lp))
    high_rows[...] = high
    low_rows[...] = low


def analyse_kernel(plan, flag_ref, values_ref, plane_ref, depth_ref, turn_ref, *refs):
    keep_refs, send_refs, (lines_ref, total_ref) = refs[:2], refs[2:4], refs[4:]
    step = pl.program_id(0)

    @pl.loop(0, plan.cc, step=plan.batch)
    def _(c):
        values = [values_ref[:, c + j].reshape(plan.blk, plan.nz) for j in range(plan.batch)]
        for j, lines in enumerate(depth_analysis(plan, depth_ref, values)):
            lines_ref[c + j] = lines

    plane_analysis(plan, step, lines_ref, plane_ref, total_ref)

    @pl.when(step == pl.num_programs(0) - 1)
    def _():
        emit_modes(plan, flag_ref, turn_ref, total_ref, keep_refs, send_refs)


def fields(plan, inverse_ref, lines_ref, first):
    lines = jnp.concatenate([lines_ref[first + j] for j in range(plan.batch)], axis=1)
    values = depth_synthesis(plan, inverse_ref, lines)
    return [values[j * plan.blk : (j + 1) * plan.blk] for j in range(plan.batch)]


def middle_kernel(plan, flag_ref, *refs):
    own_refs, other_refs, refs = refs[:2], refs[2:4], refs[4:]
    linear_ref, cotangent_ref, plane_ref, depth_ref, inverse_ref, turn_ref, output_ref, gradient_ref = refs[:8]
    keep_refs, send_refs, (lines_ref, back_ref, total_ref, high_rows, low_rows) = refs[8:10], refs[10:12], refs[12:]
    step = pl.program_id(0)

    @pl.when(step == 0)
    def _():
        take_modes(plan, flag_ref, turn_ref, own_refs, other_refs, total_ref, high_rows, low_rows)

    plane_synthesis(plan, high_rows, low_rows, plane_ref, lines_ref)
    shape = (plan.xb, plan.ny, plan.nz)

    @pl.loop(0, plan.cc, step=plan.batch)
    def _(first):
        gradients = []
        for j, field in enumerate(fields(plan, inverse_ref, lines_ref, first)):
            value = field + linear_ref[:, first + j].reshape(plan.blk, plan.nz)
            gate = 0.5 * (1.0 + lax.erf(value * root_half))
            slope = gate + value * jnp.exp(-0.5 * value * value) * inv_root_two_pi
            output_ref[:, first + j] = (value * gate).reshape(shape)
            gradients.append(cotangent_ref[:, first + j].reshape(plan.blk, plan.nz) * slope)
            gradient_ref[:, first + j] = gradients[-1].reshape(shape)
        for j, lines in enumerate(depth_analysis(plan, depth_ref, gradients)):
            back_ref[first + j] = lines

    plane_analysis(plan, step, back_ref, plane_ref, total_ref)

    @pl.when(step == pl.num_programs(0) - 1)
    def _():
        emit_modes(plan, flag_ref, turn_ref, total_ref, keep_refs, send_refs)


def synthesise_kernel(plan, flag_ref, *refs):
    own_refs, other_refs, refs = refs[:2], refs[2:4], refs[4:]
    linear_ref, plane_ref, inverse_ref, turn_ref, output_ref, lines_ref, total_ref, high_rows, low_rows = refs

    @pl.when(pl.program_id(0) == 0)
    def _():
        take_modes(plan, flag_ref, turn_ref, own_refs, other_refs, total_ref, high_rows, low_rows)

    plane_synthesis(plan, high_rows, low_rows, plane_ref, lines_ref)

    @pl.loop(0, plan.cc, step=plan.batch)
    def _(first):
        for j, field in enumerate(fields(plan, inverse_ref, lines_ref, first)):
            value = field + linear_ref[:, first + j].reshape(plan.blk, plan.nz)
            output_ref[:, first + j] = value.reshape(plan.xb, plan.ny, plan.nz)


def linear_kernel(plan, values_ref, weight_ref, bias_ref, output_ref):
    tiles = [(x, slice(t * 8, (t + 1) * 8)) for x in range(plan.lb) for t in range(plan.ny // 8)]
    values = [values_ref[x, :, t, :].reshape(plan.c * 8, plan.nz) for x, t in tiles]
    high, low = split(jnp.concatenate(values, axis=1))
    size = 8 * plan.c
    row, column = (lax.broadcasted_iota(jnp.int32, (size, plan.c), n) for n in (0, 1))
    repeat = (row // 8 == column).astype(f32)
    exact = partial(lax.dot_general, precision=lax.Precision.HIGHEST, preferred_element_type=f32)
    spread = exact(exact(repeat, weight_ref[...], (((1,), (0,)), ((), ()))), repeat, NT)
    row, column = (lax.broadcasted_iota(jnp.int32, (size, size), n) for n in (0, 1))
    high_matrix, low_matrix = split(jnp.where(row % 8 == column % 8, spread, 0.0))
    bias = exact(repeat, bias_ref[...], (((1,), (1,)), ((), ())))
    matrix = jnp.concatenate([high_matrix, high_matrix, low_matrix], axis=1)
    mixed = dot(matrix, jnp.concatenate([high, low, high], axis=0)) + bias
    for n, (x, t) in enumerate(tiles):
        output_ref[x, :, t, :] = mixed[:, n * plan.nz : (n + 1) * plan.nz].reshape(plan.c, 8, plan.nz)


def pick(plan, parts, chosen_ref, ordered_ref):
    @pl.when(pl.program_id(0) == 0)
    def _():
        for n in range(2):
            found = [moved(part[n][...], part[2][...], left=True) for part in parts]
            ordered_ref[:, n * plan.ll : (n + 1) * plan.ll] = sum(found[1:], found[0])

    return [moved(ordered_ref[...], chosen_ref[n]) for n in range(plan.bb)]


def give(plan, made_ref, order_ref, back_ref, own_ref, mirror_ref, sums_ref):
    part = moved(made_ref[0], back_ref[0])
    for n in range(1, plan.bb):
        part = part + moved(made_ref[n], back_ref[n])
    step = pl.program_id(0)

    @pl.when(step == 0)
    def _():
        sums_ref[...] = part

    @pl.when(step > 0)
    def _():
        sums_ref[...] += part

    @pl.when(step == pl.num_programs(0) - 1)
    def _():
        own_ref[...] = moved(sums_ref[:, : plan.ll], order_ref[...], left=True)
        mirror_ref[...] = moved(sums_ref[:, plan.ll :], order_ref[...], left=True)


def mix_kernel(
    plan, own_ref, mirror_ref, order_ref, disorder_ref, chosen_ref, back_ref, weight_ref,
    own_out, mirror_out, ordered_ref, made_ref, sums_ref,
):
    wk, quarters = plan.wk, 128 // plan.mx
    picked = pick(plan, [(own_ref, mirror_ref, order_ref)], chosen_ref, ordered_ref)
    place = lax.broadcasted_iota(jnp.int32, (wk, 128), 1) // plan.mx
    for n, modes in enumerate(picked):
        for t in range(plan.c // quarters):
            columns = slice(t * 128, (t + 1) * 128)
            real = imag = 0.0
            for i in range(plan.c):
                x_real, x_imag = modes[i * wk : (i + 1) * wk, :128], modes[i * wk : (i + 1) * wk, 128:]
                w_real, w_imag = weight_ref[n, 0, i, :, columns], weight_ref[n, 1, i, :, columns]
                real = real + (w_real * x_real - w_imag * x_imag)
                imag = imag + (w_real * x_imag + w_imag * x_real)
            for q in range(quarters):
                o = t * quarters + q
                made_ref[n, o * wk : (o + 1) * wk, :128] = jnp.where(place == q, real, 0.0)
                made_ref[n, o * wk : (o + 1) * wk, 128:] = jnp.where(place == q, imag, 0.0)
    give(plan, made_ref, disorder_ref, back_ref, own_out, mirror_out, sums_ref)


def along(plan, modes):
    wk, quarters = plan.wk, 128 // plan.mx
    place = lax.broadcasted_iota(jnp.int32, (wk, 128), 1) // plan.mx
    lined = []
    for t in range(plan.c // quarters):
        real = imag = 0.0
        for q in range(quarters):
            o = t * quarters + q
            real = jnp.where(place == q, modes[o * wk : (o + 1) * wk, :128], real)
            imag = jnp.where(place == q, modes[o * wk : (o + 1) * wk, 128:], imag)
        lined.append((slice(t * 128, (t + 1) * 128), real, imag))
    return lined


def mix_back_kernel(
    plan, own_ref, mirror_ref, order_ref, disorder_ref, chosen_ref, back_ref, weight_ref,
    own_out, mirror_out, ordered_ref, made_ref, sums_ref,
):
    wk = plan.wk
    for n, grads in enumerate(pick(plan, [(own_ref, mirror_ref, order_ref)], chosen_ref, ordered_ref)):
        lined = along(plan, grads)
        for i in range(plan.c):
            back_real = back_imag = 0.0
            for columns, real, imag in lined:
                w_real, w_imag = weight_ref[n, 0, i, :, columns], weight_ref[n, 1, i, :, columns]
                back_real = back_real + (w_real * real + w_imag * imag)
                back_imag = back_imag + (w_real * imag - w_imag * real)
            made_ref[n, i * wk : (i + 1) * wk, :128] = back_real
            made_ref[n, i * wk : (i + 1) * wk, 128:] = back_imag
    give(plan, made_ref, disorder_ref, back_ref, own_out, mirror_out, sums_ref)


def outer_kernel(plan, *refs):
    parts = [refs[:8][2 * m : 2 * m + 2] for m in range(4)]
    orders, chosen_ref, gradient_ref, mode_rows, grad_rows = refs[8:10], refs[10], refs[11], refs[12], refs[13]
    wk = plan.wk
    modes = pick(plan, [(*parts[m], orders[m]) for m in range(2)], chosen_ref, mode_rows)
    grads = pick(plan, [(*parts[2 + m], orders[m]) for m in range(2)], chosen_ref, grad_rows)
    for n in range(plan.bb):
        lined = along(plan, grads[n])
        for i in range(plan.c):
            rows = slice(i * wk, (i + 1) * wk)
            x_real, x_imag = modes[n][rows, :128], modes[n][rows, 128:]
            for columns, real, imag in lined:
                gradient_ref[n, 0, i, :, columns] = real * x_real + imag * x_imag
                gradient_ref[n, 1, i, :, columns] = imag * x_real - real * x_imag


def halve_kernel(flag_ref, keep_ref, arrived_ref, kept_ref, send_ref):
    odd = flag_ref[0] == 1
    for pair in range(kept_ref.shape[0]):
        low = keep_ref[2 * pair] + arrived_ref[2 * pair]
        high = keep_ref[2 * pair + 1] + arrived_ref[2 * pair + 1]
        kept_ref[pair] = jnp.where(odd, high, low)
        send_ref[pair] = jnp.where(odd, low, high)


def cut_kernel(plan, slab_ref, keep_ref, arrived_ref, *refs):
    out_refs, held_ref = refs[:-1], refs[-1]
    lane = lax.broadcasted_iota(jnp.int32, held_ref.shape[1:], 1)
    real = keep_ref[0, 0] + arrived_ref[0, 0]
    imag = keep_ref[0, 1] + arrived_ref[0, 1]
    for g in range(plan.s):
        first = pltpu.roll(real, (plan.lp - g * plan.span) % plan.lp, 1)[:, : plan.ll]
        second = pltpu.roll(imag, (plan.lp - g * plan.span + plan.span) % plan.lp, 1)[:, : plan.ll]
        held_ref[g] = jnp.where(lane < plan.span, first, jnp.where(lane < 2 * plan.span, second, 0.0))
    for j, out_ref in enumerate(out_refs):
        out_ref[...] = held_ref[slab_ref[0] ^ j]


def join_kernel(plan, slab_ref, *refs):
    piece_refs, total_ref, held_ref = refs[:-2], refs[-2], refs[-1]
    for j, piece_ref in enumerate(piece_refs):
        held_ref[j] = piece_ref[...]
    rows = held_ref.shape[1]
    lane = lax.broadcasted_iota(jnp.int32, (rows, plan.lp), 1)
    real = imag = jnp.zeros((rows, plan.lp), f32)
    blank = jnp.zeros((rows, plan.lp - plan.ll), f32)
    for g in range(plan.s):
        piece = jnp.concatenate([held_ref[slab_ref[0] ^ g], blank], axis=1)
        here = (lane >= g * plan.span) & (lane < (g + 1) * plan.span)
        real = jnp.where(here, pltpu.roll(piece, g * plan.span, 1), real)
        imag = jnp.where(here, pltpu.roll(piece, (g * plan.span - plan.span) % plan.lp, 1), imag)
    total_ref[0, 0] = real
    total_ref[0, 1] = imag


def whole(array):
    zeros = (0,) * array.ndim
    return pl.BlockSpec(array.shape, lambda i: zeros, pipeline_mode=pl.Buffered(1))


def whole_shape(shape):
    zeros = (0,) * len(shape)
    return pl.BlockSpec(shape, lambda i: zeros, pipeline_mode=pl.Buffered(1))


def leading(shape):
    rest = (0,) * (len(shape) - 1)
    return pl.BlockSpec(shape, lambda i: (i,) + rest)


def shaped(*shape):
    return jax.ShapeDtypeStruct(shape, f32)


def anywhere():
    return pl.BlockSpec(memory_space=pl.ANY)


def scalar():
    return pl.BlockSpec(memory_space=pltpu.SMEM)


def call(kernel, name, grid, in_specs, out_specs, out_shape, scratch, cost, before=(), aliases=None):
    skipped = len(before)
    run = pl.pallas_call(
        lambda *refs: kernel(*refs[skipped:]),
        grid=(grid,),
        in_specs=[anywhere()] * skipped + list(in_specs),
        out_specs=out_specs,
        out_shape=out_shape,
        scratch_shapes=scratch,
        name=name,
        input_output_aliases=aliases or {},
        compiler_params=pltpu.CompilerParams(vmem_limit_bytes=VMEM_LIMIT, dimension_semantics=("arbitrary",)),
        cost_estimate=pl.CostEstimate(flops=int(cost * 1.15e9), bytes_accessed=int(cost * 3.6e6), transcendentals=0),
    )
    return partial(run, *before)


def tie(value, *before):
    if not before:
        return value
    return pl.pallas_call(
        lambda *refs: None,
        in_specs=[anywhere()] * (1 + len(before)),
        out_specs=anywhere(),
        out_shape=jax.ShapeDtypeStruct(value.shape, value.dtype),
        input_output_aliases={0: 0},
        name="tie",
    )(value, *before)


class Program:
    def __init__(self, plan):
        self.plan = plan
        self.plane = jnp.asarray(plan.plane_table())
        self.depth = jnp.asarray(plan.depth_forward())
        self.inverse = jnp.asarray(plan.depth_inverse())
        slab, chan = lax.axis_index("slab"), lax.axis_index("chan")
        self.slab, self.chan = slab, chan
        turns = jnp.asarray(plan.turns())
        self.turn = lax.dynamic_index_in_dim(
            lax.dynamic_index_in_dim(turns, slab, 0, False), chan, 0, False
        )
        self.slab_index = slab.astype(jnp.int32).reshape(1)
        self.flag = (chan % 2).astype(jnp.int32).reshape(1)
        upper = (chan >= plan.half).astype(jnp.int32)
        tables = [plan.orders(m) for m in range(plan.chunks)]
        self.order = [lax.dynamic_index_in_dim(jnp.asarray(t), upper, 0, False) for t in tables]
        tables = [np.ascontiguousarray(np.swapaxes(t, 1, 2)) for t in tables]
        self.disorder = [lax.dynamic_index_in_dim(jnp.asarray(t), upper, 0, False) for t in tables]
        chosen, back = plan.selections()
        self.chosen, self.back = jnp.asarray(chosen), jnp.asarray(back)

    def half_shapes(self):
        plan = self.plan
        return [(plan.half, 2, rt, plan.lp) for rt in plan.rts]

    def field_spec(self):
        plan = self.plan
        return leading((plan.xb, plan.c, plan.ny, plan.nz))

    def table(self):
        plan = self.plan
        return leading((1, 3 * plan.blk, 2 * plan.lp))

    def lines(self):
        plan = self.plan
        return pltpu.VMEM((plan.cc, plan.rc, plan.blk), f32)

    def spectra(self):
        plan = self.plan
        rows = pltpu.VMEM((plan.cc * plan.rc, 2 * plan.lp), bf16)
        return [pltpu.VMEM((plan.cc, plan.rc, 2 * plan.lp), f32), rows, rows]

    def analyse(self, values):
        plan = self.plan
        halves = self.half_shapes()
        made = call(
            partial(analyse_kernel, plan), "analyse", plan.nx // plan.xb,
            [scalar(), self.field_spec(), self.table(), whole(self.depth), whole(self.turn)],
            [whole_shape(h) for h in halves * 2], [shaped(*h) for h in halves * 2],
            [self.lines(), self.spectra()[0]], 26,
        )(self.flag, values, self.plane, self.depth, self.turn)
        return made[:2], made[2:]

    def middle(self, owns, others, linear, cotangent):
        plan = self.plan
        halves = self.half_shapes()
        field, spec = shaped(plan.nx, plan.c, plan.ny, plan.nz), self.field_spec()
        modes = [whole_shape(h) for h in halves * 2]
        output, gradient, *made = call(
            partial(middle_kernel, plan), "middle", plan.nx // plan.xb,
            [scalar(), *modes, spec, spec, self.table(), whole(self.depth), whole(self.inverse), whole(self.turn)],
            [spec, spec, *modes], [field, field, *[shaped(*h) for h in halves * 2]],
            [self.lines(), self.lines(), *self.spectra()], 47,
        )(self.flag, *owns, *others, linear, cotangent, self.plane, self.depth, self.inverse, self.turn)
        return output, gradient, made[:2], made[2:]

    def synthesise(self, before, owns, others, linear):
        plan = self.plan
        spec = self.field_spec()
        return call(
            partial(synthesise_kernel, plan), "synthesise", plan.nx // plan.xb,
            [scalar(), *[whole_shape(h) for h in self.half_shapes() * 2], spec, self.table(),
             whole(self.inverse), whole(self.turn)],
            spec, shaped(plan.nx, plan.c, plan.ny, plan.nz),
            [self.lines(), *self.spectra()], 20, before,
        )(self.flag, *owns, *others, linear, self.plane, self.inverse, self.turn)

    def linear(self, before, values, matrix, bias):
        plan = self.plan
        bias = bias[None]
        spec = leading((plan.lb, plan.c, plan.ny, plan.nz))
        return call(
            partial(linear_kernel, plan), "linear", plan.nx // plan.lb,
            [spec, whole(matrix), whole(bias)],
            spec, shaped(plan.nx, plan.c, plan.ny, plan.nz), [],
            12, before,
        )(values, matrix, bias)

    def mix(self, kernel, name, chunk, before, own, mirror, weights):
        plan = self.plan
        modes = (plan.rts[chunk], plan.ll)
        order, disorder = self.order[chunk], self.disorder[chunk]
        ordered = pltpu.VMEM((plan.rows, 2 * plan.ll), f32)
        return call(
            partial(kernel, plan), name, plan.wb // plan.bb,
            [
                whole_shape(modes), whole_shape(modes), whole(order), whole(disorder),
                leading((plan.bb,) + self.chosen.shape[1:]), leading((plan.bb,) + self.back.shape[1:]),
                leading((plan.bb, *weights.shape[1:])),
            ],
            [whole_shape(modes)] * 2, [shaped(*modes)] * 2,
            [ordered, pltpu.VMEM((plan.bb, plan.rows, 256), f32), ordered], 9, before,
        )(own, mirror, order, disorder, self.chosen, self.back, weights)

    def outer(self, before, modes, grads, weights):
        plan = self.plan
        parts = [part for pair in (*modes, *grads) for part in pair]
        ordered = pltpu.VMEM((plan.rows, 2 * plan.ll), f32)
        out = leading((plan.bb, *weights.shape[1:]))
        return call(
            partial(outer_kernel, plan), "outer", plan.wb // plan.bb,
            [*[whole(p) for p in parts], *[whole(o) for o in self.order], leading((plan.bb,) + self.chosen.shape[1:])],
            out, shaped(*weights.shape), [ordered, ordered], 9, before,
        )(*parts, *self.order, self.chosen)

    def across(self, value, axis, bit):
        size = lax.axis_size(axis)
        return lax.ppermute(value, axis, [(i, i ^ bit) for i in range(size)])

    def mirrored(self, value):
        total = self.plan.s * self.plan.ch
        return lax.ppermute(value, ("slab", "chan"), [(i, total - 1 - i) for i in range(total)])

    def halve(self, keep, arrived, bit):
        mine = ((self.chan // bit) % 2).astype(jnp.int32).reshape(1)
        half = (keep.shape[0] // 2,) + keep.shape[1:]
        return call(
            halve_kernel, "halve", 1, [scalar(), whole(keep), whole(keep)], [whole_shape(half)] * 2,
            [shaped(*half)] * 2, [], 2,
        )(mine, keep, arrived)

    def sums_over_chan(self, keep, arrived, before):
        bit, sent = 2, arrived
        while bit < self.plan.ch:
            keep, sent = self.halve(keep, arrived, bit)
            arrived = self.across(tie(sent, *before) if bit == 2 else sent, "chan", bit)
            bit *= 2
        return keep, sent, arrived

    def cut(self, keep, arrived):
        plan = self.plan
        size = (keep.shape[2], plan.ll)
        mine, *pieces = call(
            partial(cut_kernel, plan), "cut", 1, [scalar(), whole(keep), whole(keep)],
            [whole_shape(size)] * plan.s, [shaped(*size)] * plan.s, [pltpu.VMEM((plan.s, *size), f32)], 2,
        )(self.slab_index, keep, arrived)
        return mine, pieces

    def join(self, mine, arrived):
        plan = self.plan
        total = (1, 2, mine.shape[0], plan.lp)
        return call(
            partial(join_kernel, plan), "join", 1, [scalar()] + [whole(mine)] * plan.s,
            whole_shape(total), shaped(*total), [pltpu.VMEM((plan.s, *mine.shape), f32)], 2,
        )(self.slab_index, mine, *arrived)

    def exchange(self, keeps, sends, linear, mix, outer=None):
        plan = self.plan
        first = [self.across(send, "chan", 1) for send in sends]
        keep0, sent0, came0 = self.sums_over_chan(keeps[0], first[0], [])
        extra = linear([sent0, first[1]])
        came0 = tie(came0, extra)
        keep1, sent1, came1 = self.sums_over_chan(keeps[1], first[1], [came0])

        mine, pieces = self.cut(keep0, came0)
        for j, piece in enumerate(pieces):
            mine = mine + self.across(piece, "slab", j + 1)
        own0 = mine
        mirror0 = self.mirrored(own0)
        mine, pieces = self.cut(keep1, tie(came1, own0))
        arrived = [self.across(piece, "slab", j + 1) for j, piece in enumerate(pieces)]
        out0, back0 = mix(0, [mine], own0, mirror0)
        for piece in [tie(arrived[0], out0)] + arrived[1:]:
            mine = mine + piece
        own1 = mine
        mirror1 = self.mirrored(own1)

        full0 = out0 + self.mirrored(back0)
        arrived = [self.across(full0, "slab", j) for j in range(1, plan.s)]
        out1, back1 = mix(1, [full0], own1, mirror1)
        full1 = out1 + self.mirrored(back1)
        total0 = self.join(full0, [tie(arrived[0], back1)] + arrived[1:])
        came0 = self.across(total0, "chan", plan.ch // 2)
        full1 = tie(full1, total0)
        arrived = [self.across(full1, "slab", j) for j in range(1, plan.s)]
        made = None
        if outer is not None:
            made = outer([total0], ((own0, mirror0), (own1, mirror1)))
            came0 = tie(came0, made)
        total1 = tie(self.join(full1, arrived), came0)
        came1 = self.across(total1, "chan", plan.ch // 2)
        if outer is not None:
            made = tie(jnp.transpose(made, (0, 3, 2, 1, 4)), total1)
            came1 = tie(came1, made)

        owns, others = [], []
        for total, other in ((total0, came0), (total1, came1)):
            bit = plan.ch // 2
            while bit > 1:
                upper = (self.chan // bit) % 2 == 1
                total = jnp.stack([jnp.where(upper, other, total), jnp.where(upper, total, other)], axis=1)
                total = total.reshape((-1,) + total.shape[2:])
                bit //= 2
                other = self.across(total, "chan", bit)
            owns.append(total)
            others.append(other)
        return owns, others, extra, made, ((own0, mirror0), (own1, mirror1))


def local(inputs, cotangent, spectral, local_weight, bias_vector):
    nx, ny, channels, nz = inputs.shape
    wb, wk = spectral.shape[0], spectral.shape[1]
    plan = Plan(nx, ny, nz, channels, wb, wk, spectral.shape[4] // channels, lax.axis_size("slab"), lax.axis_size("chan"))
    program = Program(plan)
    values = jnp.transpose(inputs, (0, 2, 1, 3))
    slopes = jnp.transpose(cotangent, (0, 2, 1, 3))
    weights = jnp.transpose(spectral, (0, 2, 3, 1, 4))

    keeps, sends = program.analyse(values)
    owns, others, linear, _, modes = program.exchange(
        keeps, sends,
        lambda before: program.linear(before, values, local_weight.T, bias_vector),
        lambda m, before, own, mirror: program.mix(mix_kernel, "mix", m, before, own, mirror, weights),
    )
    output, gradient, keeps, sends = program.middle(owns, others, linear, slopes)
    owns, others, linear, grad_spectral, _ = program.exchange(
        keeps, sends,
        lambda before: program.linear(before, gradient, local_weight, jnp.zeros_like(bias_vector)),
        lambda m, before, own, mirror: program.mix(mix_back_kernel, "mix_back", m, before, own, mirror, weights),
        lambda before, grads: program.outer(before, modes, grads, weights),
    )
    grad_inputs = program.synthesise([], owns, others, linear)
    return (
        jnp.transpose(output, (0, 2, 1, 3)),
        jnp.transpose(grad_inputs, (0, 2, 1, 3)),
        jnp.transpose(grad_spectral, (0, 1, 3, 2, 4)),
    )


def solution(mesh):
    in_specs = (
        P(("groups", "slab"), "chan", None, None),
        P(("groups", "slab"), "chan", None, None),
        P("slab", "chan", None, None, None),
        P(),
        P(),
    )
    out_specs = (
        P(("groups", "slab"), "chan", None, None),
        P(("groups", "slab"), "chan", None, None),
        P(("groups", "slab"), "chan", None, None, None),
    )
    return jax.shard_map(local, mesh=mesh, in_specs=in_specs, out_specs=out_specs, check_vma=False)
```

time: 407 us -> 402 us (0.988)
  waiting for transfers between devices: 98.3 us -> 66.6 us
  Pallas kernels: 184 us -> 203 us
  other arithmetic: 12.9 us -> 6.91 us
  starting transfers between devices: 66.6 us -> 72.3 us
  local copies, waits for them, and re-layouts: 42.3 us -> 47.7 us
    ppermute x40, waiting for transfers between devices: 80.9 us -> 53.6 us  [across(): return lax.ppermute(value, axis, [(i, i ^ bit) for i in range(size)])]
    pallas_call x14 -> x17, Pallas kernels: 48.5 us -> 69.9 us  [the longest x4 33.7 us: mix(): call(partial(kernel, plan), name, plan.wb // plan.bb, [whole_shape(modes)...]
    pallas_call x2, Pallas kernels: 28.3 us -> 39.5 us  [linear(): call(partial(linear_kernel, plan), 'linear', plan.nx // plan.lb, [spec, w...]
    pallas_call x2 -> x1, Pallas kernels: 32 us -> 27.1 us  [analyse(): call(partial(analyse_kernel, plan), 'analyse', plan.nx // plan.xb, [scala...]
    pallas_call x2 -> x1, Pallas kernels: 51.7 us -> 47.1 us  [middle(): call(partial(middle_kernel, plan), 'middle', plan.nx // plan.xb, [scalar(...]
    unnamed x102 -> x124, local copies, waits for them, and re-layouts: 28.2 us -> 32.6 us
    ppermute x8, waiting for transfers between devices: 17.5 us -> 13 us  [mirrored(): lax.ppermute(value, ('slab', 'chan'), [(i, total - 1 - i) for i in range(...]
    ppermute x40, starting transfers between devices: 53.6 us -> 57.8 us  [across(): return lax.ppermute(value, axis, [(i, i ^ bit) for i in range(size)])]
  transfers between devices with their start and end apart: 48 -> 48, of which waited for: 20 -> 16; matrix products, arithmetic and copies ran while one was open for 7% -> 6% of each run, Pallas kernels for 31% -> 27%
where the time goes in v1:
time: 402 us; the launch traced here: 398 us
  Pallas kernels  203 us (50%)
  starting transfers between devices  72.3 us (18%)
  waiting for transfers between devices  66.6 us (17%)
  local copies, waits for them, and re-layouts  47.7 us (12%)
  other arithmetic  6.91 us (2%)
    ppermute x40, starting transfers between devices, across(): return lax.ppermute(value, axis, [(i, i ^ bit) for i in range(size)])  57.8 us
    ppermute x40, waiting for transfers between devices, across(): return lax.ppermute(value, axis, [(i, i ^ bit) for i in range(size)])  53.6 us
    pallas_call x1, Pallas kernels, middle(): call(partial(middle_kernel, plan), 'middle', plan.nx // plan.xb, [scalar(...  47.1 us
    pallas_call x2, Pallas kernels, linear(): call(partial(linear_kernel, plan), 'linear', plan.nx // plan.lb, [spec, w...  39.5 us
    pallas_call x4, Pallas kernels, mix(): call(partial(kernel, plan), name, plan.wb // plan.bb, [whole_shape(modes)...  33.7 us
    unnamed x124, local copies, waits for them, and re-layouts  32.6 us
    pallas_call x1, Pallas kernels, analyse(): call(partial(analyse_kernel, plan), 'analyse', plan.nx // plan.xb, [scala...  27.1 us
    pallas_call x1, Pallas kernels, synthesise(): call(partial(synthesise_kernel, plan), 'synthesise', plan.nx // plan.xb,...  19.8 us
  transfers between devices with their start and end apart: 48, of which 16 were waited for; matrix products, arithmetic and copies ran while one was open for 6% of the time, Pallas kernels for 27%

profile of v1, /device:TPU:0, one launch (start us, length us, event | category | flops | bytes accessed | tf_op | source)
XLA Modules:
  0.0 398.1 jit_solution(14597696163372810067)
XLA Ops:
  1.9 27.1 %analyse.1 = (f32[2,2,80,640]{3,2,1,0:T(8,128)}, f32[2,2,104,640]{3,2,1,0:T(8,128)}, f32[2,2,80,640]{3,2,1,0:T(8,128)}, f32[2,2,104,640]{3,2,1,0:T(8,128)}) custom-call(s32[1]{0:T(128)} %bitcast.refs_0_, f32[32,20,32,128]{3,2,1,0:T(8,128)} %bitcast.57, bf16[4,768,1280]{2,1,0:T(8,128)(2,1)} %constant.132.clone.refs_2_.refs_7_.refs_6_, ...), custom_call_target="tpu_custom_call" | custom-call | flops 29899999232 | bytes 93600000 | tf_op jit(solution)/shard_map/analyse/pallas_call | solution.py:613
  40.3 14.1 %linear.2.refs_1_.refs_5_ = f32[32,20,32,128]{3,2,1,0:T(8,128)} custom-call(f32[1,2,80,640]{3,2,1,0:T(8,128)} %get-tuple-element.51.refs_0_, f32[2,2,104,640]{3,2,1,0:T(8,128)} %copy-done.38, f32[32,20,32,128]{3,2,1,0:T(8,128)} %bitcast.58, f32[20,20]{1,0:T(8,128)} %bitcast.56, f32[1,20]{1,0:T(1,128)} %bitcast.60), custom_call_target="tpu_custom_call" | custom-call | flops 13799999488 | bytes 43200000 | tf_op jit(solution)/shard_map/linear/pallas_call | solution.py:649
  65.4 6.8 %copy.41 = f32[8,8,2,20,640]{4,1,3,2,0:T(8,128)} copy(f32[8,8,2,20,640]{4,2,3,1,0:T(2,128)} %param.17) | data formatting | bytes 13107200 | tf_op args[2]
  84.3 8.4 %mix.2 = (f32[80,384]{1,0:T(8,128)}, f32[80,384]{1,0:T(8,128)}) custom-call(f32[104,384]{1,0:T(8,128)} %get-tuple-element.57.refs_0_, f32[80,384]{1,0:T(8,128)} %copy-done.18, f32[80,384]{1,0:T(8,128)} %copy-done.54, bf16[160,80]{1,0:T(8,128)(2,1)} %dynamic-slice_bitcast_fusion.3.refs_3_.refs_9_, bf16[80,160]{1,0:T(8,128)(2,1)} %dynamic-slice_bitcast_fusion.2.refs_4_, ...), custom_call_target="tpu_custom_call" | custom-call | flops 10350000128 | bytes 32400000 | tf_op jit(solution)/shard_map/mix/pallas_call | solution.py:661
  100.3 8.4 %collective-permute-start.9 = (f32[80,384]{1,0:T(8,128)S(1)}, f32[80,384]{1,0:T(8,128)S(1)}, u32[]{:S(2)}, u32[]{:S(2)}) collective-permute-start(f32[80,384]{1,0:T(8,128)S(1)} %add.93.refs_0_.refs_1_), channel_id=1, source_target_pairs={{0,4},{4,0},{8,12},{12,8},{1,5},{5,1},{9,13},{13,9},{2,6},{6,2},{1... | collective-permute-start | bytes 368648 | tf_op jit(solution)/shard_map/ppermute | solution.py:685
  111.8 8.7 %mix.3 = (f32[104,384]{1,0:T(8,128)}, f32[104,384]{1,0:T(8,128)}) custom-call(f32[80,384]{1,0:T(8,128)} %copy-done.30, f32[104,384]{1,0:T(8,128)} %copy-done.22, f32[104,384]{1,0:T(8,128)} %copy-done.46, bf16[160,104]{1,0:T(8,128)(2,1)} %dynamic-slice_bitcast_fusion.1.refs_3_.refs_10_, bf16[104,160]{1,0:T(8,128)(2,1)} %dynamic-slice_bitcast_fusion.refs_4_, ...), custom_call_target="tpu_custom_call" | custom-call | flops 10350000128 | bytes 32400000 | tf_op jit(solution)/shard_map/mix/pallas_call | solution.py:661
  135.6 3.8 collective-permute-done.18.refs_2_
  139.3 8.8 %collective-permute-done.19.refs_3_ = f32[104,384]{1,0:T(8,128)S(1)} collective-permute-done((f32[104,384]{1,0:T(8,128)}, f32[104,384]{1,0:T(8,128)S(1)}, u32[]{:S(2)}, u32[]{:S(2)}) %collective-permute-start.19) | collective-permute-done | bytes 159776 | tf_op jit(solution)/shard_map/ppermute | solution.py:685
  152.7 11.8 %collective-permute-done.21 = f32[1,2,104,640]{3,2,1,0:T(8,128)S(1)} collective-permute-done((f32[1,2,104,640]{3,2,1,0:T(8,128)}, f32[1,2,104,640]{3,2,1,0:T(8,128)S(1)}, u32[]{:S(2)}, u32[]{:S(2)}) %collective-permute-start.21) | collective-permute-done | bytes 532512 | tf_op jit(solution)/shard_map/ppermute | solution.py:685
  170.9 47.1 %middle.1 = (f32[32,20,32,128]{3,2,1,0:T(8,128)}, f32[32,20,32,128]{3,2,1,0:T(8,128)}, f32[2,2,80,640]{3,2,1,0:T(8,128)}, f32[2,2,104,640]{3,2,1,0:T(8,128)}, f3...) custom-call(s32[1]{0:T(128)} %bitcast.refs_0_, f32[2,2,80,640]{3,2,1,0:T(8,128)} %copy-done.12, ...), custom_call_target="tpu_custom_call" | custom-call | flops 54050000896 | bytes 169200000 | tf_op jit(solution)/shard_map/middle/pallas_call | solution.py:626
  218.6 3.6 collective-permute-done.25.refs_2_
  226.7 25.4 %linear.3.refs_1_.refs_5_ = f32[32,20,32,128]{3,2,1,0:T(8,128)} custom-call(f32[1,2,80,640]{3,2,1,0:T(8,128)} %get-tuple-element.72.refs_0_, f32[2,2,104,640]{3,2,1,0:T(8,128)} %copy-done.39, f32[32,20,32,128]{3,2,1,0:T(8,128)} %get-tuple-element.73.refs_2_, f32[20,20]{1,0:T(8,128)} %refs_3_.2, f32[1,20]{1,0:T(1,128)} %broadcast_1_refs_4_.2.refs_4_), custom_call_target="tpu_custom_call" | custom-call | flops 13799999488 | bytes 43200000 | tf_op jit(solution)/shard_map/linear/pallas_call | solution.py:649
  259.5 3.3 collective-permute-start.28
  266.9 7.6 %collective-permute-done.29 = f32[80,384]{1,0:T(8,128)S(1)} collective-permute-done((f32[80,384]{1,0:T(8,128)}, f32[80,384]{1,0:T(8,128)S(1)}, u32[]{:S(2)}, u32[]{:S(2)}) %collective-permute-start.29) | collective-permute-done | bytes 122912 | tf_op jit(solution)/shard_map/ppermute | solution.py:685
  284.6 8.3 %mix_back.2 = (f32[80,384]{1,0:T(8,128)}, f32[80,384]{1,0:T(8,128)}) custom-call(f32[104,384]{1,0:T(8,128)} %get-tuple-element.79.refs_0_, f32[80,384]{1,0:T(8,128)} %copy-done.19, f32[80,384]{1,0:T(8,128)} %copy-done.55, bf16[160,80]{1,0:T(8,128)(2,1)} %dynamic-slice_bitcast_fusion.3.refs_3_.refs_9_, bf16[80,160]{1,0:T(8,128)(2,1)} %dynamic-slice_bitcast_fusion.2.refs_4_, ...), custom_call_target="tpu_custom_call" | custom-call | flops 10350000128 | bytes 32400000 | tf_op jit(solution)/shard_map/mix_back/pallas_call | solution.py:661
  293.6 3.0 collective-permute-done.35
  302.0 7.2 %collective-permute-done.32 = f32[80,384]{1,0:T(8,128)S(1)} collective-permute-done((f32[80,384]{1,0:T(8,128)S(1)}, f32[80,384]{1,0:T(8,128)S(1)}, u32[]{:S(2)}, u32[]{:S(2)}) %collective-permute-start.32) | collective-permute-done | bytes 122912 | tf_op jit(solution)/shard_map/ppermute | solution.py:689
  309.3 6.6 %collective-permute-start.33 = (f32[80,384]{1,0:T(8,128)S(1)}, f32[80,384]{1,0:T(8,128)S(1)}, u32[]{:S(2)}, u32[]{:S(2)}) collective-permute-start(f32[80,384]{1,0:T(8,128)S(1)} %add.101.refs_0_.refs_1_), channel_id=1, source_target_pairs={{0,4},{4,0},{8,12},{12,8},{1,5},{5,1},{9,13},{13,9},{2,6},{6,2},{1... | collective-permute-start | bytes 368648 | tf_op jit(solution)/shard_map/ppermute | solution.py:685
  319.0 8.3 %mix_back.3 = (f32[104,384]{1,0:T(8,128)}, f32[104,384]{1,0:T(8,128)}) custom-call(f32[80,384]{1,0:T(8,128)} %copy-done.29, f32[104,384]{1,0:T(8,128)} %copy-done.23, f32[104,384]{1,0:T(8,128)} %copy-done.47, bf16[160,104]{1,0:T(8,128)(2,1)} %dynamic-slice_bitcast_fusion.1.refs_3_.refs_10_, bf16[104,160]{1,0:T(8,128)(2,1)} %dynamic-slice_bitcast_fusion.refs_4_, ...), custom_call_target="tpu_custom_call" | custom-call | flops 10350000128 | bytes 32400000 | tf_op jit(solution)/shard_map/mix_back/pallas_call | solution.py:661
  333.4 3.1 collective-permute-done.41
  341.9 8.2 %outer.1.refs_1_ = f32[8,2,20,8,640]{4,3,2,1,0:T(8,128)} custom-call(f32[1,2,80,640]{3,2,1,0:T(8,128)} %join.6.refs_0_.refs_1_, f32[80,384]{1,0:T(8,128)} %copy-done.18, f32[80,384]{1,0:T(8,128)} %copy-done.54, f32[104,384]{1,0:T(8,128)} %copy-done.22, f32[104,384]{1,0:T(8,128)} %copy-done.46, f32[80,384]{1,0:T(8,128)} %copy-done.19, f32[80,384]{1,0:T(8,128)} %copy-done.55, ...), custom_call_target="tpu_custom_call" | custom-call | flops 10350000128 | bytes 32400000 | tf_op jit(solution)/shard_map/outer/pallas_call | solution.py:677
  350.2 3.9 collective-permute-done.43.refs_3_
  359.4 10.7 %copy.40 = f32[8,2,20,8,640]{4,1,2,3,0:T(2,128)} copy(f32[8,2,20,8,640]{4,3,2,1,0:T(8,128)} %outer.1.refs_1_) | data formatting | bytes 13107200 | tf_op jit(solution)/shard_map/outer/pallas_call | solution.py:677
  378.2 19.8 %synthesise.1 = f32[32,20,32,128]{3,2,1,0:T(8,128)} custom-call(s32[1]{0:T(128)} %bitcast.refs_0_, f32[2,2,80,640]{3,2,1,0:T(8,128)} %copy-done.13, f32[2,2,104,640]{3,2,1,0:T(8,128)} %copy-done.11, f32[2,2,80,640]{3,2,1,0:T(8,128)} %copy-done.44, f32[2,2,104,640]{3,2,1,0:T(8,128)} %copy-done.41, f32[32,20,32,128]{3,2,1,0:T(8,128)} %linear.3.refs_1_.refs_5_, ...), custom_call_target="tpu_custom_call" | custom-call | flops 23000000512 | bytes 72000000 | tf_op jit(solution)/shard_map/synthesise/pallas_call | solution.py:637
  (258 shorter events, 132.9 us)
Async XLA Ops:
  36.5 20.7 %collective-permute-start.2 = (f32[1,2,80,640]{3,2,1,0:T(8,128)}, f32[1,2,80,640]{3,2,1,0:T(8,128)S(1)}, u32[]{:S(2)}, u32[]{:S(2)}) collective-permute-start(f32[1,2,80,640]{3,2,1,0:T(8,128)} %get-tuple-element.51.refs_0_), channel_id=1, source_target_pairs={{0,2},{1,3},{2,0},{3,1},{4,6},{5,7},{6,4},{7,5},{8,10},{9,11},{10,... | collective-permute-start | bytes 1228808 | tf_op jit(solution)/shard_map/ppermute | solution.py:685
  57.9 18.2 %collective-permute-start.3 = (f32[1,2,104,640]{3,2,1,0:T(8,128)}, f32[1,2,104,640]{3,2,1,0:T(8,128)S(1)}, u32[]{:S(2)}, u32[]{:S(2)}) collective-permute-start(f32[1,2,104,640]{3,2,1,0:T(8,128)} %tie.18), channel_id=1, source_target_pairs={{0,2},{1,3},{2,0},{3,1},{4,6},{5,7},{6,4},{7,5},{8,10},{9,11},{10,... | collective-permute-start | bytes 1597448 | tf_op jit(solution)/shard_map/ppermute | solution.py:685
  79.3 15.6 %collective-permute-start.10 = (f32[104,384]{1,0:T(8,128)}, f32[104,384]{1,0:T(8,128)S(1)}, u32[]{:S(2)}, u32[]{:S(2)}) collective-permute-start(f32[104,384]{1,0:T(8,128)} %get-tuple-element.60), channel_id=1, source_target_pairs={{0,4},{4,0},{8,12},{12,8},{1,5},{5,1},{9,13},{13,9},{2,6},{6,2},{1... | collective-permute-start | bytes 479240 | tf_op jit(solution)/shard_map/ppermute | solution.py:685
  80.2 15.3 %collective-permute-start.11 = (f32[104,384]{1,0:T(8,128)}, f32[104,384]{1,0:T(8,128)S(1)}, u32[]{:S(2)}, u32[]{:S(2)}) collective-permute-start(f32[104,384]{1,0:T(8,128)} %get-tuple-element.61), channel_id=1, source_target_pairs={{0,8},{4,12},{8,0},{12,4},{1,9},{5,13},{9,1},{13,5},{2,10},{6,14},... | collective-permute-start | bytes 479240 | tf_op jit(solution)/shard_map/ppermute | solution.py:685
  81.4 14.2 %collective-permute-start.12 = (f32[104,384]{1,0:T(8,128)}, f32[104,384]{1,0:T(8,128)S(1)}, u32[]{:S(2)}, u32[]{:S(2)}) collective-permute-start(f32[104,384]{1,0:T(8,128)} %get-tuple-element.62), channel_id=1, source_target_pairs={{0,12},{4,8},{8,4},{12,0},{1,13},{5,9},{9,5},{13,1},{2,14},{6,10},... | collective-permute-start | bytes 479240 | tf_op jit(solution)/shard_map/ppermute | solution.py:685
  96.6 14.5 %collective-permute-start.13 = (f32[104,384]{1,0:T(8,128)S(1)}, f32[104,384]{1,0:T(8,128)S(1)}, u32[]{:S(2)}, u32[]{:S(2)}) collective-permute-start(f32[104,384]{1,0:T(8,128)S(1)} %add_add_fusion.1.refs_1_.refs_3_), channel_id=1, source_target_pairs={{0,15},{1,14},{2,13},{3,12},{4,11},{5,10},{6,9},{7,8},{8,7},{9,6},... | collective-permute-start | bytes 479240 | tf_op jit(solution)/shard_map/ppermute | solution.py:689
  100.3 22.1 %collective-permute-start.9 = (f32[80,384]{1,0:T(8,128)S(1)}, f32[80,384]{1,0:T(8,128)S(1)}, u32[]{:S(2)}, u32[]{:S(2)}) collective-permute-start(f32[80,384]{1,0:T(8,128)S(1)} %add.93.refs_0_.refs_1_), channel_id=1, source_target_pairs={{0,4},{4,0},{8,12},{12,8},{1,5},{5,1},{9,13},{13,9},{2,6},{6,2},{1... | collective-permute-start | bytes 368648 | tf_op jit(solution)/shard_map/ppermute | solution.py:685
  108.7 14.4 %collective-permute-start.14 = (f32[80,384]{1,0:T(8,128)S(1)}, f32[80,384]{1,0:T(8,128)S(1)}, u32[]{:S(2)}, u32[]{:S(2)}) collective-permute-start(f32[80,384]{1,0:T(8,128)S(1)} %add.93.refs_0_.refs_1_), channel_id=1, source_target_pairs={{0,8},{4,12},{8,0},{12,4},{1,9},{5,13},{9,1},{13,5},{2,10},{6,14},... | collective-permute-start | bytes 368648 | tf_op jit(solution)/shard_map/ppermute | solution.py:685
  108.7 14.4 %collective-permute-start.15 = (f32[80,384]{1,0:T(8,128)S(1)}, f32[80,384]{1,0:T(8,128)S(1)}, u32[]{:S(2)}, u32[]{:S(2)}) collective-permute-start(f32[80,384]{1,0:T(8,128)S(1)} %add.93.refs_0_.refs_1_), channel_id=1, source_target_pairs={{0,12},{4,8},{8,4},{12,0},{1,13},{5,9},{9,5},{13,1},{2,14},{6,10},... | collective-permute-start | bytes 368648 | tf_op jit(solution)/shard_map/ppermute | solution.py:685
  126.4 25.2 %collective-permute-start.16 = (f32[1,2,80,640]{3,2,1,0:T(8,128)}, f32[1,2,80,640]{3,2,1,0:T(8,128)S(1)}, u32[]{:S(2)}, u32[]{:S(2)}) collective-permute-start(f32[1,2,80,640]{3,2,1,0:T(8,128)} %join.4.refs_1_), channel_id=1, source_target_pairs={{0,2},{1,3},{2,0},{3,1},{4,6},{5,7},{6,4},{7,5},{8,10},{9,11},{10,... | collective-permute-start | bytes 1228808 | tf_op jit(solution)/shard_map/ppermute | solution.py:685
  133.2 14.9 %collective-permute-start.19 = (f32[104,384]{1,0:T(8,128)}, f32[104,384]{1,0:T(8,128)S(1)}, u32[]{:S(2)}, u32[]{:S(2)}) collective-permute-start(f32[104,384]{1,0:T(8,128)} %tie.22.refs_1_), channel_id=1, source_target_pairs={{0,8},{4,12},{8,0},{12,4},{1,9},{5,13},{9,1},{13,5},{2,10},{6,14},... | collective-permute-start | bytes 479240 | tf_op jit(solution)/shard_map/ppermute | solution.py:685
  133.2 14.9 %collective-permute-start.20 = (f32[104,384]{1,0:T(8,128)}, f32[104,384]{1,0:T(8,128)S(1)}, u32[]{:S(2)}, u32[]{:S(2)}) collective-permute-start(f32[104,384]{1,0:T(8,128)} %tie.22.refs_1_), channel_id=1, source_target_pairs={{0,12},{4,8},{8,4},{12,0},{1,13},{5,9},{9,5},{13,1},{2,14},{6,10},... | collective-permute-start | bytes 479240 | tf_op jit(solution)/shard_map/ppermute | solution.py:685
  225.4 29.4 %collective-permute-start.26 = (f32[1,2,80,640]{3,2,1,0:T(8,128)}, f32[1,2,80,640]{3,2,1,0:T(8,128)S(1)}, u32[]{:S(2)}, u32[]{:S(2)}) collective-permute-start(f32[1,2,80,640]{3,2,1,0:T(8,128)} %get-tuple-element.72.refs_0_), channel_id=1, source_target_pairs={{0,2},{1,3},{2,0},{3,1},{4,6},{5,7},{6,4},{7,5},{8,10},{9,11},{10,... | collective-permute-start | bytes 1228808 | tf_op jit(solution)/shard_map/ppermute | solution.py:685
  255.5 20.3 %collective-permute-start.27 = (f32[1,2,104,640]{3,2,1,0:T(8,128)}, f32[1,2,104,640]{3,2,1,0:T(8,128)S(1)}, u32[]{:S(2)}, u32[]{:S(2)}) collective-permute-start(f32[1,2,104,640]{3,2,1,0:T(8,128)} %tie.25), channel_id=1, source_target_pairs={{0,2},{1,3},{2,0},{3,1},{4,6},{5,7},{6,4},{7,5},{8,10},{9,11},{10,... | collective-permute-start | bytes 1597448 | tf_op jit(solution)/shard_map/ppermute | solution.py:685
  279.3 13.6 %collective-permute-start.34 = (f32[104,384]{1,0:T(8,128)}, f32[104,384]{1,0:T(8,128)S(1)}, u32[]{:S(2)}, u32[]{:S(2)}) collective-permute-start(f32[104,384]{1,0:T(8,128)} %get-tuple-element.82), channel_id=1, source_target_pairs={{0,4},{4,0},{8,12},{12,8},{1,5},{5,1},{9,13},{13,9},{2,6},{6,2},{1... | collective-permute-start | bytes 479240 | tf_op jit(solution)/shard_map/ppermute | solution.py:685
  281.6 15.0 %collective-permute-start.35 = (f32[104,384]{1,0:T(8,128)}, f32[104,384]{1,0:T(8,128)S(1)}, u32[]{:S(2)}, u32[]{:S(2)}) collective-permute-start(f32[104,384]{1,0:T(8,128)} %get-tuple-element.83), channel_id=1, source_target_pairs={{0,8},{4,12},{8,0},{12,4},{1,9},{5,13},{9,1},{13,5},{2,10},{6,14},... | collective-permute-start | bytes 479240 | tf_op jit(solution)/shard_map/ppermute | solution.py:685
  281.6 14.9 %collective-permute-start.36 = (f32[104,384]{1,0:T(8,128)}, f32[104,384]{1,0:T(8,128)S(1)}, u32[]{:S(2)}, u32[]{:S(2)}) collective-permute-start(f32[104,384]{1,0:T(8,128)} %get-tuple-element.84), channel_id=1, source_target_pairs={{0,12},{4,8},{8,4},{12,0},{1,13},{5,9},{9,5},{13,1},{2,14},{6,10},... | collective-permute-start | bytes 479240 | tf_op jit(solution)/shard_map/ppermute | solution.py:685
  297.5 20.8 %collective-permute-start.37 = (f32[104,384]{1,0:T(8,128)S(1)}, f32[104,384]{1,0:T(8,128)S(1)}, u32[]{:S(2)}, u32[]{:S(2)}) collective-permute-start(f32[104,384]{1,0:T(8,128)S(1)} %add_add_fusion.refs_1_.refs_7_), channel_id=1, source_target_pairs={{0,15},{1,14},{2,13},{3,12},{4,11},{5,10},{6,9},{7,8},{8,7},{9,6},... | collective-permute-start | bytes 479240 | tf_op jit(solution)/shard_map/ppermute | solution.py:689
  309.3 19.5 %collective-permute-start.33 = (f32[80,384]{1,0:T(8,128)S(1)}, f32[80,384]{1,0:T(8,128)S(1)}, u32[]{:S(2)}, u32[]{:S(2)}) collective-permute-start(f32[80,384]{1,0:T(8,128)S(1)} %add.101.refs_0_.refs_1_), channel_id=1, source_target_pairs={{0,4},{4,0},{8,12},{12,8},{1,5},{5,1},{9,13},{13,9},{2,6},{6,2},{1... | collective-permute-start | bytes 368648 | tf_op jit(solution)/shard_map/ppermute | solution.py:685
  315.9 13.6 %collective-permute-start.38 = (f32[80,384]{1,0:T(8,128)S(1)}, f32[80,384]{1,0:T(8,128)S(1)}, u32[]{:S(2)}, u32[]{:S(2)}) collective-permute-start(f32[80,384]{1,0:T(8,128)S(1)} %add.101.refs_0_.refs_1_), channel_id=1, source_target_pairs={{0,8},{4,12},{8,0},{12,4},{1,9},{5,13},{9,1},{13,5},{2,10},{6,14},... | collective-permute-start | bytes 368648 | tf_op jit(solution)/shard_map/ppermute | solution.py:685
  315.9 13.6 %collective-permute-start.39 = (f32[80,384]{1,0:T(8,128)S(1)}, f32[80,384]{1,0:T(8,128)S(1)}, u32[]{:S(2)}, u32[]{:S(2)}) collective-permute-start(f32[80,384]{1,0:T(8,128)S(1)} %add.101.refs_0_.refs_1_), channel_id=1, source_target_pairs={{0,12},{4,8},{8,4},{12,0},{1,13},{5,9},{9,5},{13,1},{2,14},{6,10},... | collective-permute-start | bytes 368648 | tf_op jit(solution)/shard_map/ppermute | solution.py:685
  332.9 24.8 %collective-permute-start.40 = (f32[1,2,80,640]{3,2,1,0:T(8,128)}, f32[1,2,80,640]{3,2,1,0:T(8,128)S(1)}, u32[]{:S(2)}, u32[]{:S(2)}) collective-permute-start(f32[1,2,80,640]{3,2,1,0:T(8,128)} %join.6.refs_0_.refs_1_), channel_id=1, source_target_pairs={{0,2},{1,3},{2,0},{3,1},{4,6},{5,7},{6,4},{7,5},{8,10},{9,11},{10,... | collective-permute-start | bytes 1228808 | tf_op jit(solution)/shard_map/ppermute | solution.py:685
  339.6 14.5 %collective-permute-start.43 = (f32[104,384]{1,0:T(8,128)}, f32[104,384]{1,0:T(8,128)S(1)}, u32[]{:S(2)}, u32[]{:S(2)}) collective-permute-start(f32[104,384]{1,0:T(8,128)} %tie.30.refs_1_), channel_id=1, source_target_pairs={{0,8},{4,12},{8,0},{12,4},{1,9},{5,13},{9,1},{13,5},{2,10},{6,14},... | collective-permute-start | bytes 479240 | tf_op jit(solution)/shard_map/ppermute | solution.py:685
  339.6 14.5 %collective-permute-start.44 = (f32[104,384]{1,0:T(8,128)}, f32[104,384]{1,0:T(8,128)S(1)}, u32[]{:S(2)}, u32[]{:S(2)}) collective-permute-start(f32[104,384]{1,0:T(8,128)} %tie.30.refs_1_), channel_id=1, source_target_pairs={{0,12},{4,8},{8,4},{12,0},{1,13},{5,9},{9,5},{13,1},{2,14},{6,10},... | collective-permute-start | bytes 479240 | tf_op jit(solution)/shard_map/ppermute | solution.py:685
  (85 other events, 442.0 us)

commit v2 on v1

--- a/solution.py
+++ b/solution.py
@@ -14,7 +14,7 @@
 bf16 = jnp.bfloat16
 root_half = 0.7071067811865476
 inv_root_two_pi = 0.3989422804014327
-VMEM_LIMIT = 60 * 1024 * 1024
+VMEM_LIMIT = 64 * 1024 * 1024
 NT = (((1,), (1,)), ((), ()))
 TN = (((0,), (0,)), ((), ()))
 
@@ -43,6 +43,7 @@
         self.xb = math.gcd(8, nx)
         self.blk = self.xb * ny
         self.rows = self.cc * wk
+        self.tall = round_up(self.rows, 16)
         self.bb = math.gcd(2, wb)
         self.lb = math.gcd(4, nx)
         self.batch = max(d for d in range(1, 6) if self.cc % d == 0)
@@ -372,9 +373,12 @@
     def _():
         for n in range(2):
             found = [moved(part[n][...], part[2][...], left=True) for part in parts]
-            ordered_ref[:, n * plan.ll : (n + 1) * plan.ll] = sum(found[1:], found[0])
-
-    return [moved(ordered_ref[...], chosen_ref[n]) for n in range(plan.bb)]
+            high, low = split(sum(found[1:], found[0]))
+            ordered_ref[: plan.rows, n * plan.ll : (n + 1) * plan.ll] = high
+            ordered_ref[plan.tall : plan.tall + plan.rows, n * plan.ll : (n + 1) * plan.ll] = low
+
+    both = [dot(ordered_ref[...], chosen_ref[n]) for n in range(plan.bb)]
+    return [b[: plan.rows] + b[plan.tall : plan.tall + plan.rows] for b in both]
 
 
 def give(plan, made_ref, order_ref, back_ref, own_ref, mirror_ref, sums_ref):
@@ -477,17 +481,21 @@
         send_ref[pair] = jnp.where(odd, low, high)
 
 
-def cut_kernel(plan, slab_ref, keep_ref, arrived_ref, *refs):
+def send_kernel(place_ref, keep_ref, arrived_ref, send_ref):
+    send_ref[...] = keep_ref[...] + arrived_ref[...]
+
+
+def cut_kernel(plan, place_ref, keep_ref, arrived_ref, came_ref, *refs):
     out_refs, held_ref = refs[:-1], refs[-1]
     lane = lax.broadcasted_iota(jnp.int32, held_ref.shape[1:], 1)
-    real = keep_ref[0, 0] + arrived_ref[0, 0]
-    imag = keep_ref[0, 1] + arrived_ref[0, 1]
+    real = keep_ref[0, 0] + arrived_ref[0, 0] + came_ref[0, 0]
+    imag = keep_ref[0, 1] + arrived_ref[0, 1] + came_ref[0, 1]
     for g in range(plan.s):
         first = pltpu.roll(real, (plan.lp - g * plan.span) % plan.lp, 1)[:, : plan.ll]
         second = pltpu.roll(imag, (plan.lp - g * plan.span + plan.span) % plan.lp, 1)[:, : plan.ll]
         held_ref[g] = jnp.where(lane < plan.span, first, jnp.where(lane < 2 * plan.span, second, 0.0))
     for j, out_ref in enumerate(out_refs):
-        out_ref[...] = held_ref[slab_ref[0] ^ j]
+        out_ref[...] = held_ref[place_ref[0] ^ j]
 
 
 def join_kernel(plan, slab_ref, *refs):
@@ -657,7 +665,7 @@
         plan = self.plan
         modes = (plan.rts[chunk], plan.ll)
         order, disorder = self.order[chunk], self.disorder[chunk]
-        ordered = pltpu.VMEM((plan.rows, 2 * plan.ll), f32)
+        ordered = pltpu.VMEM((2 * plan.tall, 2 * plan.ll), bf16)
         return call(
             partial(kernel, plan), name, plan.wb // plan.bb,
             [
@@ -666,13 +674,13 @@
                 leading((plan.bb, *weights.shape[1:])),
             ],
             [whole_shape(modes)] * 2, [shaped(*modes)] * 2,
-            [ordered, pltpu.VMEM((plan.bb, plan.rows, 256), f32), ordered], 9, before,
+            [ordered, pltpu.VMEM((plan.bb, plan.rows, 256), f32), pltpu.VMEM((plan.rows, 2 * plan.ll), f32)], 9, before,
         )(own, mirror, order, disorder, self.chosen, self.back, weights)
 
     def outer(self, before, modes, grads, weights):
         plan = self.plan
         parts = [part for pair in (*modes, *grads) for part in pair]
-        ordered = pltpu.VMEM((plan.rows, 2 * plan.ll), f32)
+        ordered = pltpu.VMEM((2 * plan.tall, 2 * plan.ll), bf16)
         out = leading((plan.bb, *weights.shape[1:]))
         return call(
             partial(outer_kernel, plan), "outer", plan.wb // plan.bb,
@@ -687,6 +695,27 @@
     def mirrored(self, value):
         total = self.plan.s * self.plan.ch
         return lax.ppermute(value, ("slab", "chan"), [(i, total - 1 - i) for i in range(total)])
+
+    def chosen_half(self, kernel, name, grid, in_specs, out_specs, out_shape, scratch, arrays):
+        place = jnp.stack([self.slab, self.chan // (self.plan.ch // 2)]).astype(jnp.int32)
+        return pl.pallas_call(
+            kernel,
+            grid_spec=pltpu.PrefetchScalarGridSpec(
+                num_scalar_prefetch=1, grid=grid, in_specs=in_specs, out_specs=out_specs, scratch_shapes=scratch
+            ),
+            out_shape=out_shape,
+            name=name,
+            compiler_params=pltpu.CompilerParams(vmem_limit_bytes=VMEM_LIMIT, dimension_semantics=("arbitrary",)),
+            cost_estimate=pl.CostEstimate(flops=10**9, bytes_accessed=4 * 10**6, transcendentals=0),
+        )(place, *arrays)
+
+    def sent_half(self, keep, arrived):
+        block = (1, 1) + keep.shape[2:]
+        spec = pl.BlockSpec(block, lambda r, place: (1 - place[1], r, 0, 0))
+        return self.chosen_half(
+            send_kernel, "send", (2,), [spec, spec], pl.BlockSpec(block, lambda r, place: (0, r, 0, 0)),
+            shaped(1, *keep.shape[1:]), [], (keep, arrived),
+        )
 
     def halve(self, keep, arrived, bit):
         mine = ((self.chan // bit) % 2).astype(jnp.int32).reshape(1)
@@ -697,20 +726,24 @@
         )(mine, keep, arrived)
 
     def sums_over_chan(self, keep, arrived, before):
-        bit, sent = 2, arrived
-        while bit < self.plan.ch:
+        bit = 2
+        while 2 * bit < self.plan.ch:
             keep, sent = self.halve(keep, arrived, bit)
-            arrived = self.across(tie(sent, *before) if bit == 2 else sent, "chan", bit)
+            arrived = self.across(sent, "chan", bit)
             bit *= 2
-        return keep, sent, arrived
-
-    def cut(self, keep, arrived):
-        plan = self.plan
-        size = (keep.shape[2], plan.ll)
-        mine, *pieces = call(
-            partial(cut_kernel, plan), "cut", 1, [scalar(), whole(keep), whole(keep)],
-            [whole_shape(size)] * plan.s, [shaped(*size)] * plan.s, [pltpu.VMEM((plan.s, *size), f32)], 2,
-        )(self.slab_index, keep, arrived)
+        sent = tie(self.sent_half(keep, arrived), *before)
+        return (keep, arrived), sent, self.across(sent, "chan", bit)
+
+    def cut(self, kept, came):
+        plan = self.plan
+        size = (came.shape[2], plan.ll)
+        block = (1,) + came.shape[1:]
+        spec = pl.BlockSpec(block, lambda i, place: (place[1], 0, 0, 0))
+        mine, *pieces = self.chosen_half(
+            partial(cut_kernel, plan), "cut", (1,), [spec, spec, pl.BlockSpec(block, lambda i, place: (0, 0, 0, 0))],
+            [pl.BlockSpec(size, lambda i, place: (0, 0))] * plan.s, [shaped(*size)] * plan.s,
+            [pltpu.VMEM((plan.s, *size), f32)], (*kept, came),
+        )
         return mine, pieces
 
     def join(self, mine, arrived):

time: 402 us -> 411 us (1.022)
  local copies, waits for them, and re-layouts: 47.7 us -> 31.4 us
  other arithmetic: 6.91 us -> 15.4 us
  waiting for transfers between devices: 66.6 us -> 72.9 us
  starting transfers between devices: 72.3 us -> 78.1 us
    unnamed x124 -> x38, local copies, waits for them, and re-layouts: 32.6 us -> 14.9 us
    pallas_call x8, Pallas kernels: 19.3 us -> 33.9 us  [chosen_half(): pl.pallas_call(kernel, grid_spec=pltpu.PrefetchScalarGridSpec(num_scalar_...]
    pallas_call x2, Pallas kernels: 39.5 us -> 28.3 us  [linear(): call(partial(linear_kernel, plan), 'linear', plan.nx // plan.lb, [spec, w...]
    ppermute x40, starting transfers between devices: 57.8 us -> 64.8 us  [across(): return lax.ppermute(value, axis, [(i, i ^ bit) for i in range(size)])]
    ppermute x40, waiting for transfers between devices: 53.6 us -> 59.7 us  [across(): return lax.ppermute(value, axis, [(i, i ^ bit) for i in range(size)])]
  transfers between devices with their start and end apart: 48 -> 48, of which waited for: 16 -> 17; matrix products, arithmetic and copies ran while one was open for 6% -> 9% of each run, Pallas kernels for 27% -> 22%
where the time goes in v2:
time: 411 us; the launch traced here: 406 us
  Pallas kernels  207 us (50%)
  starting transfers between devices  78.1 us (19%)
  waiting for transfers between devices  72.9 us (18%)
  local copies, waits for them, and re-layouts  31.4 us (8%)
  other arithmetic  15.4 us (4%)
    ppermute x40, starting transfers between devices, across(): return lax.ppermute(value, axis, [(i, i ^ bit) for i in range(size)])  64.8 us
    ppermute x40, waiting for transfers between devices, across(): return lax.ppermute(value, axis, [(i, i ^ bit) for i in range(size)])  59.7 us
    pallas_call x1, Pallas kernels, middle(): call(partial(middle_kernel, plan), 'middle', plan.nx // plan.xb, [scalar(...  47.1 us
    pallas_call x8, Pallas kernels, chosen_half(): pl.pallas_call(kernel, grid_spec=pltpu.PrefetchScalarGridSpec(num_scalar_...  33.9 us
    pallas_call x4, Pallas kernels, mix(): call(partial(kernel, plan), name, plan.wb // plan.bb, [whole_shape(modes)...  33.5 us
    pallas_call x2, Pallas kernels, linear(): call(partial(linear_kernel, plan), 'linear', plan.nx // plan.lb, [spec, w...  28.3 us
    pallas_call x1, Pallas kernels, analyse(): call(partial(analyse_kernel, plan), 'analyse', plan.nx // plan.xb, [scala...  27.1 us
    pallas_call x1, Pallas kernels, synthesise(): call(partial(synthesise_kernel, plan), 'synthesise', plan.nx // plan.xb,...  19.8 us
  transfers between devices with their start and end apart: 48, of which 17 were waited for; matrix products, arithmetic and copies ran while one was open for 9% of the time, Pallas kernels for 22%

profile of v2, /device:TPU:0, one launch (start us, length us, event | category | flops | bytes accessed | tf_op | source)
XLA Modules:
  0.0 405.8 jit_solution(1355029365703159416)
XLA Ops:
  1.9 27.1 %analyse.1 = (f32[2,2,80,640]{3,2,1,0:T(8,128)}, f32[2,2,104,640]{3,2,1,0:T(8,128)}, f32[2,2,80,640]{3,2,1,0:T(8,128)}, f32[2,2,104,640]{3,2,1,0:T(8,128)}) custom-call(s32[1]{0:T(128)} %bitcast.refs_0_, f32[32,20,32,128]{3,2,1,0:T(8,128)} %bitcast.57, bf16[4,768,1280]{2,1,0:T(8,128)(2,1)} %constant.132.clone.refs_2_.refs_7_.refs_6_, ...), custom_call_target="tpu_custom_call" | custom-call | flops 29899999232 | bytes 93600000 | tf_op jit(solution)/shard_map/analyse/pallas_call | solution.py:621
  38.8 14.2 %linear.2.refs_1_.refs_5_ = f32[32,20,32,128]{3,2,1,0:T(8,128)} custom-call(f32[1,2,80,640]{3,2,1,0:T(8,128)} %send.5.refs_0_, f32[2,2,104,640]{3,2,1,0:T(8,128)} %collective-permute-done.arrived_ref.refs_1_, f32[32,20,32,128]{3,2,1,0:T(8,128)} %bitcast.58, f32[20,20]{1,0:T(8,128)} %bitcast.56, f32[1,20]{1,0:T(1,128)} %bitcast.60), custom_call_target="tpu_custom_call" | custom-call | flops 13799999488 | bytes 43200000 | tf_op jit(solution)/shard_map/linear/pallas_call | solution.py:657
  65.2 7.8 %collective-permute-done.5 = f32[80,384]{1,0:T(8,128)S(1)} collective-permute-done((f32[80,384]{1,0:T(8,128)}, f32[80,384]{1,0:T(8,128)S(1)}, u32[]{:S(2)}, u32[]{:S(2)}) %collective-permute-start.5) | collective-permute-done | bytes 122912 | tf_op jit(solution)/shard_map/ppermute | solution.py:693
  75.9 6.8 %copy.41 = f32[8,8,2,20,640]{4,1,3,2,0:T(8,128)} copy(f32[8,8,2,20,640]{4,2,3,1,0:T(2,128)} %param.17) | data formatting | bytes 13107200 | tf_op args[2]
  90.7 8.3 %mix.2 = (f32[80,384]{1,0:T(8,128)}, f32[80,384]{1,0:T(8,128)}) custom-call(f32[104,384]{1,0:T(8,128)} %get-tuple-element.45.refs_0_, f32[80,384]{1,0:T(8,128)} %add_add_fusion.3.refs_1_, f32[80,384]{1,0:T(8,128)} %collective-permute-done.7.refs_2_, bf16[160,80]{1,0:T(8,128)(2,1)} %dynamic-slice_bitcast_fusion.3.refs_3_.refs_9_, ...), custom_call_target="tpu_custom_call" | custom-call | flops 10350000128 | bytes 32400000 | tf_op jit(solution)/shard_map/mix/pallas_call | solution.py:669
  107.8 9.3 %collective-permute-start.9 = (f32[80,384]{1,0:T(8,128)}, f32[80,384]{1,0:T(8,128)}, u32[]{:S(2)}, u32[]{:S(2)}) collective-permute-start(f32[80,384]{1,0:T(8,128)} %add.89.refs_0_.refs_1_), channel_id=1, source_target_pairs={{0,4},{4,0},{8,12},{12,8},{1,5},{5,1},{9,13},{13,9},{2,6},{6,2},{1... | collective-permute-start | bytes 368648 | tf_op jit(solution)/shard_map/ppermute | solution.py:693
  119.7 8.6 %mix.3 = (f32[104,384]{1,0:T(8,128)}, f32[104,384]{1,0:T(8,128)}) custom-call(f32[80,384]{1,0:T(8,128)} %add.89.refs_0_.refs_1_, f32[104,384]{1,0:T(8,128)} %copy-done.10, f32[104,384]{1,0:T(8,128)} %collective-permute-done.13.refs_2_.refs_4_, bf16[160,104]{1,0:T(8,128)(2,1)} %dynamic-slice_bitcast_fusion.1.refs_3_.refs_10_, ...), custom_call_target="tpu_custom_call" | custom-call | flops 10350000128 | bytes 32400000 | tf_op jit(solution)/shard_map/mix/pallas_call | solution.py:669
  144.4 4.4 %collective-permute-done.18.refs_2_ = f32[104,384]{1,0:T(8,128)} collective-permute-done((f32[104,384]{1,0:T(8,128)}, f32[104,384]{1,0:T(8,128)}, u32[]{:S(2)}, u32[]{:S(2)}) %collective-permute-start.18) | collective-permute-done | bytes 159776 | tf_op jit(solution)/shard_map/ppermute | solution.py:693
  148.8 7.4 %collective-permute-done.19.refs_3_ = f32[104,384]{1,0:T(8,128)} collective-permute-done((f32[104,384]{1,0:T(8,128)}, f32[104,384]{1,0:T(8,128)}, u32[]{:S(2)}, u32[]{:S(2)}) %collective-permute-start.19) | collective-permute-done | bytes 159776 | tf_op jit(solution)/shard_map/ppermute | solution.py:693
  159.9 12.1 %collective-permute-done.21 = f32[1,2,104,640]{3,2,1,0:T(8,128)S(1)} collective-permute-done((f32[1,2,104,640]{3,2,1,0:T(8,128)}, f32[1,2,104,640]{3,2,1,0:T(8,128)S(1)}, u32[]{:S(2)}, u32[]{:S(2)}) %collective-permute-start.21) | collective-permute-done | bytes 532512 | tf_op jit(solution)/shard_map/ppermute | solution.py:693
  179.6 47.1 %middle.1 = (f32[32,20,32,128]{3,2,1,0:T(8,128)}, f32[32,20,32,128]{3,2,1,0:T(8,128)}, f32[2,2,80,640]{3,2,1,0:T(8,128)}, f32[2,2,104,640]{3,2,1,0:T(8,128)}, f3...) custom-call(s32[1]{0:T(128)} %bitcast.refs_0_, f32[2,2,80,640]{3,2,1,0:T(8,128)} %copy-done.6, ...), custom_call_target="tpu_custom_call" | custom-call | flops 54050000896 | bytes 169200000 | tf_op jit(solution)/shard_map/middle/pallas_call | solution.py:634
  234.7 14.2 %linear.3.refs_1_.refs_5_ = f32[32,20,32,128]{3,2,1,0:T(8,128)} custom-call(f32[1,2,80,640]{3,2,1,0:T(8,128)} %send.7.refs_0_, f32[2,2,104,640]{3,2,1,0:T(8,128)} %collective-permute-done.24.arrived_ref.refs_1_, f32[32,20,32,128]{3,2,1,0:T(8,128)} %get-tuple-element.58.refs_2_, f32[20,20]{1,0:T(8,128)} %refs_3_.2, f32[1,20]{1,0:T(1,128)} %broadcast_1_refs_4_.2.refs_4_), custom_call_target="tpu_custom_call" | custom-call | flops 13799999488 | bytes 43200000 | tf_op jit(solution)/shard_map/linear/pallas_call | solution.py:657
  248.9 13.7 %send.6.refs_0_ = f32[1,2,104,640]{3,2,1,0:T(8,128)} custom-call(s32[2]{0:T(128)} %pad_add_fusion.place_ref, f32[2,2,104,640]{3,2,1,0:T(8,128)} %get-tuple-element.54.keep_ref, f32[2,2,104,640]{3,2,1,0:T(8,128)} %collective-permute-done.24.arrived_ref.refs_1_), custom_call_target="tpu_custom_call" | custom-call | flops 1000000000 | bytes 4000000 | tf_op jit(solution)/shard_map/send/pallas_call | solution.py:701
  267.1 4.0 collective-permute-start.28
  275.2 7.6 %collective-permute-done.29 = f32[80,384]{1,0:T(8,128)S(1)} collective-permute-done((f32[80,384]{1,0:T(8,128)}, f32[80,384]{1,0:T(8,128)S(1)}, u32[]{:S(2)}, u32[]{:S(2)}) %collective-permute-start.29) | collective-permute-done | bytes 122912 | tf_op jit(solution)/shard_map/ppermute | solution.py:693
  292.2 8.3 %mix_back.2 = (f32[80,384]{1,0:T(8,128)}, f32[80,384]{1,0:T(8,128)}) custom-call(f32[104,384]{1,0:T(8,128)} %get-tuple-element.63.refs_0_, f32[80,384]{1,0:T(8,128)} %add_add_fusion.2.refs_1_.refs_5_, f32[80,384]{1,0:T(8,128)} %collective-permute-done.31.refs_2_.refs_6_, bf16[160,80]{1,0:T(8,128)(2,1)} %dynamic-slice_bitcast_fusion.3.refs_3_.refs_9_, ...), custom_call_target="tpu_custom_call" | custom-call | flops 10350000128 | bytes 32400000 | tf_op jit(solution)/shard_map/mix_back/pallas_call | solution.py:669
  300.5 4.4 %collective-permute-done.35 = f32[104,384]{1,0:T(8,128)} collective-permute-done((f32[104,384]{1,0:T(8,128)}, f32[104,384]{1,0:T(8,128)}, u32[]{:S(2)}, u32[]{:S(2)}) %collective-permute-start.35) | collective-permute-done | bytes 159776 | tf_op jit(solution)/shard_map/ppermute | solution.py:693
  310.6 5.8 %collective-permute-done.32 = f32[80,384]{1,0:T(8,128)S(1)} collective-permute-done((f32[80,384]{1,0:T(8,128)S(1)}, f32[80,384]{1,0:T(8,128)S(1)}, u32[]{:S(2)}, u32[]{:S(2)}) %collective-permute-start.32) | collective-permute-done | bytes 122912 | tf_op jit(solution)/shard_map/ppermute | solution.py:697
  317.1 7.0 %collective-permute-start.33 = (f32[80,384]{1,0:T(8,128)}, f32[80,384]{1,0:T(8,128)}, u32[]{:S(2)}, u32[]{:S(2)}) collective-permute-start(f32[80,384]{1,0:T(8,128)} %add.97.refs_0_.refs_1_), channel_id=1, source_target_pairs={{0,4},{4,0},{8,12},{12,8},{1,5},{5,1},{9,13},{13,9},{2,6},{6,2},{1... | collective-permute-start | bytes 368648 | tf_op jit(solution)/shard_map/ppermute | solution.py:693
  326.9 8.3 %mix_back.3 = (f32[104,384]{1,0:T(8,128)}, f32[104,384]{1,0:T(8,128)}) custom-call(f32[80,384]{1,0:T(8,128)} %add.97.refs_0_.refs_1_, f32[104,384]{1,0:T(8,128)} %copy-done.11, f32[104,384]{1,0:T(8,128)} %collective-permute-done.37.refs_2_.refs_8_, bf16[160,104]{1,0:T(8,128)(2,1)} %dynamic-slice_bitcast_fusion.1.refs_3_.refs_10_, ...), custom_call_target="tpu_custom_call" | custom-call | flops 10350000128 | bytes 32400000 | tf_op jit(solution)/shard_map/mix_back/pallas_call | solution.py:669
  340.4 4.2 %collective-permute-done.41 = f32[104,384]{1,0:T(8,128)} collective-permute-done((f32[104,384]{1,0:T(8,128)}, f32[104,384]{1,0:T(8,128)}, u32[]{:S(2)}, u32[]{:S(2)}) %collective-permute-start.41) | collective-permute-done | bytes 159776 | tf_op jit(solution)/shard_map/ppermute | solution.py:697
  351.2 8.3 %outer.1.refs_1_ = f32[8,2,20,8,640]{4,3,2,1,0:T(8,128)} custom-call(f32[1,2,80,640]{3,2,1,0:T(8,128)} %join.6.refs_0_.refs_1_, f32[80,384]{1,0:T(8,128)} %add_add_fusion.3.refs_1_, f32[80,384]{1,0:T(8,128)} %collective-permute-done.7.refs_2_, f32[104,384]{1,0:T(8,128)} %copy-done.10, f32[104,384]{1,0:T(8,128)} %collective-permute-done.13.refs_2_.refs_4_, ...), custom_call_target="tpu_custom_call" | custom-call | flops 10350000128 | bytes 32400000 | tf_op jit(solution)/shard_map/outer/pallas_call | solution.py:685
  367.2 10.7 %copy.40 = f32[8,2,20,8,640]{4,1,2,3,0:T(2,128)} copy(f32[8,2,20,8,640]{4,3,2,1,0:T(8,128)} %outer.1.refs_1_) | data formatting | bytes 13107200 | tf_op jit(solution)/shard_map/outer/pallas_call | solution.py:685
  385.8 19.8 %synthesise.1 = f32[32,20,32,128]{3,2,1,0:T(8,128)} custom-call(s32[1]{0:T(128)} %bitcast.refs_0_, f32[2,2,80,640]{3,2,1,0:T(8,128)} %copy-done.7, f32[2,2,104,640]{3,2,1,0:T(8,128)} %copy-done.5, f32[2,2,80,640]{3,2,1,0:T(8,128)} %copy-done.16, f32[2,2,104,640]{3,2,1,0:T(8,128)} %collective-permute-done.47.refs_4_, ...), custom_call_target="tpu_custom_call" | custom-call | flops 23000000512 | bytes 72000000 | tf_op jit(solution)/shard_map/synthesise/pallas_call | solution.py:645
  (173 shorter events, 135.3 us)
Async XLA Ops:
  35.9 19.6 %collective-permute-start.2 = (f32[1,2,80,640]{3,2,1,0:T(8,128)}, f32[1,2,80,640]{3,2,1,0:T(8,128)}, u32[]{:S(2)}, u32[]{:S(2)}) collective-permute-start(f32[1,2,80,640]{3,2,1,0:T(8,128)} %send.5.refs_0_), channel_id=1, source_target_pairs={{0,2},{1,3},{2,0},{3,1},{4,6},{5,7},{6,4},{7,5},{8,10},{9,11},{10,... | collective-permute-start | bytes 1228808 | tf_op jit(solution)/shard_map/ppermute | solution.py:693
  55.6 27.2 %collective-permute-start.3 = (f32[1,2,104,640]{3,2,1,0:T(8,128)}, f32[1,2,104,640]{3,2,1,0:T(8,128)}, u32[]{:S(2)}, u32[]{:S(2)}) collective-permute-start(f32[1,2,104,640]{3,2,1,0:T(8,128)} %tie.18), channel_id=1, source_target_pairs={{0,2},{1,3},{2,0},{3,1},{4,6},{5,7},{6,4},{7,5},{8,10},{9,11},{10,... | collective-permute-start | bytes 1597448 | tf_op jit(solution)/shard_map/ppermute | solution.py:693
  74.5 16.2 %collective-permute-start.7 = (f32[80,384]{1,0:T(8,128)}, f32[80,384]{1,0:T(8,128)}, u32[]{:S(2)}, u32[]{:S(2)}) collective-permute-start(f32[80,384]{1,0:T(8,128)} %add_add_fusion.3.refs_1_), channel_id=1, source_target_pairs={{0,15},{1,14},{2,13},{3,12},{4,11},{5,10},{6,9},{7,8},{8,7},{9,6},... | collective-permute-start | bytes 368648 | tf_op jit(solution)/shard_map/ppermute | solution.py:697
  85.9 16.4 %collective-permute-start.10 = (f32[104,384]{1,0:T(8,128)}, f32[104,384]{1,0:T(8,128)}, u32[]{:S(2)}, u32[]{:S(2)}) collective-permute-start(f32[104,384]{1,0:T(8,128)} %get-tuple-element.48), channel_id=1, source_target_pairs={{0,4},{4,0},{8,12},{12,8},{1,5},{5,1},{9,13},{13,9},{2,6},{6,2},{1... | collective-permute-start | bytes 479240 | tf_op jit(solution)/shard_map/ppermute | solution.py:693
  88.4 14.3 %collective-permute-start.11 = (f32[104,384]{1,0:T(8,128)}, f32[104,384]{1,0:T(8,128)}, u32[]{:S(2)}, u32[]{:S(2)}) collective-permute-start(f32[104,384]{1,0:T(8,128)} %get-tuple-element.49), channel_id=1, source_target_pairs={{0,8},{4,12},{8,0},{12,4},{1,9},{5,13},{9,1},{13,5},{2,10},{6,14},... | collective-permute-start | bytes 479240 | tf_op jit(solution)/shard_map/ppermute | solution.py:693
  89.0 13.7 %collective-permute-start.12 = (f32[104,384]{1,0:T(8,128)}, f32[104,384]{1,0:T(8,128)}, u32[]{:S(2)}, u32[]{:S(2)}) collective-permute-start(f32[104,384]{1,0:T(8,128)} %get-tuple-element.50), channel_id=1, source_target_pairs={{0,12},{4,8},{8,4},{12,0},{1,13},{5,9},{9,5},{13,1},{2,14},{6,10},... | collective-permute-start | bytes 479240 | tf_op jit(solution)/shard_map/ppermute | solution.py:693
  103.9 15.9 %collective-permute-start.13 = (f32[104,384]{1,0:T(8,128)S(1)}, f32[104,384]{1,0:T(8,128)}, u32[]{:S(2)}, u32[]{:S(2)}) collective-permute-start(f32[104,384]{1,0:T(8,128)S(1)} %add_add_fusion.1.refs_1_.refs_3_), channel_id=1, source_target_pairs={{0,15},{1,14},{2,13},{3,12},{4,11},{5,10},{6,9},{7,8},{8,7},{9,6},... | collective-permute-start | bytes 479240 | tf_op jit(solution)/shard_map/ppermute | solution.py:697
  107.8 21.7 %collective-permute-start.9 = (f32[80,384]{1,0:T(8,128)}, f32[80,384]{1,0:T(8,128)}, u32[]{:S(2)}, u32[]{:S(2)}) collective-permute-start(f32[80,384]{1,0:T(8,128)} %add.89.refs_0_.refs_1_), channel_id=1, source_target_pairs={{0,4},{4,0},{8,12},{12,8},{1,5},{5,1},{9,13},{13,9},{2,6},{6,2},{1... | collective-permute-start | bytes 368648 | tf_op jit(solution)/shard_map/ppermute | solution.py:693
  131.7 26.8 %collective-permute-start.16 = (f32[1,2,80,640]{3,2,1,0:T(8,128)}, f32[1,2,80,640]{3,2,1,0:T(8,128)}, u32[]{:S(2)}, u32[]{:S(2)}) collective-permute-start(f32[1,2,80,640]{3,2,1,0:T(8,128)} %join.4.refs_1_), channel_id=1, source_target_pairs={{0,2},{1,3},{2,0},{3,1},{4,6},{5,7},{6,4},{7,5},{8,10},{9,11},{10,... | collective-permute-start | bytes 1228808 | tf_op jit(solution)/shard_map/ppermute | solution.py:693
  141.2 15.0 %collective-permute-start.19 = (f32[104,384]{1,0:T(8,128)}, f32[104,384]{1,0:T(8,128)}, u32[]{:S(2)}, u32[]{:S(2)}) collective-permute-start(f32[104,384]{1,0:T(8,128)} %tie.22.refs_1_), channel_id=1, source_target_pairs={{0,8},{4,12},{8,0},{12,4},{1,9},{5,13},{9,1},{13,5},{2,10},{6,14},... | collective-permute-start | bytes 479240 | tf_op jit(solution)/shard_map/ppermute | solution.py:693
  142.9 13.3 %collective-permute-start.20 = (f32[104,384]{1,0:T(8,128)}, f32[104,384]{1,0:T(8,128)}, u32[]{:S(2)}, u32[]{:S(2)}) collective-permute-start(f32[104,384]{1,0:T(8,128)} %tie.22.refs_1_), channel_id=1, source_target_pairs={{0,12},{4,8},{8,4},{12,0},{1,13},{5,9},{9,5},{13,1},{2,14},{6,10},... | collective-permute-start | bytes 479240 | tf_op jit(solution)/shard_map/ppermute | solution.py:693
  158.5 13.5 %collective-permute-start.21 = (f32[1,2,104,640]{3,2,1,0:T(8,128)}, f32[1,2,104,640]{3,2,1,0:T(8,128)S(1)}, u32[]{:S(2)}, u32[]{:S(2)}) collective-permute-start(f32[1,2,104,640]{3,2,1,0:T(8,128)} %tie.23), channel_id=1, source_target_pairs={{0,2},{1,3},{2,0},{3,1},{4,6},{5,7},{6,4},{7,5},{8,10},{9,11},{10,... | collective-permute-start | bytes 1597448 | tf_op jit(solution)/shard_map/ppermute | solution.py:693
  233.6 29.0 %collective-permute-start.26 = (f32[1,2,80,640]{3,2,1,0:T(8,128)}, f32[1,2,80,640]{3,2,1,0:T(8,128)}, u32[]{:S(2)}, u32[]{:S(2)}) collective-permute-start(f32[1,2,80,640]{3,2,1,0:T(8,128)} %send.7.refs_0_), channel_id=1, source_target_pairs={{0,2},{1,3},{2,0},{3,1},{4,6},{5,7},{6,4},{7,5},{8,10},{9,11},{10,... | collective-permute-start | bytes 1228808 | tf_op jit(solution)/shard_map/ppermute | solution.py:693
  262.6 21.7 %collective-permute-start.27 = (f32[1,2,104,640]{3,2,1,0:T(8,128)}, f32[1,2,104,640]{3,2,1,0:T(8,128)}, u32[]{:S(2)}, u32[]{:S(2)}) collective-permute-start(f32[1,2,104,640]{3,2,1,0:T(8,128)} %tie.25), channel_id=1, source_target_pairs={{0,2},{1,3},{2,0},{3,1},{4,6},{5,7},{6,4},{7,5},{8,10},{9,11},{10,... | collective-permute-start | bytes 1597448 | tf_op jit(solution)/shard_map/ppermute | solution.py:693
  287.5 12.9 %collective-permute-start.34 = (f32[104,384]{1,0:T(8,128)}, f32[104,384]{1,0:T(8,128)}, u32[]{:S(2)}, u32[]{:S(2)}) collective-permute-start(f32[104,384]{1,0:T(8,128)} %get-tuple-element.66), channel_id=1, source_target_pairs={{0,4},{4,0},{8,12},{12,8},{1,5},{5,1},{9,13},{13,9},{2,6},{6,2},{1... | collective-permute-start | bytes 479240 | tf_op jit(solution)/shard_map/ppermute | solution.py:693
  289.9 15.1 %collective-permute-start.35 = (f32[104,384]{1,0:T(8,128)}, f32[104,384]{1,0:T(8,128)}, u32[]{:S(2)}, u32[]{:S(2)}) collective-permute-start(f32[104,384]{1,0:T(8,128)} %get-tuple-element.67), channel_id=1, source_target_pairs={{0,8},{4,12},{8,0},{12,4},{1,9},{5,13},{9,1},{13,5},{2,10},{6,14},... | collective-permute-start | bytes 479240 | tf_op jit(solution)/shard_map/ppermute | solution.py:693
  290.1 14.8 %collective-permute-start.36 = (f32[104,384]{1,0:T(8,128)}, f32[104,384]{1,0:T(8,128)}, u32[]{:S(2)}, u32[]{:S(2)}) collective-permute-start(f32[104,384]{1,0:T(8,128)} %get-tuple-element.68), channel_id=1, source_target_pairs={{0,12},{4,8},{8,4},{12,0},{1,13},{5,9},{9,5},{13,1},{2,14},{6,10},... | collective-permute-start | bytes 479240 | tf_op jit(solution)/shard_map/ppermute | solution.py:693
  306.1 20.8 %collective-permute-start.37 = (f32[104,384]{1,0:T(8,128)S(1)}, f32[104,384]{1,0:T(8,128)}, u32[]{:S(2)}, u32[]{:S(2)}) collective-permute-start(f32[104,384]{1,0:T(8,128)S(1)} %add_add_fusion.refs_1_.refs_7_), channel_id=1, source_target_pairs={{0,15},{1,14},{2,13},{3,12},{4,11},{5,10},{6,9},{7,8},{8,7},{9,6},... | collective-permute-start | bytes 479240 | tf_op jit(solution)/shard_map/ppermute | solution.py:697
  317.1 20.6 %collective-permute-start.33 = (f32[80,384]{1,0:T(8,128)}, f32[80,384]{1,0:T(8,128)}, u32[]{:S(2)}, u32[]{:S(2)}) collective-permute-start(f32[80,384]{1,0:T(8,128)} %add.97.refs_0_.refs_1_), channel_id=1, source_target_pairs={{0,4},{4,0},{8,12},{12,8},{1,5},{5,1},{9,13},{13,9},{2,6},{6,2},{1... | collective-permute-start | bytes 368648 | tf_op jit(solution)/shard_map/ppermute | solution.py:693
  324.1 13.6 %collective-permute-start.38 = (f32[80,384]{1,0:T(8,128)}, f32[80,384]{1,0:T(8,128)}, u32[]{:S(2)}, u32[]{:S(2)}) collective-permute-start(f32[80,384]{1,0:T(8,128)} %add.97.refs_0_.refs_1_), channel_id=1, source_target_pairs={{0,8},{4,12},{8,0},{12,4},{1,9},{5,13},{9,1},{13,5},{2,10},{6,14},... | collective-permute-start | bytes 368648 | tf_op jit(solution)/shard_map/ppermute | solution.py:693
  339.8 25.9 %collective-permute-start.40 = (f32[1,2,80,640]{3,2,1,0:T(8,128)}, f32[1,2,80,640]{3,2,1,0:T(8,128)}, u32[]{:S(2)}, u32[]{:S(2)}) collective-permute-start(f32[1,2,80,640]{3,2,1,0:T(8,128)} %join.6.refs_0_.refs_1_), channel_id=1, source_target_pairs={{0,2},{1,3},{2,0},{3,1},{4,6},{5,7},{6,4},{7,5},{8,10},{9,11},{10,... | collective-permute-start | bytes 1228808 | tf_op jit(solution)/shard_map/ppermute | solution.py:693
  346.3 13.2 %collective-permute-start.42 = (f32[104,384]{1,0:T(8,128)}, f32[104,384]{1,0:T(8,128)}, u32[]{:S(2)}, u32[]{:S(2)}) collective-permute-start(f32[104,384]{1,0:T(8,128)} %tie.30.refs_1_), channel_id=1, source_target_pairs={{0,4},{4,0},{8,12},{12,8},{1,5},{5,1},{9,13},{13,9},{2,6},{6,2},{1... | collective-permute-start | bytes 479240 | tf_op jit(solution)/shard_map/ppermute | solution.py:693
  348.4 15.1 %collective-permute-start.43 = (f32[104,384]{1,0:T(8,128)}, f32[104,384]{1,0:T(8,128)}, u32[]{:S(2)}, u32[]{:S(2)}) collective-permute-start(f32[104,384]{1,0:T(8,128)} %tie.30.refs_1_), channel_id=1, source_target_pairs={{0,8},{4,12},{8,0},{12,4},{1,9},{5,13},{9,1},{13,5},{2,10},{6,14},... | collective-permute-start | bytes 479240 | tf_op jit(solution)/shard_map/ppermute | solution.py:693
  349.7 13.7 %collective-permute-start.44 = (f32[104,384]{1,0:T(8,128)}, f32[104,384]{1,0:T(8,128)}, u32[]{:S(2)}, u32[]{:S(2)}) collective-permute-start(f32[104,384]{1,0:T(8,128)} %tie.30.refs_1_), channel_id=1, source_target_pairs={{0,12},{4,8},{8,4},{12,0},{1,13},{5,9},{9,5},{13,1},{2,14},{6,10},... | collective-permute-start | bytes 479240 | tf_op jit(solution)/shard_map/ppermute | solution.py:693
  (42 other events, 275.7 us)

commit v3 on v2

--- a/solution.py
+++ b/solution.py
@@ -45,7 +45,7 @@
         self.rows = self.cc * wk
         self.tall = round_up(self.rows, 16)
         self.bb = math.gcd(2, wb)
-        self.lb = math.gcd(4, nx)
+        self.lb = math.gcd(4, nx // 2)
         self.batch = max(d for d in range(1, 6) if self.cc % d == 0)
         self.full_x, self.full_y = nx * slab_count, ny * chan_count
 
@@ -368,11 +368,11 @@
         output_ref[x, :, t, :] = mixed[:, n * plan.nz : (n + 1) * plan.nz].reshape(plan.c, 8, plan.nz)
 
 
-def pick(plan, parts, chosen_ref, ordered_ref):
+def pick(plan, upper_ref, parts, chosen_ref, ordered_ref):
     @pl.when(pl.program_id(0) == 0)
     def _():
         for n in range(2):
-            found = [moved(part[n][...], part[2][...], left=True) for part in parts]
+            found = [moved(part[n][...], part[2][upper_ref[0]], left=True) for part in parts]
             high, low = split(sum(found[1:], found[0]))
             ordered_ref[: plan.rows, n * plan.ll : (n + 1) * plan.ll] = high
             ordered_ref[plan.tall : plan.tall + plan.rows, n * plan.ll : (n + 1) * plan.ll] = low
@@ -381,7 +381,7 @@
     return [b[: plan.rows] + b[plan.tall : plan.tall + plan.rows] for b in both]
 
 
-def give(plan, made_ref, order_ref, back_ref, own_ref, mirror_ref, sums_ref):
+def give(plan, upper_ref, made_ref, order_ref, back_ref, own_ref, mirror_ref, sums_ref):
     part = moved(made_ref[0], back_ref[0])
     for n in range(1, plan.bb):
         part = part + moved(made_ref[n], back_ref[n])
@@ -397,16 +397,16 @@
 
     @pl.when(step == pl.num_programs(0) - 1)
     def _():
-        own_ref[...] = moved(sums_ref[:, : plan.ll], order_ref[...], left=True)
-        mirror_ref[...] = moved(sums_ref[:, plan.ll :], order_ref[...], left=True)
+        own_ref[...] = moved(sums_ref[:, : plan.ll], order_ref[upper_ref[0]], left=True)
+        mirror_ref[...] = moved(sums_ref[:, plan.ll :], order_ref[upper_ref[0]], left=True)
 
 
 def mix_kernel(
-    plan, own_ref, mirror_ref, order_ref, disorder_ref, chosen_ref, back_ref, weight_ref,
+    plan, upper_ref, own_ref, mirror_ref, order_ref, disorder_ref, chosen_ref, back_ref, weight_ref,
     own_out, mirror_out, ordered_ref, made_ref, sums_ref,
 ):
     wk, quarters = plan.wk, 128 // plan.mx
-    picked = pick(plan, [(own_ref, mirror_ref, order_ref)], chosen_ref, ordered_ref)
+    picked = pick(plan, upper_ref, [(own_ref, mirror_ref, order_ref)], chosen_ref, ordered_ref)
     place = lax.broadcasted_iota(jnp.int32, (wk, 128), 1) // plan.mx
     for n, modes in enumerate(picked):
         for t in range(plan.c // quarters):
@@ -421,7 +421,7 @@
                 o = t * quarters + q
                 made_ref[n, o * wk : (o + 1) * wk, :128] = jnp.where(place == q, real, 0.0)
                 made_ref[n, o * wk : (o + 1) * wk, 128:] = jnp.where(place == q, imag, 0.0)
-    give(plan, made_ref, disorder_ref, back_ref, own_out, mirror_out, sums_ref)
+    give(plan, upper_ref, made_ref, disorder_ref, back_ref, own_out, mirror_out, sums_ref)
 
 
 def along(plan, modes):
@@ -439,11 +439,11 @@
 
 
 def mix_back_kernel(
-    plan, own_ref, mirror_ref, order_ref, disorder_ref, chosen_ref, back_ref, weight_ref,
+    plan, upper_ref, own_ref, mirror_ref, order_ref, disorder_ref, chosen_ref, back_ref, weight_ref,
     own_out, mirror_out, ordered_ref, made_ref, sums_ref,
 ):
     wk = plan.wk
-    for n, grads in enumerate(pick(plan, [(own_ref, mirror_ref, order_ref)], chosen_ref, ordered_ref)):
+    for n, grads in enumerate(pick(plan, upper_ref, [(own_ref, mirror_ref, order_ref)], chosen_ref, ordered_ref)):
         lined = along(plan, grads)
         for i in range(plan.c):
             back_real = back_imag = 0.0
@@ -453,15 +453,15 @@
                 back_imag = back_imag + (w_real * imag - w_imag * real)
             made_ref[n, i * wk : (i + 1) * wk, :128] = back_real
             made_ref[n, i * wk : (i + 1) * wk, 128:] = back_imag
-    give(plan, made_ref, disorder_ref, back_ref, own_out, mirror_out, sums_ref)
-
-
-def outer_kernel(plan, *refs):
+    give(plan, upper_ref, made_ref, disorder_ref, back_ref, own_out, mirror_out, sums_ref)
+
+
+def outer_kernel(plan, upper_ref, *refs):
     parts = [refs[:8][2 * m : 2 * m + 2] for m in range(4)]
     orders, chosen_ref, gradient_ref, mode_rows, grad_rows = refs[8:10], refs[10], refs[11], refs[12], refs[13]
     wk = plan.wk
-    modes = pick(plan, [(*parts[m], orders[m]) for m in range(2)], chosen_ref, mode_rows)
-    grads = pick(plan, [(*parts[2 + m], orders[m]) for m in range(2)], chosen_ref, grad_rows)
+    modes = pick(plan, upper_ref, [(*parts[m], orders[m]) for m in range(2)], chosen_ref, mode_rows)
+    grads = pick(plan, upper_ref, [(*parts[2 + m], orders[m]) for m in range(2)], chosen_ref, grad_rows)
     for n in range(plan.bb):
         lined = along(plan, grads[n])
         for i in range(plan.c):
@@ -479,10 +479,6 @@
         high = keep_ref[2 * pair + 1] + arrived_ref[2 * pair + 1]
         kept_ref[pair] = jnp.where(odd, high, low)
         send_ref[pair] = jnp.where(odd, low, high)
-
-
-def send_kernel(place_ref, keep_ref, arrived_ref, send_ref):
-    send_ref[...] = keep_ref[...] + arrived_ref[...]
 
 
 def cut_kernel(plan, place_ref, keep_ref, arrived_ref, came_ref, *refs):
@@ -586,11 +582,10 @@
         )
         self.slab_index = slab.astype(jnp.int32).reshape(1)
         self.flag = (chan % 2).astype(jnp.int32).reshape(1)
-        upper = (chan >= plan.half).astype(jnp.int32)
+        self.upper = (chan >= plan.half).astype(jnp.int32).reshape(1)
         tables = [plan.orders(m) for m in range(plan.chunks)]
-        self.order = [lax.dynamic_index_in_dim(jnp.asarray(t), upper, 0, False) for t in tables]
-        tables = [np.ascontiguousarray(np.swapaxes(t, 1, 2)) for t in tables]
-        self.disorder = [lax.dynamic_index_in_dim(jnp.asarray(t), upper, 0, False) for t in tables]
+        self.order = [jnp.asarray(t) for t in tables]
+        self.disorder = [jnp.asarray(np.ascontiguousarray(np.swapaxes(t, 1, 2))) for t in tables]
         chosen, back = plan.selections()
         self.chosen, self.back = jnp.asarray(chosen), jnp.asarray(back)
 
@@ -650,15 +645,15 @@
             [self.lines(), *self.spectra()], 20, before,
         )(self.flag, *owns, *others, linear, self.plane, self.inverse, self.turn)
 
-    def linear(self, before, values, matrix, bias):
+    def linear(self, half, before, filled, values, matrix, bias):
         plan = self.plan
         bias = bias[None]
-        spec = leading((plan.lb, plan.c, plan.ny, plan.nz))
+        steps = plan.nx // plan.lb // 2
+        spec = pl.BlockSpec((plan.lb, plan.c, plan.ny, plan.nz), lambda i: (i + half * steps, 0, 0, 0))
         return call(
-            partial(linear_kernel, plan), "linear", plan.nx // plan.lb,
+            partial(linear_kernel, plan), "linear", steps,
             [spec, whole(matrix), whole(bias)],
-            spec, shaped(plan.nx, plan.c, plan.ny, plan.nz), [],
-            12, before,
+            spec, shaped(plan.nx, plan.c, plan.ny, plan.nz), [], 7, (*filled, *before), {0: 0} if filled else None,
         )(values, matrix, bias)
 
     def mix(self, kernel, name, chunk, before, own, mirror, weights):
@@ -669,13 +664,13 @@
         return call(
             partial(kernel, plan), name, plan.wb // plan.bb,
             [
-                whole_shape(modes), whole_shape(modes), whole(order), whole(disorder),
+                scalar(), whole_shape(modes), whole_shape(modes), whole(order), whole(disorder),
                 leading((plan.bb,) + self.chosen.shape[1:]), leading((plan.bb,) + self.back.shape[1:]),
                 leading((plan.bb, *weights.shape[1:])),
             ],
             [whole_shape(modes)] * 2, [shaped(*modes)] * 2,
             [ordered, pltpu.VMEM((plan.bb, plan.rows, 256), f32), pltpu.VMEM((plan.rows, 2 * plan.ll), f32)], 9, before,
-        )(own, mirror, order, disorder, self.chosen, self.back, weights)
+        )(self.upper, own, mirror, order, disorder, self.chosen, self.back, weights)
 
     def outer(self, before, modes, grads, weights):
         plan = self.plan
@@ -684,9 +679,9 @@
         out = leading((plan.bb, *weights.shape[1:]))
         return call(
             partial(outer_kernel, plan), "outer", plan.wb // plan.bb,
-            [*[whole(p) for p in parts], *[whole(o) for o in self.order], leading((plan.bb,) + self.chosen.shape[1:])],
+            [scalar(), *[whole(p) for p in parts], *[whole(o) for o in self.order], leading((plan.bb,) + self.chosen.shape[1:])],
             out, shaped(*weights.shape), [ordered, ordered], 9, before,
-        )(*parts, *self.order, self.chosen)
+        )(self.upper, *parts, *self.order, self.chosen)
 
     def across(self, value, axis, bit):
         size = lax.axis_size(axis)
@@ -710,12 +705,8 @@
         )(place, *arrays)
 
     def sent_half(self, keep, arrived):
-        block = (1, 1) + keep.shape[2:]
-        spec = pl.BlockSpec(block, lambda r, place: (1 - place[1], r, 0, 0))
-        return self.chosen_half(
-            send_kernel, "send", (2,), [spec, spec], pl.BlockSpec(block, lambda r, place: (0, r, 0, 0)),
-            shaped(1, *keep.shape[1:]), [], (keep, arrived),
-        )
+        other = 1 - self.chan // (self.plan.ch // 2)
+        return lax.dynamic_index_in_dim(keep, other, 0) + lax.dynamic_index_in_dim(arrived, other, 0)
 
     def halve(self, keep, arrived, bit):
         mine = ((self.chan // bit) % 2).astype(jnp.int32).reshape(1)
@@ -754,17 +745,20 @@
             whole_shape(total), shaped(*total), [pltpu.VMEM((plan.s, *mine.shape), f32)], 2,
         )(self.slab_index, mine, *arrived)
 
-    def exchange(self, keeps, sends, linear, mix, outer=None):
+    def exchange(self, keeps, sends, mix, fillers):
+        def fill(n, value, *before):
+            return tie(value, fillers[n](before)) if fillers[n] else value
+
         plan = self.plan
         first = [self.across(send, "chan", 1) for send in sends]
         keep0, sent0, came0 = self.sums_over_chan(keeps[0], first[0], [])
-        extra = linear([sent0, first[1]])
-        came0 = tie(came0, extra)
+        came0 = fill(0, came0, sent0, first[1])
         keep1, sent1, came1 = self.sums_over_chan(keeps[1], first[1], [came0])
 
         mine, pieces = self.cut(keep0, came0)
-        for j, piece in enumerate(pieces):
-            mine = mine + self.across(piece, "slab", j + 1)
+        arrived = [self.across(piece, "slab", j + 1) for j, piece in enumerate(pieces)]
+        for piece in [fill(1, arrived[0], mine, sent1)] + arrived[1:]:
+            mine = mine + piece
         own0 = mine
         mirror0 = self.mirrored(own0)
         mine, pieces = self.cut(keep1, tie(came1, own0))
@@ -783,15 +777,12 @@
         came0 = self.across(total0, "chan", plan.ch // 2)
         full1 = tie(full1, total0)
         arrived = [self.across(full1, "slab", j) for j in range(1, plan.s)]
-        made = None
-        if outer is not None:
-            made = outer([total0], ((own0, mirror0), (own1, mirror1)))
-            came0 = tie(came0, made)
+        modes = ((own0, mirror0), (own1, mirror1))
+        if fillers[2]:
+            came0 = tie(came0, fillers[2]([total0], modes))
         total1 = tie(self.join(full1, arrived), came0)
         came1 = self.across(total1, "chan", plan.ch // 2)
-        if outer is not None:
-            made = tie(jnp.transpose(made, (0, 3, 2, 1, 4)), total1)
-            came1 = tie(came1, made)
+        came1 = fill(3, came1, total1)
 
         owns, others = [], []
         for total, other in ((total0, came0), (total1, came1)):
@@ -804,7 +795,7 @@
                 other = self.across(total, "chan", bit)
             owns.append(total)
             others.append(other)
-        return owns, others, extra, made, ((own0, mirror0), (own1, mirror1))
+        return owns, others, modes
 
 
 def local(inputs, cotangent, spectral, local_weight, bias_vector):
@@ -816,20 +807,42 @@
     slopes = jnp.transpose(cotangent, (0, 2, 1, 3))
     weights = jnp.transpose(spectral, (0, 2, 3, 1, 4))
 
+    held = {}
+
+    def relaid(before):
+        held["weights"] = tie(weights, *before)
+        return held["weights"]
+
+    def linear(half, name, values, matrix, bias):
+        def run(before):
+            filled = [held[name]] if half else []
+            held[name] = program.linear(half, before, filled, values, matrix, bias)
+            return held[name]
+
+        return run
+
+    def mix(kernel, name):
+        return lambda m, before, own, mirror: program.mix(kernel, name, m, before, own, mirror, held["weights"])
+
     keeps, sends = program.analyse(values)
-    owns, others, linear, _, modes = program.exchange(
-        keeps, sends,
-        lambda before: program.linear(before, values, local_weight.T, bias_vector),
-        lambda m, before, own, mirror: program.mix(mix_kernel, "mix", m, before, own, mirror, weights),
+    there = [linear(half, "linear", values, local_weight.T, bias_vector) for half in range(2)]
+    owns, others, modes = program.exchange(keeps, sends, mix(mix_kernel, "mix"), (relaid, there[0], None, there[1]))
+    output, gradient, keeps, sends = program.middle(owns, others, held["linear"], slopes)
+
+    def outer(before, grads):
+        held["outer"] = program.outer(before, modes, grads, weights)
+        return held["outer"]
+
+    def placed(before):
+        held["outer"] = tie(jnp.transpose(held["outer"], (0, 3, 2, 1, 4)), *before)
+        return held["outer"]
+
+    back = [linear(half, "back", gradient, local_weight, jnp.zeros_like(bias_vector)) for half in range(2)]
+    owns, others, _ = program.exchange(
+        keeps, sends, mix(mix_back_kernel, "mix_back"), (back[0], back[1], outer, placed)
     )
-    output, gradient, keeps, sends = program.middle(owns, others, linear, slopes)
-    owns, others, linear, grad_spectral, _ = program.exchange(
-        keeps, sends,
-        lambda before: program.linear(before, gradient, local_weight, jnp.zeros_like(bias_vector)),
-        lambda m, before, own, mirror: program.mix(mix_back_kernel, "mix_back", m, before, own, mirror, weights),
-        lambda before, grads: program.outer(before, modes, grads, weights),
-    )
-    grad_inputs = program.synthesise([], owns, others, linear)
+    grad_inputs = program.synthesise([], owns, others, held["back"])
+    grad_spectral = held["outer"]
     return (
         jnp.transpose(output, (0, 2, 1, 3)),
         jnp.transpose(grad_inputs, (0, 2, 1, 3)),

time: 411 us -> 400 us (0.973)
  waiting for transfers between devices: 72.9 us -> 63.9 us
  other arithmetic: 15.4 us -> 22.5 us
  Pallas kernels: 207 us -> 200 us
    pallas_call x8 -> x4, Pallas kernels: 33.9 us -> 12.4 us  [chosen_half(): pl.pallas_call(kernel, grid_spec=pltpu.PrefetchScalarGridSpec(num_scalar_...]
    ppermute x40, waiting for transfers between devices: 59.7 us -> 41.1 us  [across(): return lax.ppermute(value, axis, [(i, i ^ bit) for i in range(size)])]
    pallas_call x7 -> x9, Pallas kernels: 70.1 us -> 85.2 us  [the longest x4 43.3 us: linear(): call(partial(linear_kernel, plan), 'linear', steps, [spec, whole(matrix),...]
    ppermute x8, waiting for transfers between devices: 13.3 us -> 22.8 us  [mirrored(): lax.ppermute(value, ('slab', 'chan'), [(i, total - 1 - i) for i in range(...]
    ppermute x40, starting transfers between devices: 64.8 us -> 55.9 us  [across(): return lax.ppermute(value, axis, [(i, i ^ bit) for i in range(size)])]
    ppermute x8, starting transfers between devices: 13.4 us -> 18.8 us  [mirrored(): lax.ppermute(value, ('slab', 'chan'), [(i, total - 1 - i) for i in range(...]
    unnamed x38 -> x56, local copies, waits for them, and re-layouts: 14.9 us -> 19.3 us
  transfers between devices with their start and end apart: 48 -> 48, of which waited for: 17 -> 17; matrix products, arithmetic and copies ran while one was open for 9% -> 9% of each run, Pallas kernels for 22% -> 25%
where the time goes in v3:
time: 400 us; the launch traced here: 394 us
  Pallas kernels  200 us (50%)
  starting transfers between devices  74.7 us (19%)
  waiting for transfers between devices  63.9 us (16%)
  local copies, waits for them, and re-layouts  31.9 us (8%)
  other arithmetic  22.5 us (6%)
    ppermute x40, starting transfers between devices, across(): return lax.ppermute(value, axis, [(i, i ^ bit) for i in range(size)])  55.9 us
    pallas_call x1, Pallas kernels, middle(): call(partial(middle_kernel, plan), 'middle', plan.nx // plan.xb, [scalar(...  47.1 us
    pallas_call x4, Pallas kernels, linear(): call(partial(linear_kernel, plan), 'linear', steps, [spec, whole(matrix),...  43.3 us
    ppermute x40, waiting for transfers between devices, across(): return lax.ppermute(value, axis, [(i, i ^ bit) for i in range(size)])  41.1 us
    pallas_call x4, Pallas kernels, mix(): call(partial(kernel, plan), name, plan.wb // plan.bb, [scalar(), whole_sh...  33.5 us
    pallas_call x1, Pallas kernels, analyse(): call(partial(analyse_kernel, plan), 'analyse', plan.nx // plan.xb, [scala...  27.1 us
    ppermute x8, waiting for transfers between devices, mirrored(): lax.ppermute(value, ('slab', 'chan'), [(i, total - 1 - i) for i in range(...  22.8 us
    pallas_call x1, Pallas kernels, synthesise(): call(partial(synthesise_kernel, plan), 'synthesise', plan.nx // plan.xb,...  19.8 us
  transfers between devices with their start and end apart: 48, of which 17 were waited for; matrix products, arithmetic and copies ran while one was open for 9% of the time, Pallas kernels for 25%

profile of v3, /device:TPU:0, one launch (start us, length us, event | category | flops | bytes accessed | tf_op | source)
XLA Modules:
  0.0 394.4 jit_solution(13738728032282119530)
XLA Ops:
  1.9 27.1 %analyse.1 = (f32[2,2,80,640]{3,2,1,0:T(8,128)}, f32[2,2,104,640]{3,2,1,0:T(8,128)}, f32[2,2,80,640]{3,2,1,0:T(8,128)}, f32[2,2,104,640]{3,2,1,0:T(8,128)}) custom-call(s32[1]{0:T(128)} %bitcast.refs_0_, f32[32,20,32,128]{3,2,1,0:T(8,128)} %bitcast.46, bf16[4,768,1280]{2,1,0:T(8,128)(2,1)} %constant.137.clone.refs_2_.refs_7_.refs_6_, ...), custom_call_target="tpu_custom_call" | custom-call | flops 29899999232 | bytes 93600000 | tf_op jit(solution)/shard_map/analyse/pallas_call | solution.py:616
  37.2 6.8 %copy.47 = f32[8,8,2,20,640]{4,1,3,2,0:T(8,128)} copy(f32[8,8,2,20,640]{4,2,3,1,0:T(2,128)} %param.17) | data formatting | bytes 13107200 | tf_op args[2]
  57.2 7.9 %linear.4.refs_1_.refs_0_ = f32[32,20,32,128]{3,2,1,0:T(8,128)} custom-call(f32[80,384]{1,0:T(8,128)} %get-tuple-element.41.refs_0_, f32[1,2,104,640]{3,2,1,0:T(8,128)} %tie.23.refs_1_, f32[32,20,32,128]{3,2,1,0:T(8,128)} %bitcast.47, f32[20,20]{1,0:T(8,128)} %bitcast.49, f32[1,20]{1,0:T(1,128)} %bitcast.51), custom_call_target="tpu_custom_call" | custom-call | flops 8049999872 | bytes 25200000 | tf_op jit(solution)/shard_map/linear/pallas_call | solution.py:653
  78.5 8.4 %mix.2 = (f32[80,384]{1,0:T(8,128)}, f32[80,384]{1,0:T(8,128)}) custom-call(f32[104,384]{1,0:T(8,128)} %get-tuple-element.45.refs_0_, s32[1]{0:T(128)} %bitcast.8.refs_1_, f32[80,384]{1,0:T(8,128)} %add_add_fusion.3.refs_1_.refs_2_, f32[80,384]{1,0:T(8,128)} %collective-permute-done.7.refs_3_, bf16[2,160,80]{2,1,0:T(8,128)(2,1)} %constant.141.clone.refs_4_.refs_10_, ...), custom_call_target="tpu_custom_call" | custom-call | flops 10350000128 | bytes 32400000 | tf_op jit(solution)/shard_map/mix/pallas_call | solution.py:664
  95.4 7.1 %collective-permute-done.8 = f32[80,384]{1,0:T(8,128)S(1)} collective-permute-done((f32[80,384]{1,0:T(8,128)S(1)}, f32[80,384]{1,0:T(8,128)S(1)}, u32[]{:S(2)}, u32[]{:S(2)}) %collective-permute-start.8) | collective-permute-done | bytes 122912 | tf_op jit(solution)/shard_map/ppermute | solution.py:692
  104.8 9.2 %collective-permute-start.14 = (f32[80,384]{1,0:T(8,128)}, f32[80,384]{1,0:T(8,128)}, u32[]{:S(2)}, u32[]{:S(2)}) collective-permute-start(f32[80,384]{1,0:T(8,128)} %add.106.refs_0_.refs_1_), channel_id=1, source_target_pairs={{0,8},{4,12},{8,0},{12,4},{1,9},{5,13},{9,1},{13,5},{2,10},{6,14},... | collective-permute-start | bytes 368648 | tf_op jit(solution)/shard_map/ppermute | solution.py:688
  114.0 8.5 %mix.3 = (f32[104,384]{1,0:T(8,128)}, f32[104,384]{1,0:T(8,128)}) custom-call(f32[80,384]{1,0:T(8,128)} %add.106.refs_0_.refs_1_, s32[1]{0:T(128)} %bitcast.8.refs_1_, f32[104,384]{1,0:T(8,128)} %copy-done.18, f32[104,384]{1,0:T(8,128)} %collective-permute-done.13.refs_3_.refs_5_, bf16[2,160,104]{2,1,0:T(8,128)(2,1)} %constant.142.clone.refs_4_.refs_11_, ...), custom_call_target="tpu_custom_call" | custom-call | flops 10350000128 | bytes 32400000 | tf_op jit(solution)/shard_map/mix/pallas_call | solution.py:664
  126.7 5.1 %collective-permute-done.17 = f32[104,384]{1,0:T(8,128)} collective-permute-done((f32[104,384]{1,0:T(8,128)}, f32[104,384]{1,0:T(8,128)}, u32[]{:S(2)}, u32[]{:S(2)}) %collective-permute-start.17) | collective-permute-done | bytes 159776 | tf_op jit(solution)/shard_map/ppermute | solution.py:692
  142.8 8.9 %collective-permute-done.19.refs_3_ = f32[104,384]{1,0:T(8,128)} collective-permute-done((f32[104,384]{1,0:T(8,128)}, f32[104,384]{1,0:T(8,128)}, u32[]{:S(2)}, u32[]{:S(2)}) %collective-permute-start.19) | collective-permute-done | bytes 159776 | tf_op jit(solution)/shard_map/ppermute | solution.py:688
  153.9 8.2 %linear.5.refs_1_.refs_5_ = f32[32,20,32,128]{3,2,1,0:T(8,128)} custom-call(f32[32,20,32,128]{3,2,1,0:T(8,128)} %linear.4.refs_1_.refs_0_, f32[1,2,104,640]{3,2,1,0:T(8,128)} %tie.29.refs_1_, f32[32,20,32,128]{3,2,1,0:T(8,128)} %bitcast.48, f32[20,20]{1,0:T(8,128)} %bitcast.50, f32[1,20]{1,0:T(1,128)} %bitcast.52), custom_call_target="tpu_custom_call", output_to_operand_aliasing={{}: (0, {})} | custom-call | flops 8049999872 | bytes 25200000 | tf_op jit(solution)/shard_map/linear/pallas_call | solution.py:653
  162.1 6.1 %collective-permute-done.21.refs_0_ = f32[1,2,104,640]{3,2,1,0:T(8,128)} collective-permute-done((f32[1,2,104,640]{3,2,1,0:T(8,128)}, f32[1,2,104,640]{3,2,1,0:T(8,128)}, u32[]{:S(2)}, u32[]{:S(2)}) %collective-permute-start.21) | collective-permute-done | bytes 532512 | tf_op jit(solution)/shard_map/ppermute | solution.py:688
  175.8 47.1 %middle.1 = (f32[32,20,32,128]{3,2,1,0:T(8,128)}, f32[32,20,32,128]{3,2,1,0:T(8,128)}, f32[2,2,80,640]{3,2,1,0:T(8,128)}, f32[2,2,104,640]{3,2,1,0:T(8,128)}, f3...) custom-call(s32[1]{0:T(128)} %bitcast.refs_0_, f32[2,2,80,640]{3,2,1,0:T(8,128)} %copy-done.10, ...), custom_call_target="tpu_custom_call" | custom-call | flops 54050000896 | bytes 169200000 | tf_op jit(solution)/shard_map/middle/pallas_call | solution.py:629
  230.6 7.9 %linear.6.refs_1_.refs_0_ = f32[32,20,32,128]{3,2,1,0:T(8,128)} custom-call(f32[1,2,80,640]{3,2,1,0:T(8,128)} %dynamic-slice_add_fusion.2.refs_0_, f32[2,2,104,640]{3,2,1,0:T(8,128)} %collective-permute-done.24.refs_1_.arrived_ref, f32[32,20,32,128]{3,2,1,0:T(8,128)} %get-tuple-element.58.refs_2_.refs_3_, f32[20,20]{1,0:T(8,128)} %refs_4_.5, ...), custom_call_target="tpu_custom_call" | custom-call | flops 8049999872 | bytes 25200000 | tf_op jit(solution)/shard_map/linear/pallas_call | solution.py:653
  249.8 19.3 %linear.7.refs_1_.refs_5_ = f32[32,20,32,128]{3,2,1,0:T(8,128)} custom-call(f32[32,20,32,128]{3,2,1,0:T(8,128)} %linear.6.refs_1_.refs_0_, f32[80,384]{1,0:T(8,128)} %get-tuple-element.59.refs_1_, f32[1,2,104,640]{3,2,1,0:T(8,128)} %tie.32.refs_2_, f32[32,20,32,128]{3,2,1,0:T(8,128)} %get-tuple-element.58.refs_2_.refs_3_, ...), custom_call_target="tpu_custom_call", output_to_operand_aliasing={{}: (0, {})} | custom-call | flops 8049999872 | bytes 25200000 | tf_op jit(solution)/shard_map/linear/pallas_call | solution.py:653
  279.3 8.3 %mix_back.2 = (f32[80,384]{1,0:T(8,128)}, f32[80,384]{1,0:T(8,128)}) custom-call(f32[104,384]{1,0:T(8,128)} %get-tuple-element.63.refs_0_, s32[1]{0:T(128)} %bitcast.8.refs_1_, f32[80,384]{1,0:T(8,128)} %add_add_fusion.2.refs_1_.refs_2_.refs_6_, f32[80,384]{1,0:T(8,128)} %collective-permute-done.31.refs_3_.refs_7_, ...), custom_call_target="tpu_custom_call" | custom-call | flops 10350000128 | bytes 32400000 | tf_op jit(solution)/shard_map/mix_back/pallas_call | solution.py:664
  289.1 5.4 %collective-permute-start.37 = (f32[104,384]{1,0:T(8,128)S(1)}, f32[104,384]{1,0:T(8,128)}, u32[]{:S(2)}, u32[]{:S(2)}) collective-permute-start(f32[104,384]{1,0:T(8,128)S(1)} %add_add_fusion.refs_2_.refs_8_), channel_id=1, source_target_pairs={{0,15},{1,14},{2,13},{3,12},{4,11},{5,10},{6,9},{7,8},{8,7},{9,6},... | collective-permute-start | bytes 479240 | tf_op jit(solution)/shard_map/ppermute | solution.py:692
  294.6 8.0 %collective-permute-done.32 = f32[80,384]{1,0:T(8,128)S(1)} collective-permute-done((f32[80,384]{1,0:T(8,128)S(1)}, f32[80,384]{1,0:T(8,128)S(1)}, u32[]{:S(2)}, u32[]{:S(2)}) %collective-permute-start.32) | collective-permute-done | bytes 122912 | tf_op jit(solution)/shard_map/ppermute | solution.py:692
  305.0 4.8 %collective-permute-start.38 = (f32[80,384]{1,0:T(8,128)}, f32[80,384]{1,0:T(8,128)}, u32[]{:S(2)}, u32[]{:S(2)}) collective-permute-start(f32[80,384]{1,0:T(8,128)} %add.116.refs_0_.refs_1_), channel_id=1, source_target_pairs={{0,8},{4,12},{8,0},{12,4},{1,9},{5,13},{9,1},{13,5},{2,10},{6,14},... | collective-permute-start | bytes 368648 | tf_op jit(solution)/shard_map/ppermute | solution.py:688
  309.8 8.4 %mix_back.3 = (f32[104,384]{1,0:T(8,128)}, f32[104,384]{1,0:T(8,128)}) custom-call(f32[80,384]{1,0:T(8,128)} %add.116.refs_0_.refs_1_, s32[1]{0:T(128)} %bitcast.8.refs_1_, f32[104,384]{1,0:T(8,128)} %copy-done.19, f32[104,384]{1,0:T(8,128)} %collective-permute-done.37.refs_3_.refs_9_, bf16[2,160,104]{2,1,0:T(8,128)(2,1)} %constant.142.clone.refs_4_.refs_11_, ...), custom_call_target="tpu_custom_call" | custom-call | flops 10350000128 | bytes 32400000 | tf_op jit(solution)/shard_map/mix_back/pallas_call | solution.py:664
  318.2 5.9 %collective-permute-start.41 = (f32[104,384]{1,0:T(8,128)}, f32[104,384]{1,0:T(8,128)}, u32[]{:S(2)}, u32[]{:S(2)}) collective-permute-start(f32[104,384]{1,0:T(8,128)} %get-tuple-element.69.refs_1_), channel_id=1, source_target_pairs={{0,15},{1,14},{2,13},{3,12},{4,11},{5,10},{6,9},{7,8},{8,7},{9,6},... | collective-permute-start | bytes 479240 | tf_op jit(solution)/shard_map/ppermute | solution.py:692
  336.2 8.3 %outer.1.refs_1_ = f32[8,2,20,8,640]{4,3,2,1,0:T(8,128)} custom-call(f32[1,2,80,640]{3,2,1,0:T(8,128)} %join.6.refs_0_.refs_1_, s32[1]{0:T(128)} %bitcast.8.refs_1_, f32[80,384]{1,0:T(8,128)} %add_add_fusion.3.refs_1_.refs_2_, f32[80,384]{1,0:T(8,128)} %collective-permute-done.7.refs_3_, f32[104,384]{1,0:T(8,128)} %copy-done.18, ...), custom_call_target="tpu_custom_call" | custom-call | flops 10350000128 | bytes 32400000 | tf_op jit(solution)/shard_map/outer/pallas_call | solution.py:680
  344.5 4.6 %collective-permute-done.43.refs_3_ = f32[104,384]{1,0:T(8,128)} collective-permute-done((f32[104,384]{1,0:T(8,128)}, f32[104,384]{1,0:T(8,128)}, u32[]{:S(2)}, u32[]{:S(2)}) %collective-permute-start.43) | collective-permute-done | bytes 159776 | tf_op jit(solution)/shard_map/ppermute | solution.py:688
  354.5 10.7 %copy.46 = f32[8,2,20,8,640]{4,1,2,3,0:T(2,128)} copy(f32[8,2,20,8,640]{4,3,2,1,0:T(8,128)} %outer.1.refs_1_) | data formatting | bytes 13107200 | tf_op jit(solution)/shard_map/outer/pallas_call | solution.py:680
  374.4 19.8 %synthesise.1 = f32[32,20,32,128]{3,2,1,0:T(8,128)} custom-call(s32[1]{0:T(128)} %bitcast.refs_0_, f32[2,2,80,640]{3,2,1,0:T(8,128)} %copy-done.11, f32[2,2,104,640]{3,2,1,0:T(8,128)} %copy-done.9, f32[2,2,80,640]{3,2,1,0:T(8,128)} %copy-done.24, f32[2,2,104,640]{3,2,1,0:T(8,128)} %collective-permute-done.47.refs_4_, ...), custom_call_target="tpu_custom_call" | custom-call | flops 23000000512 | bytes 72000000 | tf_op jit(solution)/shard_map/synthesise/pallas_call | solution.py:640
  (193 shorter events, 131.3 us)
Async XLA Ops:
  29.5 15.2 %collective-permute-start = (f32[2,2,104,640]{3,2,1,0:T(8,128)}, f32[2,2,104,640]{3,2,1,0:T(8,128)S(1)}, u32[]{:S(2)}, u32[]{:S(2)}) collective-permute-start(f32[2,2,104,640]{3,2,1,0:T(8,128)} %get-tuple-element.38), channel_id=1, source_target_pairs={{0,1},{1,0},{2,3},{3,2},{4,5},{5,4},{6,7},{7,6},{8,9},{9,8},{10,11... | collective-permute-start | bytes 3194888 | tf_op jit(solution)/shard_map/ppermute | solution.py:688
  33.6 15.2 %collective-permute-start.2 = (f32[1,2,80,640]{3,2,1,0:T(8,128)S(1)}, f32[1,2,80,640]{3,2,1,0:T(8,128)S(1)}, u32[]{:S(2)}, u32[]{:S(2)}) collective-permute-start(f32[1,2,80,640]{3,2,1,0:T(8,128)S(1)} %dynamic-slice_add_fusion.3.refs_1_), channel_id=1, source_target_pairs={{0,2},{1,3},{2,0},{3,1},{4,6},{5,7},{6,4},{7,5},{8,10},{9,11},{10,... | collective-permute-start | bytes 1228808 | tf_op jit(solution)/shard_map/ppermute | solution.py:688
  56.9 13.9 %collective-permute-start.3 = (f32[1,2,104,640]{3,2,1,0:T(8,128)}, f32[1,2,104,640]{3,2,1,0:T(8,128)}, u32[]{:S(2)}, u32[]{:S(2)}) collective-permute-start(f32[1,2,104,640]{3,2,1,0:T(8,128)} %tie.23.refs_1_), channel_id=1, source_target_pairs={{0,2},{1,3},{2,0},{3,1},{4,6},{5,7},{6,4},{7,5},{8,10},{9,11},{10,... | collective-permute-start | bytes 1597448 | tf_op jit(solution)/shard_map/ppermute | solution.py:688
  74.2 15.5 %collective-permute-start.11 = (f32[104,384]{1,0:T(8,128)}, f32[104,384]{1,0:T(8,128)}, u32[]{:S(2)}, u32[]{:S(2)}) collective-permute-start(f32[104,384]{1,0:T(8,128)} %get-tuple-element.49), channel_id=1, source_target_pairs={{0,8},{4,12},{8,0},{12,4},{1,9},{5,13},{9,1},{13,5},{2,10},{6,14},... | collective-permute-start | bytes 479240 | tf_op jit(solution)/shard_map/ppermute | solution.py:688
  90.8 23.2 %collective-permute-start.13 = (f32[104,384]{1,0:T(8,128)S(1)}, f32[104,384]{1,0:T(8,128)}, u32[]{:S(2)}, u32[]{:S(2)}) collective-permute-start(f32[104,384]{1,0:T(8,128)S(1)} %add_add_fusion.1.refs_2_.refs_4_), channel_id=1, source_target_pairs={{0,15},{1,14},{2,13},{3,12},{4,11},{5,10},{6,9},{7,8},{8,7},{9,6},... | collective-permute-start | bytes 479240 | tf_op jit(solution)/shard_map/ppermute | solution.py:692
  103.2 19.9 %collective-permute-start.15 = (f32[80,384]{1,0:T(8,128)}, f32[80,384]{1,0:T(8,128)}, u32[]{:S(2)}, u32[]{:S(2)}) collective-permute-start(f32[80,384]{1,0:T(8,128)} %add.106.refs_0_.refs_1_), channel_id=1, source_target_pairs={{0,12},{4,8},{8,4},{12,0},{1,13},{5,9},{9,5},{13,1},{2,14},{6,10},... | collective-permute-start | bytes 368648 | tf_op jit(solution)/shard_map/ppermute | solution.py:688
  104.8 18.2 %collective-permute-start.14 = (f32[80,384]{1,0:T(8,128)}, f32[80,384]{1,0:T(8,128)}, u32[]{:S(2)}, u32[]{:S(2)}) collective-permute-start(f32[80,384]{1,0:T(8,128)} %add.106.refs_0_.refs_1_), channel_id=1, source_target_pairs={{0,8},{4,12},{8,0},{12,4},{1,9},{5,13},{9,1},{13,5},{2,10},{6,14},... | collective-permute-start | bytes 368648 | tf_op jit(solution)/shard_map/ppermute | solution.py:688
  125.1 28.7 %collective-permute-start.16 = (f32[1,2,80,640]{3,2,1,0:T(8,128)}, f32[1,2,80,640]{3,2,1,0:T(8,128)}, u32[]{:S(2)}, u32[]{:S(2)}) collective-permute-start(f32[1,2,80,640]{3,2,1,0:T(8,128)} %join.4.refs_1_), channel_id=1, source_target_pairs={{0,2},{1,3},{2,0},{3,1},{4,6},{5,7},{6,4},{7,5},{8,10},{9,11},{10,... | collective-permute-start | bytes 1228808 | tf_op jit(solution)/shard_map/ppermute | solution.py:688
  135.0 16.6 %collective-permute-start.19 = (f32[104,384]{1,0:T(8,128)}, f32[104,384]{1,0:T(8,128)}, u32[]{:S(2)}, u32[]{:S(2)}) collective-permute-start(f32[104,384]{1,0:T(8,128)} %tie.28.refs_1_), channel_id=1, source_target_pairs={{0,8},{4,12},{8,0},{12,4},{1,9},{5,13},{9,1},{13,5},{2,10},{6,14},... | collective-permute-start | bytes 479240 | tf_op jit(solution)/shard_map/ppermute | solution.py:688
  138.3 13.4 %collective-permute-start.18 = (f32[104,384]{1,0:T(8,128)}, f32[104,384]{1,0:T(8,128)}, u32[]{:S(2)}, u32[]{:S(2)}) collective-permute-start(f32[104,384]{1,0:T(8,128)} %tie.28.refs_1_), channel_id=1, source_target_pairs={{0,4},{4,0},{8,12},{12,8},{1,5},{5,1},{9,13},{13,9},{2,6},{6,2},{1... | collective-permute-start | bytes 479240 | tf_op jit(solution)/shard_map/ppermute | solution.py:688
  153.9 14.3 %collective-permute-start.21 = (f32[1,2,104,640]{3,2,1,0:T(8,128)}, f32[1,2,104,640]{3,2,1,0:T(8,128)}, u32[]{:S(2)}, u32[]{:S(2)}) collective-permute-start(f32[1,2,104,640]{3,2,1,0:T(8,128)} %tie.29.refs_1_), channel_id=1, source_target_pairs={{0,2},{1,3},{2,0},{3,1},{4,6},{5,7},{6,4},{7,5},{8,10},{9,11},{10,... | collective-permute-start | bytes 1597448 | tf_op jit(solution)/shard_map/ppermute | solution.py:688
  244.6 24.5 %collective-permute-start.28 = (f32[80,384]{1,0:T(8,128)}, f32[80,384]{1,0:T(8,128)}, u32[]{:S(2)}, u32[]{:S(2)}) collective-permute-start(f32[80,384]{1,0:T(8,128)} %get-tuple-element.60), channel_id=1, source_target_pairs={{0,4},{4,0},{8,12},{12,8},{1,5},{5,1},{9,13},{13,9},{2,6},{6,2},{1... | collective-permute-start | bytes 368648 | tf_op jit(solution)/shard_map/ppermute | solution.py:688
  244.6 24.5 %collective-permute-start.29 = (f32[80,384]{1,0:T(8,128)}, f32[80,384]{1,0:T(8,128)}, u32[]{:S(2)}, u32[]{:S(2)}) collective-permute-start(f32[80,384]{1,0:T(8,128)} %get-tuple-element.61), channel_id=1, source_target_pairs={{0,8},{4,12},{8,0},{12,4},{1,9},{5,13},{9,1},{13,5},{2,10},{6,14},... | collective-permute-start | bytes 368648 | tf_op jit(solution)/shard_map/ppermute | solution.py:688
  246.6 22.5 %collective-permute-start.30 = (f32[80,384]{1,0:T(8,128)}, f32[80,384]{1,0:T(8,128)}, u32[]{:S(2)}, u32[]{:S(2)}) collective-permute-start(f32[80,384]{1,0:T(8,128)} %get-tuple-element.62), channel_id=1, source_target_pairs={{0,12},{4,8},{8,4},{12,0},{1,13},{5,9},{9,5},{13,1},{2,14},{6,10},... | collective-permute-start | bytes 368648 | tf_op jit(solution)/shard_map/ppermute | solution.py:688
  249.0 22.7 %collective-permute-start.27 = (f32[1,2,104,640]{3,2,1,0:T(8,128)}, f32[1,2,104,640]{3,2,1,0:T(8,128)}, u32[]{:S(2)}, u32[]{:S(2)}) collective-permute-start(f32[1,2,104,640]{3,2,1,0:T(8,128)} %tie.32.refs_2_), channel_id=1, source_target_pairs={{0,2},{1,3},{2,0},{3,1},{4,6},{5,7},{6,4},{7,5},{8,10},{9,11},{10,... | collective-permute-start | bytes 1597448 | tf_op jit(solution)/shard_map/ppermute | solution.py:688
  289.1 20.7 %collective-permute-start.37 = (f32[104,384]{1,0:T(8,128)S(1)}, f32[104,384]{1,0:T(8,128)}, u32[]{:S(2)}, u32[]{:S(2)}) collective-permute-start(f32[104,384]{1,0:T(8,128)S(1)} %add_add_fusion.refs_2_.refs_8_), channel_id=1, source_target_pairs={{0,15},{1,14},{2,13},{3,12},{4,11},{5,10},{6,9},{7,8},{8,7},{9,6},... | collective-permute-start | bytes 479240 | tf_op jit(solution)/shard_map/ppermute | solution.py:692
  303.3 20.8 %collective-permute-start.39 = (f32[80,384]{1,0:T(8,128)}, f32[80,384]{1,0:T(8,128)}, u32[]{:S(2)}, u32[]{:S(2)}) collective-permute-start(f32[80,384]{1,0:T(8,128)} %add.116.refs_0_.refs_1_), channel_id=1, source_target_pairs={{0,12},{4,8},{8,4},{12,0},{1,13},{5,9},{9,5},{13,1},{2,14},{6,10},... | collective-permute-start | bytes 368648 | tf_op jit(solution)/shard_map/ppermute | solution.py:688
  305.0 19.1 %collective-permute-start.38 = (f32[80,384]{1,0:T(8,128)}, f32[80,384]{1,0:T(8,128)}, u32[]{:S(2)}, u32[]{:S(2)}) collective-permute-start(f32[80,384]{1,0:T(8,128)} %add.116.refs_0_.refs_1_), channel_id=1, source_target_pairs={{0,8},{4,12},{8,0},{12,4},{1,9},{5,13},{9,1},{13,5},{2,10},{6,14},... | collective-permute-start | bytes 368648 | tf_op jit(solution)/shard_map/ppermute | solution.py:688
  309.8 14.3 %collective-permute-start.33 = (f32[80,384]{1,0:T(8,128)}, f32[80,384]{1,0:T(8,128)}, u32[]{:S(2)}, u32[]{:S(2)}) collective-permute-start(f32[80,384]{1,0:T(8,128)} %add.116.refs_0_.refs_1_), channel_id=1, source_target_pairs={{0,4},{4,0},{8,12},{12,8},{1,5},{5,1},{9,13},{13,9},{2,6},{6,2},{1... | collective-permute-start | bytes 368648 | tf_op jit(solution)/shard_map/ppermute | solution.py:688
  326.2 25.2 %collective-permute-start.40 = (f32[1,2,80,640]{3,2,1,0:T(8,128)}, f32[1,2,80,640]{3,2,1,0:T(8,128)}, u32[]{:S(2)}, u32[]{:S(2)}) collective-permute-start(f32[1,2,80,640]{3,2,1,0:T(8,128)} %join.6.refs_0_.refs_1_), channel_id=1, source_target_pairs={{0,2},{1,3},{2,0},{3,1},{4,6},{5,7},{6,4},{7,5},{8,10},{9,11},{10,... | collective-permute-start | bytes 1228808 | tf_op jit(solution)/shard_map/ppermute | solution.py:688
  330.4 14.2 %collective-permute-start.44 = (f32[104,384]{1,0:T(8,128)}, f32[104,384]{1,0:T(8,128)}, u32[]{:S(2)}, u32[]{:S(2)}) collective-permute-start(f32[104,384]{1,0:T(8,128)} %tie.38.refs_1_), channel_id=1, source_target_pairs={{0,12},{4,8},{8,4},{12,0},{1,13},{5,9},{9,5},{13,1},{2,14},{6,10},... | collective-permute-start | bytes 479240 | tf_op jit(solution)/shard_map/ppermute | solution.py:688
  331.8 17.3 %collective-permute-start.43 = (f32[104,384]{1,0:T(8,128)}, f32[104,384]{1,0:T(8,128)}, u32[]{:S(2)}, u32[]{:S(2)}) collective-permute-start(f32[104,384]{1,0:T(8,128)} %tie.38.refs_1_), channel_id=1, source_target_pairs={{0,8},{4,12},{8,0},{12,4},{1,9},{5,13},{9,1},{13,5},{2,10},{6,14},... | collective-permute-start | bytes 479240 | tf_op jit(solution)/shard_map/ppermute | solution.py:688
  336.2 12.9 %collective-permute-start.42 = (f32[104,384]{1,0:T(8,128)}, f32[104,384]{1,0:T(8,128)}, u32[]{:S(2)}, u32[]{:S(2)}) collective-permute-start(f32[104,384]{1,0:T(8,128)} %tie.38.refs_1_), channel_id=1, source_target_pairs={{0,4},{4,0},{8,12},{12,8},{1,5},{5,1},{9,13},{13,9},{2,6},{6,2},{1... | collective-permute-start | bytes 479240 | tf_op jit(solution)/shard_map/ppermute | solution.py:688
  351.4 15.6 %collective-permute-start.45 = (f32[1,2,104,640]{3,2,1,0:T(8,128)}, f32[1,2,104,640]{3,2,1,0:T(8,128)S(1)}, u32[]{:S(2)}, u32[]{:S(2)}) collective-permute-start(f32[1,2,104,640]{3,2,1,0:T(8,128)} %tie.39.refs_1_), channel_id=1, source_target_pairs={{0,2},{1,3},{2,0},{3,1},{4,6},{5,7},{6,4},{7,5},{8,10},{9,11},{10,... | collective-permute-start | bytes 1597448 | tf_op jit(solution)/shard_map/ppermute | solution.py:688
  (51 other events, 326.6 us)

commit v4 on v3

--- a/solution.py
+++ b/solution.py
@@ -246,14 +246,16 @@
             send_refs[m][:, :, used:, :] = blank
 
 
-def take_modes(plan, flag_ref, turn_ref, own_refs, other_refs, total_ref, high_rows, low_rows):
+def take_modes(plan, flag_ref, turn_ref, group_refs, total_ref, high_rows, low_rows):
     lp, half = plan.lp, plan.half
-    odd = flag_ref[0] == 1
+    odd, upper = flag_ref[0] == 1, flag_ref[1] == 1
     cosine, sine = turn_ref[0:1, :], turn_ref[1:2, :]
 
     def group(m, g, r, rows):
-        own, other = own_refs[m][g // 2, r, rows, :], other_refs[m][g // 2, r, rows, :]
-        return jnp.where(odd, own, other) if g % 2 else jnp.where(odd, other, own)
+        here, there, core_here, core_there = (ref[g // 4, r, rows, :] for ref in group_refs[m])
+        first, second = ((here, there), (core_here, core_there)) if g % 2 else ((core_here, core_there), (here, there))
+        held, came = (jnp.where(odd, a, b) for a, b in zip(first, second))
+        return jnp.where(upper, held, came) if g // 2 % 2 else jnp.where(upper, came, held)
 
     for c in range(plan.c):
         for m, base, size, place in plan.segments(c):
@@ -301,14 +303,14 @@
 
 
 def middle_kernel(plan, flag_ref, *refs):
-    own_refs, other_refs, refs = refs[:2], refs[2:4], refs[4:]
+    group_refs, refs = (refs[:4], refs[4:8]), refs[8:]
     linear_ref, cotangent_ref, plane_ref, depth_ref, inverse_ref, turn_ref, output_ref, gradient_ref = refs[:8]
     keep_refs, send_refs, (lines_ref, back_ref, total_ref, high_rows, low_rows) = refs[8:10], refs[10:12], refs[12:]
     step = pl.program_id(0)
 
     @pl.when(step == 0)
     def _():
-        take_modes(plan, flag_ref, turn_ref, own_refs, other_refs, total_ref, high_rows, low_rows)
+        take_modes(plan, flag_ref, turn_ref, group_refs, total_ref, high_rows, low_rows)
 
     plane_synthesis(plan, high_rows, low_rows, plane_ref, lines_ref)
     shape = (plan.xb, plan.ny, plan.nz)
@@ -334,12 +336,12 @@
 
 
 def synthesise_kernel(plan, flag_ref, *refs):
-    own_refs, other_refs, refs = refs[:2], refs[2:4], refs[4:]
+    group_refs, refs = (refs[:4], refs[4:8]), refs[8:]
     linear_ref, plane_ref, inverse_ref, turn_ref, output_ref, lines_ref, total_ref, high_rows, low_rows = refs
 
     @pl.when(pl.program_id(0) == 0)
     def _():
-        take_modes(plan, flag_ref, turn_ref, own_refs, other_refs, total_ref, high_rows, low_rows)
+        take_modes(plan, flag_ref, turn_ref, group_refs, total_ref, high_rows, low_rows)
 
     plane_synthesis(plan, high_rows, low_rows, plane_ref, lines_ref)
 
@@ -581,7 +583,7 @@
             lax.dynamic_index_in_dim(turns, slab, 0, False), chan, 0, False
         )
         self.slab_index = slab.astype(jnp.int32).reshape(1)
-        self.flag = (chan % 2).astype(jnp.int32).reshape(1)
+        self.flag = jnp.stack([chan % 2, chan // 2 % 2]).astype(jnp.int32)
         self.upper = (chan >= plan.half).astype(jnp.int32).reshape(1)
         tables = [plan.orders(m) for m in range(plan.chunks)]
         self.order = [jnp.asarray(t) for t in tables]
@@ -621,29 +623,31 @@
         )(self.flag, values, self.plane, self.depth, self.turn)
         return made[:2], made[2:]
 
-    def middle(self, owns, others, linear, cotangent):
+    def middle(self, groups, linear, cotangent):
         plan = self.plan
         halves = self.half_shapes()
+        taken = [part for group in groups for part in group]
         field, spec = shaped(plan.nx, plan.c, plan.ny, plan.nz), self.field_spec()
         modes = [whole_shape(h) for h in halves * 2]
         output, gradient, *made = call(
             partial(middle_kernel, plan), "middle", plan.nx // plan.xb,
-            [scalar(), *modes, spec, spec, self.table(), whole(self.depth), whole(self.inverse), whole(self.turn)],
+            [scalar(), *[whole(t) for t in taken], spec, spec, self.table(), whole(self.depth), whole(self.inverse), whole(self.turn)],
             [spec, spec, *modes], [field, field, *[shaped(*h) for h in halves * 2]],
             [self.lines(), self.lines(), *self.spectra()], 47,
-        )(self.flag, *owns, *others, linear, cotangent, self.plane, self.depth, self.inverse, self.turn)
+        )(self.flag, *taken, linear, cotangent, self.plane, self.depth, self.inverse, self.turn)
         return output, gradient, made[:2], made[2:]
 
-    def synthesise(self, before, owns, others, linear):
-        plan = self.plan
+    def synthesise(self, before, groups, linear):
+        plan = self.plan
+        taken = [part for group in groups for part in group]
         spec = self.field_spec()
         return call(
             partial(synthesise_kernel, plan), "synthesise", plan.nx // plan.xb,
-            [scalar(), *[whole_shape(h) for h in self.half_shapes() * 2], spec, self.table(),
+            [scalar(), *[whole(t) for t in taken], spec, self.table(),
              whole(self.inverse), whole(self.turn)],
             spec, shaped(plan.nx, plan.c, plan.ny, plan.nz),
             [self.lines(), *self.spectra()], 20, before,
-        )(self.flag, *owns, *others, linear, self.plane, self.inverse, self.turn)
+        )(self.flag, *taken, linear, self.plane, self.inverse, self.turn)
 
     def linear(self, half, before, filled, values, matrix, bias):
         plan = self.plan
@@ -764,12 +768,12 @@
         mine, pieces = self.cut(keep1, tie(came1, own0))
         arrived = [self.across(piece, "slab", j + 1) for j, piece in enumerate(pieces)]
         out0, back0 = mix(0, [mine], own0, mirror0)
-        for piece in [tie(arrived[0], out0)] + arrived[1:]:
+        full0 = out0 + self.mirrored(back0)
+        for piece in [tie(arrived[0], full0)] + arrived[1:]:
             mine = mine + piece
         own1 = mine
         mirror1 = self.mirrored(own1)
 
-        full0 = out0 + self.mirrored(back0)
         arrived = [self.across(full0, "slab", j) for j in range(1, plan.s)]
         out1, back1 = mix(1, [full0], own1, mirror1)
         full1 = out1 + self.mirrored(back1)
@@ -784,18 +788,19 @@
         came1 = self.across(total1, "chan", plan.ch // 2)
         came1 = fill(3, came1, total1)
 
-        owns, others = [], []
+        groups = []
         for total, other in ((total0, came0), (total1, came1)):
+            if groups:
+                other = tie(other, *groups[0][2:])
             bit = plan.ch // 2
-            while bit > 1:
+            while bit > 2:
                 upper = (self.chan // bit) % 2 == 1
                 total = jnp.stack([jnp.where(upper, other, total), jnp.where(upper, total, other)], axis=1)
                 total = total.reshape((-1,) + total.shape[2:])
                 bit //= 2
                 other = self.across(total, "chan", bit)
-            owns.append(total)
-            others.append(other)
-        return owns, others, modes
+            groups.append((total, other, self.across(total, "chan", 1), self.across(other, "chan", 1)))
+        return groups, modes
 
 
 def local(inputs, cotangent, spectral, local_weight, bias_vector):
@@ -826,8 +831,8 @@
 
     keeps, sends = program.analyse(values)
     there = [linear(half, "linear", values, local_weight.T, bias_vector) for half in range(2)]
-    owns, others, modes = program.exchange(keeps, sends, mix(mix_kernel, "mix"), (relaid, there[0], None, there[1]))
-    output, gradient, keeps, sends = program.middle(owns, others, held["linear"], slopes)
+    groups, modes = program.exchange(keeps, sends, mix(mix_kernel, "mix"), (relaid, there[0], None, there[1]))
+    output, gradient, keeps, sends = program.middle(groups, held["linear"], slopes)
 
     def outer(before, grads):
         held["outer"] = program.outer(before, modes, grads, weights)
@@ -838,10 +843,10 @@
         return held["outer"]
 
     back = [linear(half, "back", gradient, local_weight, jnp.zeros_like(bias_vector)) for half in range(2)]
-    owns, others, _ = program.exchange(
+    groups, _ = program.exchange(
         keeps, sends, mix(mix_back_kernel, "mix_back"), (back[0], back[1], outer, placed)
     )
-    grad_inputs = program.synthesise([], owns, others, held["back"])
+    grad_inputs = program.synthesise([], groups, held["back"])
     grad_spectral = held["outer"]
     return (
         jnp.transpose(output, (0, 2, 1, 3)),

time: 400 us -> 386 us (0.965)
  waiting for transfers between devices: 63.9 us -> 57.7 us
  starting transfers between devices: 74.7 us -> 70.2 us
    ppermute x8, waiting for transfers between devices: 22.8 us -> 11.4 us  [mirrored(): lax.ppermute(value, ('slab', 'chan'), [(i, total - 1 - i) for i in range(...]
    ppermute x40 -> x44, waiting for transfers between devices: 41.1 us -> 46.2 us  [across(): return lax.ppermute(value, axis, [(i, i ^ bit) for i in range(size)])]
    ppermute x40 -> x44, starting transfers between devices: 55.9 us -> 51.2 us  [across(): return lax.ppermute(value, axis, [(i, i ^ bit) for i in range(size)])]
    unnamed x56 -> x34, local copies, waits for them, and re-layouts: 19.3 us -> 18.3 us
  transfers between devices with their start and end apart: 48 -> 52, of which waited for: 17 -> 17; matrix products, arithmetic and copies ran while one was open for 9% -> 10% of each run, Pallas kernels for 25% -> 26%
where the time goes in v4:
time: 386 us; the launch traced here: 381 us
  Pallas kernels  201 us (52%)
  starting transfers between devices  70.2 us (18%)
  waiting for transfers between devices  57.7 us (15%)
  local copies, waits for them, and re-layouts  30.8 us (8%)
  other arithmetic  20.3 us (5%)
    ppermute x44, starting transfers between devices, across(): return lax.ppermute(value, axis, [(i, i ^ bit) for i in range(size)])  51.2 us
    pallas_call x1, Pallas kernels, middle(): call(partial(middle_kernel, plan), 'middle', plan.nx // plan.xb, [scalar(...  47.3 us
    ppermute x44, waiting for transfers between devices, across(): return lax.ppermute(value, axis, [(i, i ^ bit) for i in range(size)])  46.2 us
    pallas_call x4, Pallas kernels, linear(): call(partial(linear_kernel, plan), 'linear', steps, [spec, whole(matrix),...  43.3 us
    pallas_call x4, Pallas kernels, mix(): call(partial(kernel, plan), name, plan.wb // plan.bb, [scalar(), whole_sh...  33.5 us
    pallas_call x1, Pallas kernels, analyse(): call(partial(analyse_kernel, plan), 'analyse', plan.nx // plan.xb, [scala...  27.1 us
    pallas_call x1, Pallas kernels, synthesise(): call(partial(synthesise_kernel, plan), 'synthesise', plan.nx // plan.xb,...  19.9 us
    ppermute x8, starting transfers between devices, mirrored(): lax.ppermute(value, ('slab', 'chan'), [(i, total - 1 - i) for i in range(...  18.9 us
  transfers between devices with their start and end apart: 52, of which 17 were waited for; matrix products, arithmetic and copies ran while one was open for 10% of the time, Pallas kernels for 26%

profile of v4, /device:TPU:0, one launch (start us, length us, event | category | flops | bytes accessed | tf_op | source)
XLA Modules:
  0.0 380.6 jit_solution(17009469615279757660)
XLA Ops:
  2.6 27.1 %analyse.1 = (f32[2,2,80,640]{3,2,1,0:T(8,128)}, f32[2,2,104,640]{3,2,1,0:T(8,128)}, f32[2,2,80,640]{3,2,1,0:T(8,128)}, f32[2,2,104,640]{3,2,1,0:T(8,128)}) custom-call(s32[2]{0:T(128)} %pad_add_fusion.refs_0_, f32[32,20,32,128]{3,2,1,0:T(8,128)} %bitcast.23, bf16[4,768,1280]{2,1,0:T(8,128)(2,1)} %constant.125.clone.refs_2_.refs_11_.refs_10_, ...), custom_call_target="tpu_custom_call" | custom-call | flops 29899999232 | bytes 93600000 | tf_op jit(solution)/shard_map/analyse/pallas_call | solution.py:618
  38.6 6.8 %copy.49 = f32[8,8,2,20,640]{4,1,3,2,0:T(8,128)} copy(f32[8,8,2,20,640]{4,2,3,1,0:T(2,128)} %param.17) | data formatting | bytes 13107200 | tf_op args[2]
  58.6 7.9 %linear.4.refs_1_.refs_0_ = f32[32,20,32,128]{3,2,1,0:T(8,128)} custom-call(f32[80,384]{1,0:T(8,128)} %get-tuple-element.41.refs_0_, f32[1,2,104,640]{3,2,1,0:T(8,128)} %tie.25.refs_1_, f32[32,20,32,128]{3,2,1,0:T(8,128)} %bitcast.24, f32[20,20]{1,0:T(8,128)} %bitcast.26, f32[1,20]{1,0:T(1,128)} %bitcast.28), custom_call_target="tpu_custom_call" | custom-call | flops 8049999872 | bytes 25200000 | tf_op jit(solution)/shard_map/linear/pallas_call | solution.py:657
  79.8 8.4 %mix.2 = (f32[80,384]{1,0:T(8,128)}, f32[80,384]{1,0:T(8,128)}) custom-call(f32[104,384]{1,0:T(8,128)} %get-tuple-element.45.refs_0_, s32[1]{0:T(128)} %bitcast.9.refs_1_, f32[80,384]{1,0:T(8,128)} %add_add_fusion.3.refs_1_.refs_2_, f32[80,384]{1,0:T(8,128)} %collective-permute-done.7.refs_3_, bf16[2,160,80]{2,1,0:T(8,128)(2,1)} %constant.129.clone.refs_4_.refs_10_, ...), custom_call_target="tpu_custom_call" | custom-call | flops 10350000128 | bytes 32400000 | tf_op jit(solution)/shard_map/mix/pallas_call | solution.py:668
  89.4 6.4 %collective-permute-done.8 = f32[80,384]{1,0:T(8,128)S(1)} collective-permute-done((f32[80,384]{1,0:T(8,128)}, f32[80,384]{1,0:T(8,128)S(1)}, u32[]{:S(2)}, u32[]{:S(2)}) %collective-permute-start.8) | collective-permute-done | bytes 122912 | tf_op jit(solution)/shard_map/ppermute | solution.py:696
  107.3 8.5 %mix.3 = (f32[104,384]{1,0:T(8,128)}, f32[104,384]{1,0:T(8,128)}) custom-call(f32[80,384]{1,0:T(8,128)} %add.103.refs_1_.refs_0_, s32[1]{0:T(128)} %bitcast.9.refs_1_, f32[104,384]{1,0:T(8,128)} %copy-done.12, f32[104,384]{1,0:T(8,128)} %collective-permute-done.13.refs_3_.refs_5_, bf16[2,160,104]{2,1,0:T(8,128)(2,1)} %constant.130.clone.refs_4_.refs_11_, ...), custom_call_target="tpu_custom_call" | custom-call | flops 10350000128 | bytes 32400000 | tf_op jit(solution)/shard_map/mix/pallas_call | solution.py:668
  117.6 7.2 %collective-permute-done.14.refs_3_ = f32[80,384]{1,0:T(8,128)} collective-permute-done((f32[80,384]{1,0:T(8,128)}, f32[80,384]{1,0:T(8,128)}, u32[]{:S(2)}, u32[]{:S(2)}) %collective-permute-start.14) | collective-permute-done | bytes 122912 | tf_op jit(solution)/shard_map/ppermute | solution.py:692
  131.3 5.4 %collective-permute-start.21 = (f32[104,384]{1,0:T(8,128)}, f32[104,384]{1,0:T(8,128)}, u32[]{:S(2)}, u32[]{:S(2)}) collective-permute-start(f32[104,384]{1,0:T(8,128)} %tie.30.refs_1_), channel_id=1, source_target_pairs={{0,8},{4,12},{8,0},{12,4},{1,9},{5,13},{9,1},{13,5},{2,10},{6,14},... | collective-permute-start | bytes 479240 | tf_op jit(solution)/shard_map/ppermute | solution.py:692
  138.1 10.2 %collective-permute-done.21.refs_3_ = f32[104,384]{1,0:T(8,128)} collective-permute-done((f32[104,384]{1,0:T(8,128)}, f32[104,384]{1,0:T(8,128)}, u32[]{:S(2)}, u32[]{:S(2)}) %collective-permute-start.21) | collective-permute-done | bytes 159776 | tf_op jit(solution)/shard_map/ppermute | solution.py:692
  151.3 8.2 %linear.5.refs_1_.refs_9_ = f32[32,20,32,128]{3,2,1,0:T(8,128)} custom-call(f32[32,20,32,128]{3,2,1,0:T(8,128)} %linear.4.refs_1_.refs_0_, f32[1,2,104,640]{3,2,1,0:T(8,128)} %tie.31.refs_1_.refs_5_, f32[32,20,32,128]{3,2,1,0:T(8,128)} %bitcast.25, f32[20,20]{1,0:T(8,128)} %bitcast.27, f32[1,20]{1,0:T(1,128)} %bitcast.29), custom_call_target="tpu_custom_call", output_to_operand_aliasing={{}: (0, {})} | custom-call | flops 8049999872 | bytes 25200000 | tf_op jit(solution)/shard_map/linear/pallas_call | solution.py:657
  159.5 6.0 %collective-permute-done.23.refs_0_ = f32[1,2,104,640]{3,2,1,0:T(8,128)} collective-permute-done((f32[1,2,104,640]{3,2,1,0:T(8,128)}, f32[1,2,104,640]{3,2,1,0:T(8,128)}, u32[]{:S(2)}, u32[]{:S(2)}) %collective-permute-start.23) | collective-permute-done | bytes 532512 | tf_op jit(solution)/shard_map/ppermute | solution.py:692
  167.8 47.3 %middle.1 = (f32[32,20,32,128]{3,2,1,0:T(8,128)}, f32[32,20,32,128]{3,2,1,0:T(8,128)}, f32[2,2,80,640]{3,2,1,0:T(8,128)}, f32[2,2,104,640]{3,2,1,0:T(8,128)}, f3...) custom-call(s32[2]{0:T(128)} %pad_add_fusion.refs_0_, f32[1,2,80,640]{3,2,1,0:T(8,128)} %join.4.refs_1_, ...), custom_call_target="tpu_custom_call" | custom-call | flops 54050000896 | bytes 169200000 | tf_op jit(solution)/shard_map/middle/pallas_call | solution.py:632
  222.9 7.9 %linear.6.refs_1_.refs_0_ = f32[32,20,32,128]{3,2,1,0:T(8,128)} custom-call(f32[1,2,80,640]{3,2,1,0:T(8,128)} %dynamic-slice_add_fusion.2.refs_0_, f32[2,2,104,640]{3,2,1,0:T(8,128)} %collective-permute-done.26.refs_1_.arrived_ref, f32[32,20,32,128]{3,2,1,0:T(8,128)} %get-tuple-element.58.refs_2_.refs_3_, f32[20,20]{1,0:T(8,128)} %refs_4_.5, ...), custom_call_target="tpu_custom_call" | custom-call | flops 8049999872 | bytes 25200000 | tf_op jit(solution)/shard_map/linear/pallas_call | solution.py:657
  241.9 19.3 %linear.7.refs_1_.refs_9_ = f32[32,20,32,128]{3,2,1,0:T(8,128)} custom-call(f32[32,20,32,128]{3,2,1,0:T(8,128)} %linear.6.refs_1_.refs_0_, f32[80,384]{1,0:T(8,128)} %get-tuple-element.59.refs_1_, f32[1,2,104,640]{3,2,1,0:T(8,128)} %tie.35.refs_2_, f32[32,20,32,128]{3,2,1,0:T(8,128)} %get-tuple-element.58.refs_2_.refs_3_, ...), custom_call_target="tpu_custom_call", output_to_operand_aliasing={{}: (0, {})} | custom-call | flops 8049999872 | bytes 25200000 | tf_op jit(solution)/shard_map/linear/pallas_call | solution.py:657
  271.4 8.3 %mix_back.2 = (f32[80,384]{1,0:T(8,128)}, f32[80,384]{1,0:T(8,128)}) custom-call(f32[104,384]{1,0:T(8,128)} %get-tuple-element.63.refs_0_, s32[1]{0:T(128)} %bitcast.9.refs_1_, f32[80,384]{1,0:T(8,128)} %add_add_fusion.2.refs_1_.refs_2_.refs_6_, f32[80,384]{1,0:T(8,128)} %collective-permute-done.33.refs_3_.refs_7_, ...), custom_call_target="tpu_custom_call" | custom-call | flops 10350000128 | bytes 32400000 | tf_op jit(solution)/shard_map/mix_back/pallas_call | solution.py:668
  283.3 3.8 %collective-permute-done.34 = f32[80,384]{1,0:T(8,128)S(1)} collective-permute-done((f32[80,384]{1,0:T(8,128)}, f32[80,384]{1,0:T(8,128)S(1)}, u32[]{:S(2)}, u32[]{:S(2)}) %collective-permute-start.34) | collective-permute-done | bytes 122912 | tf_op jit(solution)/shard_map/ppermute | solution.py:696
  290.5 3.7 collective-permute-start.39
  298.8 8.4 %mix_back.3 = (f32[104,384]{1,0:T(8,128)}, f32[104,384]{1,0:T(8,128)}) custom-call(f32[80,384]{1,0:T(8,128)} %add.113.refs_1_.refs_0_, s32[1]{0:T(128)} %bitcast.9.refs_1_, f32[104,384]{1,0:T(8,128)} %copy-done.13, f32[104,384]{1,0:T(8,128)} %collective-permute-done.39.refs_3_.refs_9_, bf16[2,160,104]{2,1,0:T(8,128)(2,1)} %constant.130.clone.refs_4_.refs_11_, ...), custom_call_target="tpu_custom_call" | custom-call | flops 10350000128 | bytes 32400000 | tf_op jit(solution)/shard_map/mix_back/pallas_call | solution.py:668
  307.1 4.8 %collective-permute-start.45 = (f32[104,384]{1,0:T(8,128)}, f32[104,384]{1,0:T(8,128)}, u32[]{:S(2)}, u32[]{:S(2)}) collective-permute-start(f32[104,384]{1,0:T(8,128)} %get-tuple-element.69.refs_1_), channel_id=1, source_target_pairs={{0,15},{1,14},{2,13},{3,12},{4,11},{5,10},{6,9},{7,8},{8,7},{9,6},... | collective-permute-start | bytes 479240 | tf_op jit(solution)/shard_map/ppermute | solution.py:696
  312.0 5.3 %collective-permute-done.40.refs_3_ = f32[80,384]{1,0:T(8,128)} collective-permute-done((f32[80,384]{1,0:T(8,128)}, f32[80,384]{1,0:T(8,128)}, u32[]{:S(2)}, u32[]{:S(2)}) %collective-permute-start.40) | collective-permute-done | bytes 122912 | tf_op jit(solution)/shard_map/ppermute | solution.py:692
  321.9 6.0 %collective-permute-start.47 = (f32[104,384]{1,0:T(8,128)}, f32[104,384]{1,0:T(8,128)}, u32[]{:S(2)}, u32[]{:S(2)}) collective-permute-start(f32[104,384]{1,0:T(8,128)} %tie.41.refs_1_), channel_id=1, source_target_pairs={{0,8},{4,12},{8,0},{12,4},{1,9},{5,13},{9,1},{13,5},{2,10},{6,14},... | collective-permute-start | bytes 479240 | tf_op jit(solution)/shard_map/ppermute | solution.py:692
  327.9 8.3 %outer.1.refs_1_ = f32[8,2,20,8,640]{4,3,2,1,0:T(8,128)} custom-call(f32[1,2,80,640]{3,2,1,0:T(8,128)} %join.6.refs_0_.refs_1_, s32[1]{0:T(128)} %bitcast.9.refs_1_, f32[80,384]{1,0:T(8,128)} %add_add_fusion.3.refs_1_.refs_2_, f32[80,384]{1,0:T(8,128)} %collective-permute-done.7.refs_3_, f32[104,384]{1,0:T(8,128)} %copy-done.12, ...), custom_call_target="tpu_custom_call" | custom-call | flops 10350000128 | bytes 32400000 | tf_op jit(solution)/shard_map/outer/pallas_call | solution.py:684
  344.2 10.7 %copy.48 = f32[8,2,20,8,640]{4,1,2,3,0:T(2,128)} copy(f32[8,2,20,8,640]{4,3,2,1,0:T(8,128)} %outer.1.refs_1_) | data formatting | bytes 13107200 | tf_op jit(solution)/shard_map/outer/pallas_call | solution.py:684
  360.5 19.9 %synthesise.1 = f32[32,20,32,128]{3,2,1,0:T(8,128)} custom-call(s32[2]{0:T(128)} %pad_add_fusion.refs_0_, f32[1,2,80,640]{3,2,1,0:T(8,128)} %join.6.refs_0_.refs_1_, f32[1,2,80,640]{3,2,1,0:T(8,128)} %tie.40.refs_1_.refs_2_, f32[1,2,80,640]{3,2,1,0:T(8,128)} %copy-done.6, f32[1,2,80,640]{3,2,1,0:T(8,128)} %copy-done.7, ...), custom_call_target="tpu_custom_call" | custom-call | flops 23000000512 | bytes 72000000 | tf_op jit(solution)/shard_map/synthesise/pallas_call | solution.py:644
  (174 shorter events, 123.7 us)
Async XLA Ops:
  30.2 15.8 %collective-permute-start = (f32[2,2,104,640]{3,2,1,0:T(8,128)}, f32[2,2,104,640]{3,2,1,0:T(8,128)S(1)}, u32[]{:S(2)}, u32[]{:S(2)}) collective-permute-start(f32[2,2,104,640]{3,2,1,0:T(8,128)} %get-tuple-element.38), channel_id=1, source_target_pairs={{0,1},{1,0},{2,3},{3,2},{4,5},{5,4},{6,7},{7,6},{8,9},{9,8},{10,11... | collective-permute-start | bytes 3194888 | tf_op jit(solution)/shard_map/ppermute | solution.py:692
  34.3 15.9 %collective-permute-start.2 = (f32[1,2,80,640]{3,2,1,0:T(8,128)S(1)}, f32[1,2,80,640]{3,2,1,0:T(8,128)S(1)}, u32[]{:S(2)}, u32[]{:S(2)}) collective-permute-start(f32[1,2,80,640]{3,2,1,0:T(8,128)S(1)} %dynamic-slice_add_fusion.3.refs_1_), channel_id=1, source_target_pairs={{0,2},{1,3},{2,0},{3,1},{4,6},{5,7},{6,4},{7,5},{8,10},{9,11},{10,... | collective-permute-start | bytes 1228808 | tf_op jit(solution)/shard_map/ppermute | solution.py:692
  75.4 21.9 %collective-permute-start.10 = (f32[104,384]{1,0:T(8,128)}, f32[104,384]{1,0:T(8,128)}, u32[]{:S(2)}, u32[]{:S(2)}) collective-permute-start(f32[104,384]{1,0:T(8,128)} %get-tuple-element.48), channel_id=1, source_target_pairs={{0,4},{4,0},{8,12},{12,8},{1,5},{5,1},{9,13},{13,9},{2,6},{6,2},{1... | collective-permute-start | bytes 479240 | tf_op jit(solution)/shard_map/ppermute | solution.py:692
  75.5 21.8 %collective-permute-start.11 = (f32[104,384]{1,0:T(8,128)}, f32[104,384]{1,0:T(8,128)}, u32[]{:S(2)}, u32[]{:S(2)}) collective-permute-start(f32[104,384]{1,0:T(8,128)} %get-tuple-element.49), channel_id=1, source_target_pairs={{0,8},{4,12},{8,0},{12,4},{1,9},{5,13},{9,1},{13,5},{2,10},{6,14},... | collective-permute-start | bytes 479240 | tf_op jit(solution)/shard_map/ppermute | solution.py:692
  79.0 18.3 %collective-permute-start.12 = (f32[104,384]{1,0:T(8,128)}, f32[104,384]{1,0:T(8,128)}, u32[]{:S(2)}, u32[]{:S(2)}) collective-permute-start(f32[104,384]{1,0:T(8,128)} %get-tuple-element.50), channel_id=1, source_target_pairs={{0,12},{4,8},{8,4},{12,0},{1,13},{5,9},{9,5},{13,1},{2,14},{6,10},... | collective-permute-start | bytes 479240 | tf_op jit(solution)/shard_map/ppermute | solution.py:692
  100.5 17.1 %collective-permute-start.15 = (f32[80,384]{1,0:T(8,128)}, f32[80,384]{1,0:T(8,128)}, u32[]{:S(2)}, u32[]{:S(2)}) collective-permute-start(f32[80,384]{1,0:T(8,128)} %add.103.refs_1_.refs_0_), channel_id=1, source_target_pairs={{0,12},{4,8},{8,4},{12,0},{1,13},{5,9},{9,5},{13,1},{2,14},{6,10},... | collective-permute-start | bytes 368648 | tf_op jit(solution)/shard_map/ppermute | solution.py:692
  103.5 21.3 %collective-permute-start.14 = (f32[80,384]{1,0:T(8,128)}, f32[80,384]{1,0:T(8,128)}, u32[]{:S(2)}, u32[]{:S(2)}) collective-permute-start(f32[80,384]{1,0:T(8,128)} %add.103.refs_1_.refs_0_), channel_id=1, source_target_pairs={{0,8},{4,12},{8,0},{12,4},{1,9},{5,13},{9,1},{13,5},{2,10},{6,14},... | collective-permute-start | bytes 368648 | tf_op jit(solution)/shard_map/ppermute | solution.py:692
  126.9 23.7 %collective-permute-start.16 = (f32[1,2,80,640]{3,2,1,0:T(8,128)}, f32[1,2,80,640]{3,2,1,0:T(8,128)}, u32[]{:S(2)}, u32[]{:S(2)}) collective-permute-start(f32[1,2,80,640]{3,2,1,0:T(8,128)} %join.4.refs_1_), channel_id=1, source_target_pairs={{0,2},{1,3},{2,0},{3,1},{4,6},{5,7},{6,4},{7,5},{8,10},{9,11},{10,... | collective-permute-start | bytes 1228808 | tf_op jit(solution)/shard_map/ppermute | solution.py:692
  131.3 17.1 %collective-permute-start.21 = (f32[104,384]{1,0:T(8,128)}, f32[104,384]{1,0:T(8,128)}, u32[]{:S(2)}, u32[]{:S(2)}) collective-permute-start(f32[104,384]{1,0:T(8,128)} %tie.30.refs_1_), channel_id=1, source_target_pairs={{0,8},{4,12},{8,0},{12,4},{1,9},{5,13},{9,1},{13,5},{2,10},{6,14},... | collective-permute-start | bytes 479240 | tf_op jit(solution)/shard_map/ppermute | solution.py:692
  136.7 28.8 %collective-permute-start.17 = (f32[1,2,80,640]{3,2,1,0:T(8,128)}, f32[1,2,80,640]{3,2,1,0:T(8,128)}, u32[]{:S(2)}, u32[]{:S(2)}) collective-permute-start(f32[1,2,80,640]{3,2,1,0:T(8,128)} %join.4.refs_1_), channel_id=1, source_target_pairs={{0,1},{1,0},{2,3},{3,2},{4,5},{5,4},{6,7},{7,6},{8,9},{9,8},{10,11... | collective-permute-start | bytes 1228808 | tf_op jit(solution)/shard_map/ppermute | solution.py:692
  150.6 14.9 %collective-permute-start.24 = (f32[1,2,104,640]{3,2,1,0:T(8,128)}, f32[1,2,104,640]{3,2,1,0:T(8,128)}, u32[]{:S(2)}, u32[]{:S(2)}) collective-permute-start(f32[1,2,104,640]{3,2,1,0:T(8,128)} %tie.31.refs_1_.refs_5_), channel_id=1, source_target_pairs={{0,1},{1,0},{2,3},{3,2},{4,5},{5,4},{6,7},{7,6},{8,9},{9,8},{10,11... | collective-permute-start | bytes 1597448 | tf_op jit(solution)/shard_map/ppermute | solution.py:692
  236.7 24.4 %collective-permute-start.30 = (f32[80,384]{1,0:T(8,128)}, f32[80,384]{1,0:T(8,128)}, u32[]{:S(2)}, u32[]{:S(2)}) collective-permute-start(f32[80,384]{1,0:T(8,128)} %get-tuple-element.60), channel_id=1, source_target_pairs={{0,4},{4,0},{8,12},{12,8},{1,5},{5,1},{9,13},{13,9},{2,6},{6,2},{1... | collective-permute-start | bytes 368648 | tf_op jit(solution)/shard_map/ppermute | solution.py:692
  236.7 24.4 %collective-permute-start.31 = (f32[80,384]{1,0:T(8,128)}, f32[80,384]{1,0:T(8,128)}, u32[]{:S(2)}, u32[]{:S(2)}) collective-permute-start(f32[80,384]{1,0:T(8,128)} %get-tuple-element.61), channel_id=1, source_target_pairs={{0,8},{4,12},{8,0},{12,4},{1,9},{5,13},{9,1},{13,5},{2,10},{6,14},... | collective-permute-start | bytes 368648 | tf_op jit(solution)/shard_map/ppermute | solution.py:692
  238.4 22.8 %collective-permute-start.32 = (f32[80,384]{1,0:T(8,128)}, f32[80,384]{1,0:T(8,128)}, u32[]{:S(2)}, u32[]{:S(2)}) collective-permute-start(f32[80,384]{1,0:T(8,128)} %get-tuple-element.62), channel_id=1, source_target_pairs={{0,12},{4,8},{8,4},{12,0},{1,13},{5,9},{9,5},{13,1},{2,14},{6,10},... | collective-permute-start | bytes 368648 | tf_op jit(solution)/shard_map/ppermute | solution.py:692
  241.1 22.6 %collective-permute-start.29 = (f32[1,2,104,640]{3,2,1,0:T(8,128)}, f32[1,2,104,640]{3,2,1,0:T(8,128)}, u32[]{:S(2)}, u32[]{:S(2)}) collective-permute-start(f32[1,2,104,640]{3,2,1,0:T(8,128)} %tie.35.refs_2_), channel_id=1, source_target_pairs={{0,2},{1,3},{2,0},{3,1},{4,6},{5,7},{6,4},{7,5},{8,10},{9,11},{10,... | collective-permute-start | bytes 1597448 | tf_op jit(solution)/shard_map/ppermute | solution.py:692
  267.0 21.7 %collective-permute-start.36 = (f32[104,384]{1,0:T(8,128)}, f32[104,384]{1,0:T(8,128)}, u32[]{:S(2)}, u32[]{:S(2)}) collective-permute-start(f32[104,384]{1,0:T(8,128)} %get-tuple-element.66), channel_id=1, source_target_pairs={{0,4},{4,0},{8,12},{12,8},{1,5},{5,1},{9,13},{13,9},{2,6},{6,2},{1... | collective-permute-start | bytes 479240 | tf_op jit(solution)/shard_map/ppermute | solution.py:692
  267.0 21.7 %collective-permute-start.37 = (f32[104,384]{1,0:T(8,128)}, f32[104,384]{1,0:T(8,128)}, u32[]{:S(2)}, u32[]{:S(2)}) collective-permute-start(f32[104,384]{1,0:T(8,128)} %get-tuple-element.67), channel_id=1, source_target_pairs={{0,8},{4,12},{8,0},{12,4},{1,9},{5,13},{9,1},{13,5},{2,10},{6,14},... | collective-permute-start | bytes 479240 | tf_op jit(solution)/shard_map/ppermute | solution.py:692
  269.8 18.8 %collective-permute-start.38 = (f32[104,384]{1,0:T(8,128)}, f32[104,384]{1,0:T(8,128)}, u32[]{:S(2)}, u32[]{:S(2)}) collective-permute-start(f32[104,384]{1,0:T(8,128)} %get-tuple-element.68), channel_id=1, source_target_pairs={{0,12},{4,8},{8,4},{12,0},{1,13},{5,9},{9,5},{13,1},{2,14},{6,10},... | collective-permute-start | bytes 479240 | tf_op jit(solution)/shard_map/ppermute | solution.py:692
  294.2 17.8 %collective-permute-start.41 = (f32[80,384]{1,0:T(8,128)}, f32[80,384]{1,0:T(8,128)}, u32[]{:S(2)}, u32[]{:S(2)}) collective-permute-start(f32[80,384]{1,0:T(8,128)} %add.113.refs_1_.refs_0_), channel_id=1, source_target_pairs={{0,12},{4,8},{8,4},{12,0},{1,13},{5,9},{9,5},{13,1},{2,14},{6,10},... | collective-permute-start | bytes 368648 | tf_op jit(solution)/shard_map/ppermute | solution.py:692
  295.7 21.6 %collective-permute-start.40 = (f32[80,384]{1,0:T(8,128)}, f32[80,384]{1,0:T(8,128)}, u32[]{:S(2)}, u32[]{:S(2)}) collective-permute-start(f32[80,384]{1,0:T(8,128)} %add.113.refs_1_.refs_0_), channel_id=1, source_target_pairs={{0,8},{4,12},{8,0},{12,4},{1,9},{5,13},{9,1},{13,5},{2,10},{6,14},... | collective-permute-start | bytes 368648 | tf_op jit(solution)/shard_map/ppermute | solution.py:692
  296.8 15.2 %collective-permute-start.35 = (f32[80,384]{1,0:T(8,128)}, f32[80,384]{1,0:T(8,128)}, u32[]{:S(2)}, u32[]{:S(2)}) collective-permute-start(f32[80,384]{1,0:T(8,128)} %add.113.refs_1_.refs_0_), channel_id=1, source_target_pairs={{0,4},{4,0},{8,12},{12,8},{1,5},{5,1},{9,13},{13,9},{2,6},{6,2},{1... | collective-permute-start | bytes 368648 | tf_op jit(solution)/shard_map/ppermute | solution.py:692
  319.4 22.5 %collective-permute-start.42 = (f32[1,2,80,640]{3,2,1,0:T(8,128)}, f32[1,2,80,640]{3,2,1,0:T(8,128)}, u32[]{:S(2)}, u32[]{:S(2)}) collective-permute-start(f32[1,2,80,640]{3,2,1,0:T(8,128)} %join.6.refs_0_.refs_1_), channel_id=1, source_target_pairs={{0,2},{1,3},{2,0},{3,1},{4,6},{5,7},{6,4},{7,5},{8,10},{9,11},{10,... | collective-permute-start | bytes 1228808 | tf_op jit(solution)/shard_map/ppermute | solution.py:692
  321.1 15.2 %collective-permute-start.48 = (f32[104,384]{1,0:T(8,128)}, f32[104,384]{1,0:T(8,128)}, u32[]{:S(2)}, u32[]{:S(2)}) collective-permute-start(f32[104,384]{1,0:T(8,128)} %tie.41.refs_1_), channel_id=1, source_target_pairs={{0,12},{4,8},{8,4},{12,0},{1,13},{5,9},{9,5},{13,1},{2,14},{6,10},... | collective-permute-start | bytes 479240 | tf_op jit(solution)/shard_map/ppermute | solution.py:692
  321.9 17.7 %collective-permute-start.47 = (f32[104,384]{1,0:T(8,128)}, f32[104,384]{1,0:T(8,128)}, u32[]{:S(2)}, u32[]{:S(2)}) collective-permute-start(f32[104,384]{1,0:T(8,128)} %tie.41.refs_1_), channel_id=1, source_target_pairs={{0,8},{4,12},{8,0},{12,4},{1,9},{5,13},{9,1},{13,5},{2,10},{6,14},... | collective-permute-start | bytes 479240 | tf_op jit(solution)/shard_map/ppermute | solution.py:692
  (44 other events, 306.5 us)
